TPU v7x, 32 devices: a whole 2x2x4 slice. The times are simulated.
32 devices in a mesh: section: 4 (over y, core), dp: 4 (over z), mp: 2 (over x).
Axes of the slice: x: 2, y: 2, z: 4, core: 2. Of those that a mesh axis runs over, the one named last changes fastest.
Arguments:
- encoder_rows: bfloat16 [48, 256, 4096], P(('section', 'dp')), may hold values from -6 to 6
- w_key: bfloat16 [4096, 4096], P(('section', 'dp'), 'mp'), may hold values from -0.09375 to 0.09375
- w_value: bfloat16 [4096, 4096], P(('section', 'dp'), 'mp'), may hold values from -0.09375 to 0.09375
- query: bfloat16 [64, 128, 4096], P(('section', 'dp'), None, 'mp'), may hold values from -80 to 80
- grad_context: bfloat16 [64, 128, 4096], P(('section', 'dp'), None, 'mp'), may hold values from -6 to 6
- source: int32 [64], replicated, may hold values from 0 to 47, as said below
Outputs:
- context: bfloat16 [64, 128, 4096], P(('section', 'dp'), None, 'mp')
- grad_query: bfloat16 [64, 128, 4096], P(('section', 'dp'), None, 'mp')
- grad_kv_weights: float32 [2, 4096, 4096], P(None, ('section', 'dp'), 'mp')
Inputs may be any that keep to these rules, and one draw needn't show every extreme that they name: `source`: the sequences of one section index (the 16 consecutive sequences held at that section index) read only examples held at the same section index; the 4 sequences of one device read examples held at 4 different dp indices.
All inputs are finite; a program needn't handle non-finite values.
Results may differ from a plain program's by a relative error of at most 0.025.
The roundings to bfloat16 on the way count: a program that leaves them out, or rounds other values in their place, can miss the bound.
Values may be sent and summed in bfloat16 or wider, within the bound.
No kernel may reach another device: no remote copies, remote signals or barrier semaphores. Data moves between devices by JAX's collectives and lax.ppermute only.
A program may use at most 192 MiB of HBM per device.

v0:
```python
import jax
import jax.numpy as jnp
from jax import lax
from jax.sharding import PartitionSpec as P

HEAD_DIM = 64


def per_device(encoder_rows, w_key, w_value, query, grad_context, source):
    ex_dev, seq_len, width = encoder_rows.shape
    dec_dev, q_rows, inner_dev = query.shape
    heads_dev = inner_dev // HEAD_DIM
    n_dp = lax.axis_size("dp")
    section_idx = lax.axis_index("section")
    dp_idx = lax.axis_index("dp")
    flat = encoder_rows.reshape(ex_dev * seq_len, width)
    key_acc = jnp.dot(
        flat,
        lax.all_gather(w_key, ("section", "dp"), axis=0, tiled=True),
        preferred_element_type=jnp.float32,
    )
    value_acc = jnp.dot(
        flat,
        lax.all_gather(w_value, ("section", "dp"), axis=0, tiled=True),
        preferred_element_type=jnp.float32,
    )
    keys = key_acc.astype(jnp.bfloat16).reshape(ex_dev, seq_len, inner_dev)
    values = value_acc.astype(jnp.bfloat16).reshape(ex_dev, seq_len, inner_dev)
    per_section = n_dp * dec_dev
    row_plan = lax.dynamic_slice_in_dim(source, section_idx * per_section, per_section).reshape(
        n_dp, dec_dev
    )
    holder_dp = row_plan // ex_dev - section_idx * n_dp
    local_ex = row_plan % ex_dev
    mine = holder_dp == dp_idx
    wanted = mine[:, :, None] & (
        local_ex[:, :, None] == jnp.arange(ex_dev, dtype=jnp.int32)[None, None, :]
    )
    pick = jnp.sum(wanted.astype(jnp.float32), axis=1).astype(jnp.bfloat16)
    my_holder = lax.dynamic_index_in_dim(holder_dp, dp_idx, 0, keepdims=False)
    send_keys = jnp.einsum("pk,ksc->psc", pick, keys, preferred_element_type=jnp.float32).astype(
        jnp.bfloat16
    )
    send_values = jnp.einsum(
        "pk,ksc->psc", pick, values, preferred_element_type=jnp.float32
    ).astype(jnp.bfloat16)
    recv_keys, recv_values = (
        lax.all_to_all(send_keys, "dp", split_axis=0, concat_axis=0, tiled=True),
        lax.all_to_all(send_values, "dp", split_axis=0, concat_axis=0, tiled=True),
    )
    tile_keys = jnp.take(recv_keys, my_holder, axis=0)
    tile_values = jnp.take(recv_values, my_holder, axis=0)
    q_four = query.reshape(dec_dev, q_rows, heads_dev, HEAD_DIM)
    g_four = grad_context.reshape(dec_dev, q_rows, heads_dev, HEAD_DIM)
    k_four = tile_keys.reshape(dec_dev, seq_len, heads_dev, HEAD_DIM)
    v_four = tile_values.reshape(dec_dev, seq_len, heads_dev, HEAD_DIM)
    scores = jnp.einsum("nthc,nuhc->nhtu", q_four, k_four, preferred_element_type=jnp.float32)
    top = jnp.max(scores, axis=-1, keepdims=True)
    expo = jnp.exp(scores - top)
    weights = expo / jnp.sum(expo, axis=-1, keepdims=True)
    probs = weights.astype(jnp.bfloat16)
    context = jnp.einsum(
        "nhtu,nuhc->nthc", probs, v_four, preferred_element_type=jnp.float32
    ).astype(jnp.bfloat16)
    dprobs = jnp.einsum("nthc,nuhc->nhtu", g_four, v_four, preferred_element_type=jnp.float32)
    delta = jnp.sum(weights * dprobs, axis=-1, keepdims=True)
    score_grads = (weights * (dprobs - delta)).astype(jnp.bfloat16)
    grad_query = jnp.einsum(
        "nhtu,nuhc->nthc", score_grads, k_four, preferred_element_type=jnp.float32
    ).astype(jnp.bfloat16)
    key_terms = jnp.einsum(
        "nhtu,nthc->nuhc", score_grads, q_four, preferred_element_type=jnp.float32
    ).astype(jnp.bfloat16)
    value_terms = jnp.einsum(
        "nhtu,nthc->nuhc", probs, g_four, preferred_element_type=jnp.float32
    ).astype(jnp.bfloat16)
    key_terms = key_terms.reshape(dec_dev, seq_len, inner_dev)
    value_terms = value_terms.reshape(dec_dev, seq_len, inner_dev)
    to_holder = (my_holder[:, None] == jnp.arange(n_dp, dtype=jnp.int32)[None, :]).astype(
        jnp.bfloat16
    )
    back_keys = jnp.einsum(
        "np,nsc->psc", to_holder, key_terms, preferred_element_type=jnp.float32
    ).astype(jnp.bfloat16)
    back_values = jnp.einsum(
        "np,nsc->psc", to_holder, value_terms, preferred_element_type=jnp.float32
    ).astype(jnp.bfloat16)
    ret_keys, ret_values = (
        lax.all_to_all(back_keys, "dp", split_axis=0, concat_axis=0, tiled=True),
        lax.all_to_all(back_values, "dp", split_axis=0, concat_axis=0, tiled=True),
    )
    summed_keys = jnp.einsum("pk,psc->ksc", pick, ret_keys, preferred_element_type=jnp.float32)
    summed_values = jnp.einsum("pk,psc->ksc", pick, ret_values, preferred_element_type=jnp.float32)
    grad_keys = summed_keys.astype(jnp.bfloat16).reshape(ex_dev * seq_len, inner_dev)
    grad_values = summed_values.astype(jnp.bfloat16).reshape(ex_dev * seq_len, inner_dev)
    part_keys = lax.dot_general(
        flat, grad_keys, (((0,), (0,)), ((), ())), preferred_element_type=jnp.float32
    )
    part_values = lax.dot_general(
        flat, grad_values, (((0,), (0,)), ((), ())), preferred_element_type=jnp.float32
    )
    grad_rows = lax.psum_scatter(
        jnp.concatenate([part_keys, part_values], axis=1).astype(jnp.bfloat16),
        ("section", "dp"),
        scatter_dimension=0,
        tiled=True,
    ).astype(jnp.float32)
    grad_kv_weights = jnp.stack([grad_rows[:, :inner_dev], grad_rows[:, inner_dev:]], axis=0)
    return (
        context.reshape(dec_dev, q_rows, inner_dev),
        grad_query.reshape(dec_dev, q_rows, inner_dev),
        grad_kv_weights,
    )


def solution(mesh):
    return jax.shard_map(
        per_device,
        mesh=mesh,
        in_specs=(
            P(("section", "dp"), None, None),
            P(("section", "dp"), "mp"),
            P(("section", "dp"), "mp"),
            P(("section", "dp"), None, "mp"),
            P(("section", "dp"), None, "mp"),
            P(),
        ),
        out_specs=(
            P(("section", "dp"), None, "mp"),
            P(("section", "dp"), None, "mp"),
            P(None, ("section", "dp"), "mp"),
        ),
        check_vma=False,
    )
```

profile of v0, /device:TPU:11, one launch (start us, length us, event | category | flops | bytes accessed | tf_op | source)
XLA Modules:
  0.0 1157.9 jit_solution(15414151239167961353)
XLA Ops:
  7.2 0.0 all-gather.3.cloned.1.call-start
  7.2 0.7 all-gather.3.cloned.1.call-update
  7.9 0.0 all-gather.5.cloned.1.call-start
  7.9 0.7 all-gather.5.cloned.1.call-update
  8.7 0.7 sign_compare_fusion
  9.4 0.1 ne.38
  9.5 0.7 broadcast_divide_fusion.1
  10.2 0.1 div.22
  10.3 0.1 rem.26
  10.4 0.1 convert_reduce_fusion
  10.5 126.3 %all-gather.3.cloned.1.call-done = bf16[4096,2048]{1,0:T(8,128)(2,1)} async-done(((bf16[256,2048]{1,0:T(8,128)(2,1)}), bf16[4096,2048]{1,0:T(8,128)(2,1)}) %all-gather.3.cloned.1.call-update) | async-done | bytes 16777232 | tf_op jit(solution)/shard_map/all_gather | solution.py:24
  136.8 18.5 %convolution_convert_fusion.3 = bf16[768,2048]{1,0:T(8,128)(2,1)S(1)} fusion(bf16[768,4096]{1,0:T(8,128)(2,1)} %bitcast.105, bf16[4096,2048]{1,0:T(8,128)(2,1)} %all-gather.3.cloned.1.call-done), kind=kOutput, calls=%fused_computation.40 | convolution fusion | flops 12886474752 | bytes 26214400 | tf_op jit(solution)/shard_map/dot_general | solution.py:22
  155.3 6.1 fusion.22
  161.4 4.3 copy.89
  165.7 7.2 all-to-all-start
  172.8 167.0 %all-gather.5.cloned.1.call-done = bf16[4096,2048]{1,0:T(8,128)(2,1)} async-done(((bf16[256,2048]{1,0:T(8,128)(2,1)}), bf16[4096,2048]{1,0:T(8,128)(2,1)}) %all-gather.5.cloned.1.call-update) | async-done | bytes 16777232 | tf_op jit(solution)/shard_map/all_gather | solution.py:19
  339.9 18.5 %convolution_convert_fusion.2 = bf16[768,2048]{1,0:T(8,128)(2,1)S(1)} fusion(bf16[768,4096]{1,0:T(8,128)(2,1)} %bitcast.106, bf16[4096,2048]{1,0:T(8,128)(2,1)} %all-gather.5.cloned.1.call-done), kind=kOutput, calls=%fused_computation.39 | convolution fusion | flops 12886474752 | bytes 26214400 | tf_op jit(solution)/shard_map/dot_general | solution.py:17
  358.4 6.1 fusion.25
  364.5 4.3 copy.93
  368.8 0.0 all-to-all-done
  368.8 11.2 all-to-all-start.1
  380.0 3.0 copy.95
  383.0 3.9 copy.97
  387.0 5.0 gather_fusion
  392.0 78.0 %all-to-all-done.1 = bf16[4,256,2048]{2,1,0:T(8,128)(2,1)} async-done(((bf16[4,256,2048]{2,1,0:T(8,128)(2,1)}), bf16[4,256,2048]{2,1,0:T(8,128)(2,1)}, u32[]{:S(2)}, u32[]{:S(2)}) %all-to-all-start.1) | async-done | bytes 4194336 | tf_op jit(solution)/shard_map/all_to_all | solution.py:48
  470.0 5.0 gather_fusion.1
  475.0 7.6 broadcast_select_fusion
  482.6 6.2 copy.94
  488.8 6.2 copy.90
  495.0 10.2 fusion.56
  505.2 13.2 %fusion.1 = (f32[4,32,128]{2,1,0:T(8,128)S(1)}, f32[4,32,256,128]{3,2,1,0:T(8,128)}) fusion(f32[4,32,128,256]{2,3,1,0:T(8,128)} %get-tuple-element.30, f32[4,32,128]{2,1,0:T(8,128)S(1)} %get-tuple-element.29, bf16[4,256,32,64]{1,3,2,0:T(8,128)(2,1)} %bitcast.99, bf16[4,128,32,64]{1,3,2,0:T(8,128)(2,1)} %bitcast.102), kind=kOutput, calls=%fused_computation.8 | convolution fusion | flops 549437440 | bytes 39976960 | tf_op jit(solution)/shard_map/nthc,nuhc->nhtu/dot_general | solution.py:65
  518.4 15.1 %fusion.3 = bf16[4,32,128,256]{2,3,1,0:T(8,128)(2,1)} fusion(f32[4,32,256,128]{3,2,1,0:T(8,128)} %get-tuple-element.32, f32[4,32,128]{2,1,0:T(8,128)S(1)} %get-tuple-element.31, f32[4,32,128,256]{2,3,1,0:T(8,128)} %get-tuple-element.30, f32[4,32,128]{2,1,0:T(8,128)S(1)} %get-tuple-element.29), kind=kLoop, calls=%fused_computation.10 | loop fusion | flops 16777216 | bytes 42074112 | tf_op jit(solution)/shard_map/convert_element_type | solution.py:67
  533.5 8.3 convolution_convert_fusion.4
  541.8 8.0 copy.100
  549.8 4.5 convolution_convert_fusion.1
  554.3 4.3 copy.101
  558.6 0.0 copy-start
  558.6 8.2 all-to-all-start.2
  566.8 0.0 copy-done
  566.8 13.3 %fusion.36 = bf16[4,32,256,64]{2,3,1,0:T(8,128)(2,1)} fusion(bf16[4,128,32,64]{1,3,2,0:T(8,128)(2,1)S(1)} %bitcast.103, f32[4,32,128,256]{2,3,1,0:T(8,128)} %get-tuple-element.30, f32[4,32,128]{2,1,0:T(8,128)S(1)} %get-tuple-element.29), kind=kOutput, calls=%fused_computation.44 | convolution fusion | flops 547356672 | bytes 23134208 | tf_op jit(solution)/shard_map/nhtu,nthc->nuhc/dot_general | solution.py:74
  580.1 7.9 copy.105
  588.0 4.5 convolution_convert_fusion
  592.5 4.3 copy.106
  596.8 59.0 %all-to-all-done.2 = bf16[4,256,2048]{2,1,0:T(8,128)(2,1)} async-done(((bf16[4,256,2048]{2,1,0:T(8,128)(2,1)}), bf16[4,256,2048]{2,1,0:T(8,128)(2,1)}, u32[]{:S(2)}, u32[]{:S(2)}) %all-to-all-start.2) | async-done | bytes 4194336 | tf_op jit(solution)/shard_map/all_to_all | solution.py:89
  655.9 8.4 all-to-all-start.3
  664.3 0.0 reduce-scatter.2.cloned.1.call-start
  664.3 5.5 fusion.28
  669.8 24.1 %fusion.6 = bf16[4096,2048]{0,1:T(8,128)(2,1)} fusion(bf16[3,256,4096]{2,1,0:T(8,128)(2,1)} %param.8, bf16[3,256,2048]{2,0,1:T(4,128)(2,1)S(1)} %fusion.28), kind=kOutput, calls=%fused_computation.15 | convolution fusion | flops 12893290496 | bytes 26214400 | tf_op jit(solution)/shard_map/dot_general | solution.py:96
  693.9 59.1 %all-to-all-done.3 = bf16[4,256,2048]{2,1,0:T(8,128)(2,1)} async-done(((bf16[4,256,2048]{2,1,0:T(8,128)(2,1)}), bf16[4,256,2048]{2,1,0:T(8,128)(2,1)}, u32[]{:S(2)}, u32[]{:S(2)}) %all-to-all-start.3) | async-done | bytes 4194336 | tf_op jit(solution)/shard_map/all_to_all | solution.py:90
  753.0 5.5 fusion.31
  758.5 24.2 %fusion.7 = bf16[4096,2048]{0,1:T(8,128)(2,1)} fusion(bf16[3,256,4096]{2,1,0:T(8,128)(2,1)} %param.8, bf16[3,256,2048]{2,0,1:T(4,128)(2,1)S(1)} %fusion.31), kind=kOutput, calls=%fused_computation.16 | convolution fusion | flops 12893290496 | bytes 26214400 | tf_op jit(solution)/shard_map/dot_general | solution.py:99
  782.7 23.8 %pad_maximum_fusion = bf16[4096,4096]{0,1:T(8,128)(2,1)} fusion(bf16[4096,2048]{0,1:T(8,128)(2,1)} %fusion.7, bf16[4096,2048]{0,1:T(8,128)(2,1)} %fusion.6), kind=kLoop, calls=%fused_computation.3 | loop fusion | flops 67108864 | bytes 67108864 | tf_op jit(solution)/shard_map/concatenate | solution.py:103
  806.5 0.0 reduce-scatter.2.cloned.1.call-update
  806.5 8.5 fusion.39
  815.0 2.6 copy.109
  817.6 8.6 convolution_convert_fusion.5
  826.2 2.6 copy.110
  828.8 312.3 %reduce-scatter.2.cloned.1.call-done = bf16[256,4096]{0,1:T(8,128)(2,1)} async-done(((bf16[4096,4096]{0,1:T(8,128)(2,1)}), bf16[256,4096]{0,1:T(8,128)(2,1)}) %reduce-scatter.2.cloned.1.call-update) | async-done | bytes 2097168 | tf_op jit(solution)/shard_map/reduce_scatter | solution.py:102
  1141.2 1.9 convert_element_type.85
  1143.1 0.3 slice_bitcast_fusion.1
  1143.4 2.2 pad_maximum_fusion.1
  1145.6 5.3 copy.111
  (5 shorter events, 0.0 us)
Async XLA Ops:
  7.2 129.7 %all-gather.3.cloned.1.call-start = ((), (), s32[]{:S(2)}) async-start(), calls=%async_computation.5 | async-start | bytes 17825792 | tf_op jit(solution)/shard_map/all_gather | solution.py:24
  7.9 332.0 %all-gather.5.cloned.1.call-start = ((), (), s32[]{:S(2)}) async-start(), calls=%async_computation.6 | async-start | bytes 17825792 | tf_op jit(solution)/shard_map/all_gather | solution.py:19
  165.7 203.1 %all-to-all-start = ((bf16[4,256,2048]{2,1,0:T(8,128)(2,1)}), bf16[4,256,2048]{2,1,0:T(8,128)(2,1)}, u32[]{:S(2)}, u32[]{:S(2)}) async-start(bf16[4,256,2048]{2,1,0:T(8,128)(2,1)} %copy.89), calls=%async_computation | async-start | bytes 8388608 | tf_op jit(solution)/shard_map/all_to_all | solution.py:49
  368.8 101.2 %all-to-all-start.1 = ((bf16[4,256,2048]{2,1,0:T(8,128)(2,1)}), bf16[4,256,2048]{2,1,0:T(8,128)(2,1)}, u32[]{:S(2)}, u32[]{:S(2)}) async-start(bf16[4,256,2048]{2,1,0:T(8,128)(2,1)} %copy.93), calls=%async_computation.1 | async-start | bytes 8388608 | tf_op jit(solution)/shard_map/all_to_all | solution.py:48
  558.6 8.2 copy-start
  558.6 97.3 %all-to-all-start.2 = ((bf16[4,256,2048]{2,1,0:T(8,128)(2,1)}), bf16[4,256,2048]{2,1,0:T(8,128)(2,1)}, u32[]{:S(2)}, u32[]{:S(2)}) async-start(bf16[4,256,2048]{2,1,0:T(8,128)(2,1)} %copy.101), calls=%async_computation.2 | async-start | bytes 8388608 | tf_op jit(solution)/shard_map/all_to_all | solution.py:89
  655.9 97.2 %all-to-all-start.3 = ((bf16[4,256,2048]{2,1,0:T(8,128)(2,1)}), bf16[4,256,2048]{2,1,0:T(8,128)(2,1)}, u32[]{:S(2)}, u32[]{:S(2)}) async-start(bf16[4,256,2048]{2,1,0:T(8,128)(2,1)} %copy.106), calls=%async_computation.3 | async-start | bytes 8388608 | tf_op jit(solution)/shard_map/all_to_all | solution.py:90
  664.3 476.9 %reduce-scatter.2.cloned.1.call-start = ((), (), s32[]{:S(2)}) async-start(), calls=%async_computation.7 | async-start | bytes 35651584 | tf_op jit(solution)/shard_map/reduce_scatter | solution.py:102
Sparse Core Ops, SparseCore 0:
  10.2 126.5 all-gather.2
  139.0 200.8 all-gather.4
  806.7 334.4 reduce-scatter.1
where the time goes:
time: 1170 us; the launch traced here: 1160 us
  waiting for transfers between devices  803 us (69%)
  matrix products  179 us (15%)
  local copies, waits for them, and re-layouts  73.4 us (6%)
  other arithmetic  52.2 us (4%)
  starting transfers between devices  35.1 us (3%)
  between operations  14.4 us (1%)
    reduce_scatter x1, waiting for transfers between devices, per_device(): lax.psum_scatter(jnp.concatenate([part_keys, part_values], axis=1).astype...  312 us
    all_gather x1, waiting for transfers between devices, per_device(): lax.all_gather(w_key, ('section', 'dp'), axis=0, tiled=True)  167 us
    all_gather x1, waiting for transfers between devices, per_device(): lax.all_gather(w_value, ('section', 'dp'), axis=0, tiled=True)  126 us
    all_to_all x1, waiting for transfers between devices, per_device(): lax.all_to_all(send_keys, 'dp', split_axis=0, concat_axis=0, tiled=True)  78 us
    all_to_all x1, waiting for transfers between devices, per_device(): lax.all_to_all(back_values, 'dp', split_axis=0, concat_axis=0, tiled=True)  59.1 us
    all_to_all x1, waiting for transfers between devices, per_device(): lax.all_to_all(back_keys, 'dp', split_axis=0, concat_axis=0, tiled=True)  59 us
    dot_general x1, matrix products, per_device(): lax.dot_general(flat, grad_values, (((0,), (0,)), ((), ())), preferred_el...  24.2 us
    dot_general x1, matrix products, per_device(): lax.dot_general(flat, grad_keys, (((0,), (0,)), ((), ())), preferred_elem...  24.1 us
  transfers between devices with their start and end apart: 7, of which 6 were waited for; matrix products, arithmetic and copies ran while one was open for 13% of the time, Pallas kernels for 0%

commit v1 on v0

v1 whole, which is shorter than its diff:
```python
import functools

import jax
import jax.numpy as jnp
from jax import lax
from jax.experimental import pallas as pl
from jax.experimental.pallas import tpu as pltpu
from jax.sharding import PartitionSpec as P

HEAD_DIM = 64
LANES = 128
CHUNKS = 2
MIB = 1024 * 1024
BF = jnp.bfloat16
F32 = jnp.float32


def dot(a, b, dims):
    return lax.dot_general(a, b, (dims, ((), ())), preferred_element_type=F32)


def params(mib):
    return pltpu.CompilerParams(vmem_limit_bytes=mib * MIB)


def pack_weights_kernel(chunks, cols, k_ref, v_ref, *outs):
    for c in range(chunks):
        outs[c][0, :, :cols] = k_ref[:, c * cols:(c + 1) * cols]
        outs[c][0, :, cols:] = v_ref[:, c * cols:(c + 1) * cols]


def pack_weights(me, w_key, w_value, n_section, chunks, cols):
    rows = w_key.shape[0]
    own = chunks * cols
    block = pl.BlockSpec((rows, own), lambda r, at: (0, at[0] ^ r))
    return pl.pallas_call(
        lambda at, *refs: pack_weights_kernel(chunks, cols, *refs),
        grid_spec=pltpu.PrefetchScalarGridSpec(
            num_scalar_prefetch=1,
            grid=(n_section,),
            in_specs=[block, block],
            out_specs=[pl.BlockSpec((1, rows, 2 * cols), lambda r, at: (r, 0, 0))] * chunks,
        ),
        out_shape=[jax.ShapeDtypeStruct((n_section, rows, 2 * cols), BF)] * chunks,
        compiler_params=params(32),
    )(me, w_key, w_value)


def pack_queries_kernel(n_section, chunks, cols, all_filled, n_dp, at, q_ref, g_ref, *outs):
    q, g = q_ref[0], g_ref[0]
    if not all_filled:
        keep = at[n_dp + pl.program_id(0)] > 0
        q = jnp.where(keep, q, jnp.zeros_like(q))
        g = jnp.where(keep, g, jnp.zeros_like(g))
    for s in range(n_section):
        for c in range(chunks):
            lo = (s * chunks + c) * cols
            outs[c][s, 0, 0] = q[:, lo:lo + cols]
            outs[c][s, 0, 1] = g[:, lo:lo + cols]


def pack_queries(slot, filled, query, grad, n_section, n_dp, chunks, cols):
    dec_dev, q_rows, inner = query.shape
    block = pl.BlockSpec((1, q_rows, inner), lambda p, at: (at[p], 0, 0))
    return pl.pallas_call(
        functools.partial(pack_queries_kernel, n_section, chunks, cols, n_dp == dec_dev, n_dp),
        grid_spec=pltpu.PrefetchScalarGridSpec(
            num_scalar_prefetch=1,
            grid=(n_dp,),
            in_specs=[block, block],
            out_specs=[
                pl.BlockSpec((n_section, 1, 2, q_rows, cols), lambda p, at: (0, p, 0, 0, 0))
            ] * chunks,
        ),
        out_shape=[jax.ShapeDtypeStruct((n_section, n_dp, 2, q_rows, cols), BF)] * chunks,
        compiler_params=params(32),
    )(jnp.concatenate([slot, filled]).astype(jnp.int32), query, grad)


def unpack_outputs_kernel(n_section, chunks, cols, at, *refs):
    ctx_ref, gq_ref = refs[chunks:]
    for s in range(n_section):
        for c in range(chunks):
            lo = (s * chunks + c) * cols
            ctx_ref[0, :, lo:lo + cols] = refs[c][s, 0, 0]
            gq_ref[0, :, lo:lo + cols] = refs[c][s, 0, 1]


def unpack_outputs(my_holder, parts, dec_dev):
    n_section, n_dp, _, q_rows, cols = parts[0].shape
    chunks = len(parts)
    inner = n_section * chunks * cols
    block = pl.BlockSpec((n_section, 1, 2, q_rows, cols), lambda j, at: (0, at[j], 0, 0, 0))
    out = pl.BlockSpec((1, q_rows, inner), lambda j, at: (j, 0, 0))
    return pl.pallas_call(
        functools.partial(unpack_outputs_kernel, n_section, chunks, cols),
        grid_spec=pltpu.PrefetchScalarGridSpec(
            num_scalar_prefetch=1,
            grid=(dec_dev,),
            in_specs=[block] * chunks,
            out_specs=[out, out],
        ),
        out_shape=[jax.ShapeDtypeStruct((dec_dev, q_rows, inner), BF)] * 2,
        compiler_params=params(32),
    )(my_holder, *parts)


def project_kernel(n_dp, n_section, at, x_ref, *refs):
    own, below, above = refs[0], refs[1:n_dp], refs[n_dp:2 * n_dp - 1]
    out_ref, w_ref = refs[2 * n_dp - 1:]
    dp, me = at[0], at[1]
    rows = own.shape[1]

    @pl.when(pl.program_id(0) == 0)
    def _():
        for r in range(n_section):
            w_ref[me ^ r, dp] = own[r]
        for k in range(1, n_dp):
            @pl.when(dp >= k)
            def _():
                for r in range(n_section):
                    w_ref[me ^ r, dp - k] = below[k - 1][r]

            @pl.when(dp + k < n_dp)
            def _():
                for r in range(n_section):
                    w_ref[me ^ r, dp + k] = above[k - 1][r]

    w = w_ref[...].reshape(n_section * n_dp * rows, own.shape[2])
    out_ref[...] = dot(x_ref[...], w, ((1,), (0,))).astype(BF)


def project(at, flat, own, below, above):
    n_section, rows, both = own.shape
    total, width = flat.shape
    n_dp = len(below) + 1
    tile = 512 if total % 512 == 0 else 256
    w_block = pl.BlockSpec((n_section, rows, both), lambda i, at: (0, 0, 0))
    return pl.pallas_call(
        functools.partial(project_kernel, n_dp, n_section),
        grid_spec=pltpu.PrefetchScalarGridSpec(
            num_scalar_prefetch=1,
            grid=(total // tile,),
            in_specs=[pl.BlockSpec((tile, width), lambda i, at: (i, 0))] + [w_block] * (2 * n_dp - 1),
            out_specs=pl.BlockSpec((tile, both), lambda i, at: (i, 0)),
            scratch_shapes=[pltpu.VMEM((n_section, n_dp, rows, both), BF)],
        ),
        out_shape=jax.ShapeDtypeStruct((total, both), BF),
        compiler_params=params(56),
        cost_estimate=pl.CostEstimate(
            flops=2 * total * width * both,
            bytes_accessed=2 * (total * width + 2 * width * both + total * both),
            transcendentals=0,
        ),
    )(at, flat, own, *below, *above)


def weight_grad_kernel(x_ref, g_ref, out_ref):
    both = out_ref.shape[1]
    g = g_ref[...].reshape(both, g_ref.shape[2])
    out_ref[0] = dot(g, x_ref[...], ((1,), (0,))).astype(BF)


def weight_grad(flat, dkv, n_section, n_dp):
    total, width = flat.shape
    both = 2 * dkv.shape[1]
    rows = width // (n_section * n_dp)
    return pl.pallas_call(
        weight_grad_kernel,
        grid=(n_dp, n_section),
        in_specs=[
            pl.BlockSpec((total, rows), lambda d, s: (0, s * n_dp + d)),
            pl.BlockSpec((2, dkv.shape[1], total), lambda d, s: (0, 0, 0)),
        ],
        out_specs=pl.BlockSpec((1, both, rows), lambda d, s: (d, 0, s)),
        out_shape=jax.ShapeDtypeStruct((n_dp, both, n_section * rows), BF),
        compiler_params=params(56),
        cost_estimate=pl.CostEstimate(
            flops=2 * total * width * both,
            bytes_accessed=2 * (total * width + width * both + total * both),
            transcendentals=0,
        ),
    )(flat, dkv)


def attend_kernel(seqs, ex_dev, seq_len, q_rows, local_ref, k_ref, v_ref, qg_ref,
                  out_ref, dkv_ref, dk_acc, dv_acc):
    section = pl.program_id(0)
    dk_acc[...] = jnp.zeros_like(dk_acc)
    dv_acc[...] = jnp.zeros_like(dv_acc)
    low = lax.broadcasted_iota(jnp.int32, (q_rows, LANES), 1) < HEAD_DIM

    def stack(rows):
        zero = jnp.zeros_like(rows)
        return jnp.concatenate([jnp.where(low, rows, zero), jnp.where(low, zero, rows)], axis=0)

    def merge(rows):
        return jnp.where(low, rows[:q_rows], rows[q_rows:])

    for i in range(seqs):
        at = local_ref[section * seqs + i]
        keys = k_ref[0, at]
        values = v_ref[0, at]
        q_two = stack(qg_ref[0, i, 0])
        g_two = stack(qg_ref[0, i, 1])
        scores = dot(q_two, keys, ((1,), (1,)))
        top = jnp.max(scores, axis=-1, keepdims=True)
        expo = jnp.exp(scores - top)
        weights = expo * (1.0 / jnp.sum(expo, axis=-1, keepdims=True))
        probs = weights.astype(BF)
        out_ref[0, i, 0] = merge(dot(probs, values, ((1,), (0,)))).astype(BF)
        dprobs = dot(g_two, values, ((1,), (1,)))
        delta = jnp.sum(weights * dprobs, axis=-1, keepdims=True)
        score_grads = (weights * (dprobs - delta)).astype(BF)
        out_ref[0, i, 1] = merge(dot(score_grads, keys, ((1,), (0,)))).astype(BF)
        dk_acc[at] += dot(q_two, score_grads, ((0,), (0,))).astype(BF).astype(F32)
        dv_acc[at] += dot(g_two, probs, ((0,), (0,))).astype(BF).astype(F32)

    for e in range(ex_dev):
        dkv_ref[0, :, e * seq_len:(e + 1) * seq_len] = dk_acc[e].astype(BF)
        dkv_ref[1, :, e * seq_len:(e + 1) * seq_len] = dv_acc[e].astype(BF)


def attend(local, kv, qg):
    n_section, ex_dev, seq_len, both = kv.shape
    seqs, q_rows, width = qg.shape[1], qg.shape[3], qg.shape[4]
    pairs = width // LANES
    rows = ex_dev * seq_len
    qg_block = pl.BlockSpec((1, seqs, 2, q_rows, LANES), lambda s, p, _: (s, 0, 0, 0, p))
    kv_block = (1, ex_dev, seq_len, LANES)
    return pl.pallas_call(
        functools.partial(attend_kernel, seqs, ex_dev, seq_len, q_rows),
        grid_spec=pltpu.PrefetchScalarGridSpec(
            num_scalar_prefetch=1,
            grid=(n_section, pairs),
            in_specs=[
                pl.BlockSpec(kv_block, lambda s, p, _: (s, 0, 0, p)),
                pl.BlockSpec(kv_block, lambda s, p, _: (s, 0, 0, pairs + p)),
                qg_block,
            ],
            out_specs=[
                qg_block,
                pl.BlockSpec((2, LANES, rows), lambda s, p, _: (0, p, s)),
            ],
            scratch_shapes=[
                pltpu.VMEM((ex_dev, LANES, seq_len), F32),
                pltpu.VMEM((ex_dev, LANES, seq_len), F32),
            ],
        ),
        out_shape=[
            jax.ShapeDtypeStruct(qg.shape, BF),
            jax.ShapeDtypeStruct((2, width, n_section * rows), BF),
        ],
        compiler_params=params(32),
        cost_estimate=pl.CostEstimate(
            flops=6 * 2 * n_section * seqs * pairs * 2 * q_rows * seq_len * LANES,
            bytes_accessed=2 * (2 * kv.size + 2 * qg.size),
            transcendentals=n_section * seqs * pairs * 2 * q_rows * seq_len,
        ),
    )(local, kv, kv, qg)


def finish_grads_kernel(chunks, cols, at, *refs):
    out_ref = refs[chunks]
    for c in range(chunks):
        for kv in range(2):
            block = refs[c][0, kv * cols:(kv + 1) * cols].astype(F32)
            out_ref[kv, :, c * cols:(c + 1) * cols] = block.T


def finish_grads(me, parts, cols):
    n_section, both, rows = parts[0].shape
    chunks = len(parts)
    own = chunks * cols
    return pl.pallas_call(
        functools.partial(finish_grads_kernel, chunks, cols),
        grid_spec=pltpu.PrefetchScalarGridSpec(
            num_scalar_prefetch=1,
            grid=(n_section,),
            in_specs=[pl.BlockSpec((1, both, rows), lambda r, at: (r, 0, 0))] * chunks,
            out_specs=pl.BlockSpec((2, rows, own), lambda r, at: (0, 0, at[0] ^ r)),
        ),
        out_shape=jax.ShapeDtypeStruct((2, rows, n_section * own), F32),
        compiler_params=params(32),
    )(me, *parts)


def section_swap(blocks):
    n_section = lax.axis_size("section")
    out = [blocks[0]]
    for r in range(1, n_section):
        out.append(lax.ppermute(blocks[r], "section", [(i, i ^ r) for i in range(n_section)]))
    return out


def gather_line(block):
    n = lax.axis_size("dp")
    below, above = [], []
    up = down = block
    for k in range(1, n):
        up = lax.ppermute(up, "dp", [(i, i + 1) for i in range(k - 1, n - 1)])
        down = lax.ppermute(down, "dp", [(i, i - 1) for i in range(1, n - k + 1)])
        below.append(up)
        above.append(down)
    return below, above


def scatter_line(part):
    n = lax.axis_size("dp")
    me = lax.axis_index("dp")

    def own(k):
        return lax.dynamic_index_in_dim(part, jnp.clip(me + k, 0, n - 1), 0, keepdims=False)

    up = down = None
    for k in range(n - 1, 0, -1):
        send_up = own(k) if up is None else own(k) + up
        send_down = own(-k) if down is None else own(-k) + down
        up = lax.ppermute(send_up, "dp", [(i, i + 1) for i in range(0, n - k)])
        down = lax.ppermute(send_down, "dp", [(i, i - 1) for i in range(k, n)])
    return (own(0).astype(F32) + up.astype(F32) + down.astype(F32)).astype(BF)


def spread_examples(rows):
    ex_dev, seq_len, width = rows.shape
    n_section, n_mp = lax.axis_size("section"), lax.axis_size("mp")
    mp_idx, me = lax.axis_index("mp"), lax.axis_index("section")
    part = seq_len // n_mp
    mine = lax.dynamic_slice_in_dim(rows, mp_idx * part, part, axis=1)
    if n_mp != 2 or n_section != 4:
        every = lax.all_gather(mine, ("section", "mp"), axis=0)
        every = every.reshape(n_section, n_mp, ex_dev, part, width).swapaxes(1, 2)
        return every.reshape(n_section, ex_dev, seq_len, width)
    core = [(i, i ^ 1) for i in range(4)]
    far = [(i, i ^ 2) for i in range(4)]
    swap = [(0, 1), (1, 0)]
    zero = jnp.int32(0)
    whole = jnp.zeros((n_section, ex_dev, seq_len, width), BF)

    def put(whole, piece, section, example, row):
        return lax.dynamic_update_slice(whole, piece[None], (section, example, row, zero))

    whole = put(whole, rows, me, zero, zero)
    whole = put(whole, lax.ppermute(rows, "section", core), me ^ 1, zero, zero)
    for e in range(ex_dev):
        at = jnp.int32(e)
        from_far = lax.ppermute(mine[e:e + 1], "section", far)
        from_side = lax.ppermute(from_far, "mp", swap)
        other_far = lax.ppermute(from_far, "section", core)
        other_side = lax.ppermute(from_side, "section", core)
        whole = put(whole, from_far, me ^ 2, at, mp_idx * part)
        whole = put(whole, other_far, me ^ 3, at, mp_idx * part)
        whole = put(whole, from_side, me ^ 2, at, (1 - mp_idx) * part)
        whole = put(whole, other_side, me ^ 3, at, (1 - mp_idx) * part)
    return whole


def per_device(encoder_rows, w_key, w_value, query, grad_context, source):
    ex_dev, seq_len, width = encoder_rows.shape
    dec_dev, q_rows, inner_dev = query.shape
    d_rows = w_key.shape[0]
    n_section, n_dp = lax.axis_size("section"), lax.axis_size("dp")
    section_idx, dp_idx = lax.axis_index("section"), lax.axis_index("dp")
    own = inner_dev // n_section
    chunks = min(CHUNKS, own // LANES)
    cols = own // chunks
    me = section_idx.reshape(1)
    at = jnp.stack([dp_idx, section_idx])

    plan = source.reshape(n_section, n_dp, dec_dev)
    holder = plan // ex_dev - jnp.arange(n_section, dtype=jnp.int32)[:, None, None] * n_dp
    reads_me = holder == dp_idx
    local = jnp.sum(jnp.where(reads_me, plan % ex_dev, 0), axis=-1).reshape(-1)
    my_holder = holder[section_idx, dp_idx]
    hit = my_holder[None, :] == jnp.arange(n_dp, dtype=jnp.int32)[:, None]
    slot = jnp.sum(jnp.where(hit, jnp.arange(dec_dev, dtype=jnp.int32)[None, :], 0), axis=1)
    filled = jnp.any(hit, axis=1)

    w_send = pack_weights(me, w_key, w_value, n_section, chunks, cols)
    w_own = [jnp.stack(section_swap(w)) for w in w_send]
    qg_send = pack_queries(slot, filled, query, grad_context, n_section, n_dp, chunks, cols)
    plane = spread_examples(encoder_rows)
    flat = plane.reshape(n_section * ex_dev * seq_len, width)

    outs, grads = [], []
    for c in range(chunks):
        below, above = gather_line(w_own[c])
        qg_all = lax.all_to_all(
            qg_send[c].reshape((n_section * n_dp,) + qg_send[c].shape[2:]),
            ("section", "dp"), split_axis=0, concat_axis=0, tiled=True,
        ).reshape(qg_send[c].shape)
        kv = project(at, flat, w_own[c], below, above)
        kv = kv.reshape(n_section, ex_dev, seq_len, 2 * cols)
        out, dkv = attend(local, kv, qg_all)
        part = weight_grad(flat, dkv, n_section, n_dp)
        total = scatter_line(part).reshape(2 * cols, n_section, d_rows)
        blocks = [
            lax.dynamic_index_in_dim(total, section_idx ^ r, 1, keepdims=False)
            for r in range(n_section)
        ]
        grads.append(jnp.stack(section_swap(blocks)))
        out = lax.all_to_all(
            out.reshape((n_section * n_dp,) + out.shape[2:]),
            ("section", "dp"), split_axis=0, concat_axis=0, tiled=True,
        )
        outs.append(out.reshape(qg_all.shape))

    context, grad_query = unpack_outputs(my_holder, outs, dec_dev)
    return context, grad_query, finish_grads(me, grads, cols)


def solution(mesh):
    return jax.shard_map(
        per_device,
        mesh=mesh,
        in_specs=(
            P(("section", "dp"), None, None),
            P(("section", "dp"), "mp"),
            P(("section", "dp"), "mp"),
            P(("section", "dp"), None, "mp"),
            P(("section", "dp"), None, "mp"),
            P(),
        ),
        out_specs=(
            P(("section", "dp"), None, "mp"),
            P(("section", "dp"), None, "mp"),
            P(None, ("section", "dp"), "mp"),
        ),
        check_vma=False,
    )
```

time: 1170 us -> 646 us (0.55)
  waiting for transfers between devices: 803 us -> 276 us
  matrix products: 179 us -> 0 us
  Pallas kernels: 0 us -> 140 us
  starting transfers between devices: 35.1 us -> 118 us
  other arithmetic: 52.2 us -> 30.4 us
  between operations: 14.4 us -> 1.18 us
    reduce_scatter x1 -> x0, waiting for transfers between devices: 312 us -> none  [per_device(): lax.psum_scatter(jnp.concatenate([part_keys, part_values], axis=1).astype...]
    all_gather x2 -> x0, waiting for transfers between devices: 293 us -> none  [the longest x1 167 us: per_device(): lax.all_gather(w_key, ('section', 'dp'), axis=0, tiled=True)]
    ppermute x0 -> x49, waiting for transfers between devices: none -> 276 us  [the longest x6 79.2 us: scatter_line(): down = lax.ppermute(send_down, 'dp', [(i, i - 1) for i in range(k, n)])]
    all_to_all x4, waiting for transfers between devices: 196 us -> 0.01 us  [the longest x2 0.01 us: per_device(): lax.all_to_all(qg_send[c].reshape((n_section * n_dp,) + qg_send[c].shape[...]
    dot_general x15 -> x0, matrix products: 169 us -> none  [the longest x1 24.2 us: per_device(): lax.dot_general(flat, grad_values, (((0,), (0,)), ((), ())), preferred_el...]
    pallas_call x0 -> x10, Pallas kernels: none -> 140 us  [the longest x2 46.4 us: weight_grad(): pl.pallas_call(weight_grad_kernel, grid=(n_dp, n_section), in_specs=[pl.B...]
    ppermute x0 -> x49, starting transfers between devices: none -> 82.9 us  [the longest x6 19.2 us: gather_line(): up = lax.ppermute(up, 'dp', [(i, i + 1) for i in range(k - 1, n - 1)])]
    dynamic_update_slice x0 -> x14, local copies, waits for them, and re-layouts: none -> 24.7 us  [put(): lax.dynamic_update_slice(whole, piece[None], (section, example, row, zero))]
  transfers between devices with their start and end apart: 7 -> 53, of which waited for: 6 -> 25; matrix products, arithmetic and copies ran while one was open for 13% -> 14% of each run, Pallas kernels for 0% -> 21%
where the time goes in v1:
time: 646 us; the launch traced here: 644 us
  waiting for transfers between devices  276 us (43%)
  Pallas kernels  140 us (22%)
  starting transfers between devices  118 us (18%)
  local copies, waits for them, and re-layouts  77.2 us (12%)
  other arithmetic  30.4 us (5%)
    ppermute x6, waiting for transfers between devices, scatter_line(): down = lax.ppermute(send_down, 'dp', [(i, i - 1) for i in range(k, n)])  79.2 us
    ppermute x6, waiting for transfers between devices, gather_line(): down = lax.ppermute(down, 'dp', [(i, i - 1) for i in range(1, n - k + 1)])  53.6 us
    pallas_call x2, Pallas kernels, weight_grad(): pl.pallas_call(weight_grad_kernel, grid=(n_dp, n_section), in_specs=[pl.B...  46.4 us
    ppermute x6, waiting for transfers between devices, scatter_line(): up = lax.ppermute(send_up, 'dp', [(i, i + 1) for i in range(0, n - k)])  43.6 us
    ppermute x12, waiting for transfers between devices, section_swap(): lax.ppermute(blocks[r], 'section', [(i, i ^ r) for i in range(n_section)])  43.2 us
    pallas_call x2, Pallas kernels, attend(): pl.pallas_call(functools.partial(attend_kernel, seqs, ex_dev, seq_len, q_...  43.1 us
    pallas_call x2, Pallas kernels, project(): pl.pallas_call(functools.partial(project_kernel, n_dp, n_section), grid_s...  40.4 us
    ppermute x6, waiting for transfers between devices, gather_line(): up = lax.ppermute(up, 'dp', [(i, i + 1) for i in range(k - 1, n - 1)])  29.6 us
  transfers between devices with their start and end apart: 53, of which 25 were waited for; matrix products, arithmetic and copies ran while one was open for 14% of the time, Pallas kernels for 21%

profile of v1, /device:TPU:11, one launch (start us, length us, event | category | flops | bytes accessed | tf_op | source)
XLA Modules:
  0.0 643.6 jit_solution(9141995657389465398)
XLA Ops:
  1.4 3.8 constant_dynamic-slice_fusion.10
  14.7 2.5 shard_map.87
  18.5 5.1 all-to-all-start.2
  25.0 15.4 %collective-permute-done.14 = bf16[256,512]{1,0:T(8,128)(2,1)} collective-permute-done((bf16[256,512]{1,0:T(8,128)(2,1)}, bf16[256,512]{1,0:T(8,128)(2,1)}, u32[]{:S(2)}, u32[]{:S(2)}) %collective-permute-start.14) | collective-permute-done | bytes 262176 | tf_op jit(solution)/shard_map/ppermute | solution.py:292
  42.5 8.1 %collective-permute-done.15 = bf16[256,512]{1,0:T(8,128)(2,1)} collective-permute-done((bf16[256,512]{1,0:T(8,128)(2,1)}, bf16[256,512]{1,0:T(8,128)(2,1)}, u32[]{:S(2)}, u32[]{:S(2)}) %collective-permute-start.15) | collective-permute-done | bytes 262176 | tf_op jit(solution)/shard_map/ppermute | solution.py:292
  51.5 8.8 %broadcast_in_dim.62 = bf16[4,3,256,4096]{3,2,1,0:T(8,128)(2,1)} broadcast(bf16[]{:T(256)} %constant.99.clone.1), dimensions={} | broadcast | bytes 25165826 | tf_op jit(solution)/shard_map/broadcast_in_dim | solution.py:338
  60.4 3.1 bitcast_dynamic-update-slice_fusion.1
  67.0 2.7 collective-permute-done.23
  70.9 4.8 collective-permute-done.24
  75.8 3.2 collective-permute-start.16
  80.8 6.2 bitcast_dynamic-update-slice_fusion
  87.1 2.3 bitcast_dynamic-update-slice_fusion.13
  89.4 8.3 %collective-permute-done.5 = bf16[1,128,4096]{2,1,0:T(8,128)(2,1)S(1)} collective-permute-done((bf16[1,128,4096]{2,1,0:T(8,128)(2,1)}, bf16[1,128,4096]{2,1,0:T(8,128)(2,1)S(1)}, u32[]{:S(2)}, u32[]{:S(2)}) %collective-permute-start.5) | collective-permute-done | bytes 1048608 | tf_op jit(solution)/shard_map/ppermute | solution.py:347
  101.7 3.6 collective-permute-done.3
  111.0 9.1 %collective-permute-done.9 = bf16[1,128,4096]{2,1,0:T(8,128)(2,1)S(1)} collective-permute-done((bf16[1,128,4096]{2,1,0:T(8,128)(2,1)}, bf16[1,128,4096]{2,1,0:T(8,128)(2,1)S(1)}, u32[]{:S(2)}, u32[]{:S(2)}) %collective-permute-start.9) | collective-permute-done | bytes 1048608 | tf_op jit(solution)/shard_map/ppermute | solution.py:347
  120.1 3.2 collective-permute-start.25
  126.9 6.1 collective-permute-done.7
  136.6 9.3 %collective-permute-done.25.refs_1_ = bf16[4,256,512]{2,1,0:T(8,128)(2,1)S(1)} collective-permute-done((bf16[4,256,512]{2,1,0:T(8,128)(2,1)S(1)}, bf16[4,256,512]{2,1,0:T(8,128)(2,1)S(1)}, u32[]{:S(2)}, u32[]{:S(2)}) %collective-permute-start.25) | collective-permute-done | bytes 1048608 | tf_op jit(solution)/shard_map/ppermute | solution.py:301
  145.9 4.2 collective-permute-start.17
  152.0 5.3 collective-permute-start.26
  161.4 2.5 collective-permute-start.12
  163.9 5.9 collective-permute-done.17.refs_2_
  171.5 3.2 collective-permute-done.20.refs_5_
  174.8 3.2 collective-permute-start.21
  178.0 14.4 %collective-permute-done.26.refs_2_ = bf16[4,256,512]{2,1,0:T(8,128)(2,1)} collective-permute-done((bf16[4,256,512]{2,1,0:T(8,128)(2,1)S(1)}, bf16[4,256,512]{2,1,0:T(8,128)(2,1)}, u32[]{:S(2)}, u32[]{:S(2)}) %collective-permute-start.26) | collective-permute-done | bytes 1048608 | tf_op jit(solution)/shard_map/ppermute | solution.py:301
  194.0 3.2 collective-permute-done.29.refs_5_
  197.2 3.2 collective-permute-start.30
  201.5 10.7 %all-to-all-start = ((bf16[16,2,128,256]{3,2,1,0:T(8,128)(2,1)}), bf16[16,2,128,256]{3,2,1,0:T(8,128)(2,1)}, u32[]{:S(2)}, u32[]{:S(2)}) async-start(bf16[16,2,128,256]{3,2,1,0:T(8,128)(2,1)} %bitcast.25), calls=%async_computation | async-start | bytes 4194304 | tf_op jit(solution)/shard_map/all_to_all | solution.py:388
  215.6 47.1 %collective-permute-done.30.refs_6_ = bf16[4,256,512]{2,1,0:T(8,128)(2,1)} collective-permute-done((bf16[4,256,512]{2,1,0:T(8,128)(2,1)}, bf16[4,256,512]{2,1,0:T(8,128)(2,1)}, u32[]{:S(2)}, u32[]{:S(2)}) %collective-permute-start.30) | collective-permute-done | bytes 1048608 | tf_op jit(solution)/shard_map/ppermute | solution.py:302
  262.7 20.2 %shard_map.89 = bf16[3072,512]{1,0:T(8,128)(2,1)} custom-call(s32[2]{0:T(128)} %pad_add_fusion.at, bf16[3072,4096]{1,0:T(8,128)(2,1)} %bitcast.130, bf16[4,256,512]{2,1,0:T(8,128)(2,1)} %copy-done.17, bf16[4,256,512]{2,1,0:T(8,128)(2,1)} %copy-done.21, bf16[4,256,512]{2,1,0:T(8,128)(2,1)} %collective-permute-done.26.refs_2_, ...), custom_call_target="tpu_custom_call" | custom-call | flops 12884901888 | bytes 36700160 | tf_op jit(solution)/shard_map/pallas_call | solution.py:139
  284.8 21.2 %shard_map.90 = (bf16[4,4,2,128,256]{4,3,2,1,0:T(8,128)(2,1)S(1)}, bf16[2,256,3072]{2,1,0:T(8,128)(2,1)S(1)}) custom-call(s32[16]{0:T(128)S(1)} %reshape.69.local_ref, bf16[4,3,256,512]{3,2,1,0:T(8,128)(2,1)S(1)} %bitcast.128, bf16[4,3,256,512]{3,2,1,0:T(8,128)(2,1)S(1)} %bitcast.129, bf16[4,4,2,128,256]{4,3,2,1,0:T(8,128)(2,1)S(1)} %bitcast.122), custom_call_target="tpu_custom_call" | custom-call | flops 3221225472 | bytes 10485760 | tf_op jit(solution)/shard_map/pallas_call | solution.py:231
  309.0 20.2 %shard_map.86 = bf16[3072,512]{1,0:T(8,128)(2,1)} custom-call(s32[2]{0:T(128)} %pad_add_fusion.at, bf16[3072,4096]{1,0:T(8,128)(2,1)} %bitcast.131, bf16[4,256,512]{2,1,0:T(8,128)(2,1)} %copy-done.16, bf16[4,256,512]{2,1,0:T(8,128)(2,1)} %copy-done.19, bf16[4,256,512]{2,1,0:T(8,128)(2,1)} %collective-permute-done.17.refs_2_, ...), custom_call_target="tpu_custom_call" | custom-call | flops 12884901888 | bytes 36700160 | tf_op jit(solution)/shard_map/pallas_call | solution.py:139
  329.3 10.6 %all-to-all-start.3 = ((bf16[16,2,128,256]{3,2,1,0:T(8,128)(2,1)}), bf16[16,2,128,256]{3,2,1,0:T(8,128)(2,1)S(1)}, u32[]{:S(2)}, u32[]{:S(2)}) async-start(bf16[16,2,128,256]{3,2,1,0:T(8,128)(2,1)} %bitcast.125), calls=%async_computation.3 | async-start | bytes 4194304 | tf_op jit(solution)/shard_map/all_to_all | solution.py:402
  341.8 21.9 %shard_map.88 = (bf16[4,4,2,128,256]{4,3,2,1,0:T(8,128)(2,1)S(1)}, bf16[2,256,3072]{2,1,0:T(8,128)(2,1)S(1)}) custom-call(s32[16]{0:T(128)S(1)} %reshape.69.local_ref, bf16[4,3,256,512]{3,2,1,0:T(8,128)(2,1)S(1)} %bitcast.126, bf16[4,3,256,512]{3,2,1,0:T(8,128)(2,1)S(1)} %bitcast.127, bf16[4,4,2,128,256]{4,3,2,1,0:T(8,128)(2,1)} %bitcast.26.qg_ref), custom_call_target="tpu_custom_call" | custom-call | flops 3221225472 | bytes 10485760 | tf_op jit(solution)/shard_map/pallas_call | solution.py:231
  366.6 23.2 %shard_map.92 = bf16[4,512,1024]{2,1,0:T(8,128)(2,1)} custom-call(bf16[3072,4096]{1,0:T(8,128)(2,1)} %bitcast.132, bf16[2,256,3072]{2,1,0:T(8,128)(2,1)} %copy-done.12), custom_call_target="tpu_custom_call" | custom-call | flops 12884901888 | bytes 32505856 | tf_op jit(solution)/shard_map/pallas_call | solution.py:168
  389.8 3.0 dynamic-slice_bitcast_fusion.3
  394.1 23.2 %shard_map.93 = bf16[4,512,1024]{2,1,0:T(8,128)(2,1)} custom-call(bf16[3072,4096]{1,0:T(8,128)(2,1)} %bitcast.133, bf16[2,256,3072]{2,1,0:T(8,128)(2,1)} %copy-done.11), custom_call_target="tpu_custom_call" | custom-call | flops 12884901888 | bytes 32505856 | tf_op jit(solution)/shard_map/pallas_call | solution.py:168
  417.3 2.7 dynamic-slice_bitcast_fusion.1
  423.0 2.6 bitcast_add_fusion.6
  425.6 3.4 collective-permute-start.32
  430.6 16.9 %collective-permute-done.40 = bf16[512,1024]{1,0:T(8,128)(2,1)} collective-permute-done((bf16[512,1024]{1,0:T(8,128)(2,1)}, bf16[512,1024]{1,0:T(8,128)(2,1)}, u32[]{:S(2)}, u32[]{:S(2)}) %collective-permute-start.40) | collective-permute-done | bytes 1048608 | tf_op jit(solution)/shard_map/ppermute | solution.py:319
  447.5 2.6 bitcast_add_fusion.2
  452.1 8.8 %all-to-all-start.1 = ((bf16[16,2,128,256]{3,2,1,0:T(8,128)(2,1)}), bf16[16,2,128,256]{3,2,1,0:T(8,128)(2,1)}, u32[]{:S(2)}, u32[]{:S(2)}) async-start(bf16[16,2,128,256]{3,2,1,0:T(8,128)(2,1)} %bitcast.124), calls=%async_computation.1 | async-start | bytes 4194304 | tf_op jit(solution)/shard_map/all_to_all | solution.py:402
  460.9 9.1 %collective-permute-done.32 = bf16[512,1024]{1,0:T(8,128)(2,1)} collective-permute-done((bf16[512,1024]{1,0:T(8,128)(2,1)}, bf16[512,1024]{1,0:T(8,128)(2,1)}, u32[]{:S(2)}, u32[]{:S(2)}) %collective-permute-start.32) | collective-permute-done | bytes 1048608 | tf_op jit(solution)/shard_map/ppermute | solution.py:319
  470.0 3.7 bitcast_add_fusion.7
  475.0 17.5 %collective-permute-done.41 = bf16[512,1024]{1,0:T(8,128)(2,1)} collective-permute-done((bf16[512,1024]{1,0:T(8,128)(2,1)}, bf16[512,1024]{1,0:T(8,128)(2,1)}, u32[]{:S(2)}, u32[]{:S(2)}) %collective-permute-start.41) | collective-permute-done | bytes 1048608 | tf_op jit(solution)/shard_map/ppermute | solution.py:319
  492.5 3.3 bitcast_add_fusion.3
  497.1 4.0 collective-permute-start.33
  501.1 29.5 %collective-permute-done.35 = bf16[512,1024]{1,0:T(8,128)(2,1)} collective-permute-done((bf16[512,1024]{1,0:T(8,128)(2,1)}, bf16[512,1024]{1,0:T(8,128)(2,1)}, u32[]{:S(2)}, u32[]{:S(2)}) %collective-permute-start.35) | collective-permute-done | bytes 1048608 | tf_op jit(solution)/shard_map/ppermute | solution.py:320
  530.6 2.7 bitcast_add_fusion.5
  535.2 3.6 collective-permute-start.42
  538.8 14.2 %collective-permute-done.44 = bf16[512,1024]{1,0:T(8,128)(2,1)} collective-permute-done((bf16[512,1024]{1,0:T(8,128)(2,1)}, bf16[512,1024]{1,0:T(8,128)(2,1)}, u32[]{:S(2)}, u32[]{:S(2)}) %collective-permute-start.44) | collective-permute-done | bytes 1048608 | tf_op jit(solution)/shard_map/ppermute | solution.py:320
  553.1 2.6 bitcast_add_fusion.1
  557.6 17.9 %collective-permute-done.36 = bf16[512,1024]{1,0:T(8,128)(2,1)} collective-permute-done((bf16[512,1024]{1,0:T(8,128)(2,1)}, bf16[512,1024]{1,0:T(8,128)(2,1)}, u32[]{:S(2)}, u32[]{:S(2)}) %collective-permute-start.36) | collective-permute-done | bytes 1048608 | tf_op jit(solution)/shard_map/ppermute | solution.py:320
  575.5 3.1 fusion.3
  580.5 17.5 %collective-permute-done.45 = bf16[512,1024]{1,0:T(8,128)(2,1)} collective-permute-done((bf16[512,1024]{1,0:T(8,128)(2,1)}, bf16[512,1024]{1,0:T(8,128)(2,1)}, u32[]{:S(2)}, u32[]{:S(2)}) %collective-permute-start.45) | collective-permute-done | bytes 1048608 | tf_op jit(solution)/shard_map/ppermute | solution.py:320
  598.0 3.5 fusion.1
  601.4 2.6 reshape.82
  604.1 8.6 %constant_dynamic-slice_fusion.5 = (bf16[512,1,256]{2,1,0:T(2,128)(2,1)}, bf16[512,1,256]{2,1,0:T(2,128)(2,1)S(1)}, bf16[512,1,256]{2,1,0:T(2,128)(2,1)S(1)}, bf...) fusion(bf16[512,4,256]{2,1,0:T(4,128)(2,1)} %reshape.82, ...), kind=kLoop, calls=%fused_computation.57 | loop fusion | bytes 4194320 | tf_op jit(solution)/shard_map/jit(dynamic_index_in_dim)/dynamic_slice | solution.py:398
  621.3 4.9 shard_map.91
  626.3 2.5 collective-permute-done.48
  630.1 3.9 collective-permute-done.38
  633.9 5.7 collective-permute-done.39
  640.9 2.7 shard_map.94
  (162 shorter events, 90.0 us)
Async XLA Ops:
  0.7 12.4 %copy-start = (bf16[4,128,2048]{2,1,0:T(8,128)(2,1)S(1)}, bf16[4,128,2048]{2,1,0:T(8,128)(2,1)}, u32[]{:S(2)}) copy-start(bf16[4,128,2048]{2,1,0:T(8,128)(2,1)} %q_ref.1) | copy-start | bytes 6291460
  0.7 79.9 %collective-permute-start = (bf16[3,256,4096]{2,1,0:T(8,128)(2,1)}, bf16[3,256,4096]{2,1,0:T(8,128)(2,1)}, u32[]{:S(2)}, u32[]{:S(2)}) collective-permute-start(bf16[3,256,4096]{2,1,0:T(8,128)(2,1)} %param.6), channel_id=1, source_target_pairs={{0,8},{8,0},{16,24},{24,16},{1,9},{9,1},{17,25},{25,17},{2,10},{10... | collective-permute-start | bytes 18874376 | tf_op jit(solution)/shard_map/ppermute | solution.py:344
  5.2 75.1 %collective-permute-start.1 = (bf16[1,128,4096]{2,1,0:T(8,128)(2,1)}, bf16[1,128,4096]{2,1,0:T(8,128)(2,1)}, u32[]{:S(2)}, u32[]{:S(2)}) collective-permute-start(bf16[1,128,4096]{2,1,0:T(8,128)(2,1)} %get-tuple-element.27), channel_id=1, source_target_pairs={{0,16},{8,24},{16,0},{24,8},{1,17},{9,25},{17,1},{25,9},{2,18},{10... | collective-permute-start | bytes 3145736 | tf_op jit(solution)/shard_map/ppermute | solution.py:347
  9.1 14.4 %copy-start.8 = (bf16[4,256,512]{2,1,0:T(8,128)(2,1)S(1)}, bf16[4,256,512]{2,1,0:T(8,128)(2,1)}, u32[]{:S(2)}) copy-start(bf16[4,256,512]{2,1,0:T(8,128)(2,1)} %copy-done.7) | copy-start | bytes 3145732
  10.0 14.6 %collective-permute-start.13 = (bf16[256,512]{1,0:T(8,128)(2,1)}, bf16[256,512]{1,0:T(8,128)(2,1)}, u32[]{:S(2)}, u32[]{:S(2)}) collective-permute-start(bf16[256,512]{1,0:T(8,128)(2,1)} %get-tuple-element.51), channel_id=1, source_target_pairs={{0,8},{8,0},{16,24},{24,16},{1,9},{9,1},{17,25},{25,17},{2,10},{10... | collective-permute-start | bytes 786440 | tf_op jit(solution)/shard_map/ppermute | solution.py:292
  10.3 30.1 %collective-permute-start.14 = (bf16[256,512]{1,0:T(8,128)(2,1)}, bf16[256,512]{1,0:T(8,128)(2,1)}, u32[]{:S(2)}, u32[]{:S(2)}) collective-permute-start(bf16[256,512]{1,0:T(8,128)(2,1)} %get-tuple-element.50), channel_id=1, source_target_pairs={{0,16},{8,24},{16,0},{24,8},{1,17},{9,25},{17,1},{25,9},{2,18},{10... | collective-permute-start | bytes 786440 | tf_op jit(solution)/shard_map/ppermute | solution.py:292
  10.5 40.1 %collective-permute-start.15 = (bf16[256,512]{1,0:T(8,128)(2,1)}, bf16[256,512]{1,0:T(8,128)(2,1)}, u32[]{:S(2)}, u32[]{:S(2)}) collective-permute-start(bf16[256,512]{1,0:T(8,128)(2,1)} %get-tuple-element.49), channel_id=1, source_target_pairs={{0,24},{8,16},{16,8},{24,0},{1,25},{9,17},{17,9},{25,1},{2,26},{10... | collective-permute-start | bytes 786440 | tf_op jit(solution)/shard_map/ppermute | solution.py:292
  18.5 183.0 %all-to-all-start.2 = ((bf16[16,2,128,256]{3,2,1,0:T(8,128)(2,1)}), bf16[16,2,128,256]{3,2,1,0:T(8,128)(2,1)S(1)}, u32[]{:S(2)}, u32[]{:S(2)}) async-start(bf16[16,2,128,256]{3,2,1,0:T(8,128)(2,1)} %bitcast.123), calls=%async_computation.2 | async-start | bytes 4194304 | tf_op jit(solution)/shard_map/all_to_all | solution.py:388
  24.6 40.9 %collective-permute-start.22 = (bf16[256,512]{1,0:T(8,128)(2,1)}, bf16[256,512]{1,0:T(8,128)(2,1)}, u32[]{:S(2)}, u32[]{:S(2)}) collective-permute-start(bf16[256,512]{1,0:T(8,128)(2,1)} %get-tuple-element.47), channel_id=1, source_target_pairs={{0,8},{8,0},{16,24},{24,16},{1,9},{9,1},{17,25},{25,17},{2,10},{10... | collective-permute-start | bytes 786440 | tf_op jit(solution)/shard_map/ppermute | solution.py:292
  40.4 29.3 %collective-permute-start.23 = (bf16[256,512]{1,0:T(8,128)(2,1)}, bf16[256,512]{1,0:T(8,128)(2,1)}, u32[]{:S(2)}, u32[]{:S(2)}) collective-permute-start(bf16[256,512]{1,0:T(8,128)(2,1)} %get-tuple-element.46), channel_id=1, source_target_pairs={{0,16},{8,24},{16,0},{24,8},{1,17},{9,25},{17,1},{25,9},{2,18},{10... | collective-permute-start | bytes 786440 | tf_op jit(solution)/shard_map/ppermute | solution.py:292
  50.7 25.1 %collective-permute-start.24 = (bf16[256,512]{1,0:T(8,128)(2,1)}, bf16[256,512]{1,0:T(8,128)(2,1)}, u32[]{:S(2)}, u32[]{:S(2)}) collective-permute-start(bf16[256,512]{1,0:T(8,128)(2,1)} %get-tuple-element.45), channel_id=1, source_target_pairs={{0,24},{8,16},{16,8},{24,0},{1,25},{9,17},{17,9},{25,1},{2,26},{10... | collective-permute-start | bytes 786440 | tf_op jit(solution)/shard_map/ppermute | solution.py:292
  65.5 32.2 %copy-start.16 = (bf16[4,256,512]{2,1,0:T(8,128)(2,1)}, bf16[4,256,512]{2,1,0:T(8,128)(2,1)S(1)}, u32[]{:S(2)}) copy-start(bf16[4,256,512]{2,1,0:T(8,128)(2,1)S(1)} %pad_maximum_fusion.refs_0_) | copy-start | bytes 3145732
  65.5 32.1 %collective-permute-start.5 = (bf16[1,128,4096]{2,1,0:T(8,128)(2,1)}, bf16[1,128,4096]{2,1,0:T(8,128)(2,1)S(1)}, u32[]{:S(2)}, u32[]{:S(2)}) collective-permute-start(bf16[1,128,4096]{2,1,0:T(8,128)(2,1)} %get-tuple-element.26), channel_id=1, source_target_pairs={{0,16},{8,24},{16,0},{24,8},{1,17},{9,25},{17,1},{25,9},{2,18},{10... | collective-permute-start | bytes 3145736 | tf_op jit(solution)/shard_map/ppermute | solution.py:347
  69.7 50.5 %collective-permute-start.9 = (bf16[1,128,4096]{2,1,0:T(8,128)(2,1)}, bf16[1,128,4096]{2,1,0:T(8,128)(2,1)S(1)}, u32[]{:S(2)}, u32[]{:S(2)}) collective-permute-start(bf16[1,128,4096]{2,1,0:T(8,128)(2,1)} %get-tuple-element.25), channel_id=1, source_target_pairs={{0,16},{8,24},{16,0},{24,8},{1,17},{9,25},{17,1},{25,9},{2,18},{10... | collective-permute-start | bytes 3145736 | tf_op jit(solution)/shard_map/ppermute | solution.py:347
  75.8 47.6 %collective-permute-start.16 = (bf16[4,256,512]{2,1,0:T(8,128)(2,1)S(1)}, bf16[4,256,512]{2,1,0:T(8,128)(2,1)S(1)}, u32[]{:S(2)}, u32[]{:S(2)}) collective-permute-start(bf16[4,256,512]{2,1,0:T(8,128)(2,1)S(1)} %pad_maximum_fusion.refs_0_), channel_id=1, source_target_pairs={{0,2},{2,4},{4,6},{1,3},{3,5},{5,7},{8,10},{10,12},{12,14},{9,11},... | collective-permute-start | bytes 3145736 | tf_op jit(solution)/shard_map/ppermute | solution.py:301
  80.3 43.1 %copy-start.17 = (bf16[4,256,512]{2,1,0:T(8,128)(2,1)}, bf16[4,256,512]{2,1,0:T(8,128)(2,1)S(1)}, u32[]{:S(2)}) copy-start(bf16[4,256,512]{2,1,0:T(8,128)(2,1)S(1)} %pad_maximum_fusion.1.refs_0_) | copy-start | bytes 3145732
  80.3 19.3 %collective-permute-start.2 = (bf16[1,128,4096]{2,1,0:T(8,128)(2,1)}, bf16[1,128,4096]{2,1,0:T(8,128)(2,1)S(1)}, u32[]{:S(2)}, u32[]{:S(2)}) collective-permute-start(bf16[1,128,4096]{2,1,0:T(8,128)(2,1)} %collective-permute-done.1), channel_id=1, source_target_pairs={{0,8},{8,0},{16,24},{24,16},{1,9},{9,1},{17,25},{25,17},{2,10},{10... | collective-permute-start | bytes 3145736 | tf_op jit(solution)/shard_map/ppermute | solution.py:349
  80.6 24.7 %collective-permute-start.3 = (bf16[1,128,4096]{2,1,0:T(8,128)(2,1)}, bf16[1,128,4096]{2,1,0:T(8,128)(2,1)S(1)}, u32[]{:S(2)}, u32[]{:S(2)}) collective-permute-start(bf16[1,128,4096]{2,1,0:T(8,128)(2,1)} %collective-permute-done.1), channel_id=1, source_target_pairs={{0,1},{1,0},{2,3},{3,2},{4,5},{5,4},{6,7},{7,6},{8,9},{9,8},{10,11... | collective-permute-start | bytes 3145736 | tf_op jit(solution)/shard_map/ppermute | solution.py:348
  97.7 38.7 %collective-permute-start.19 = (bf16[4,256,512]{2,1,0:T(8,128)(2,1)S(1)}, bf16[4,256,512]{2,1,0:T(8,128)(2,1)S(1)}, u32[]{:S(2)}, u32[]{:S(2)}) collective-permute-start(bf16[4,256,512]{2,1,0:T(8,128)(2,1)S(1)} %pad_maximum_fusion.refs_0_), channel_id=1, source_target_pairs={{2,0},{4,2},{6,4},{3,1},{5,3},{7,5},{10,8},{12,10},{14,12},{11,9},... | collective-permute-start | bytes 3145736 | tf_op jit(solution)/shard_map/ppermute | solution.py:302
  99.6 25.9 %collective-permute-start.6 = (bf16[1,128,4096]{2,1,0:T(8,128)(2,1)S(1)}, bf16[1,128,4096]{2,1,0:T(8,128)(2,1)S(1)}, u32[]{:S(2)}, u32[]{:S(2)}) collective-permute-start(bf16[1,128,4096]{2,1,0:T(8,128)(2,1)S(1)} %collective-permute-done.5), channel_id=1, source_target_pairs={{0,8},{8,0},{16,24},{24,16},{1,9},{9,1},{17,25},{25,17},{2,10},{10... | collective-permute-start | bytes 3145736 | tf_op jit(solution)/shard_map/ppermute | solution.py:349
  105.3 3.4 collective-permute-start.4
  108.7 24.4 %collective-permute-start.7 = (bf16[1,128,4096]{2,1,0:T(8,128)(2,1)S(1)}, bf16[1,128,4096]{2,1,0:T(8,128)(2,1)S(1)}, u32[]{:S(2)}, u32[]{:S(2)}) collective-permute-start(bf16[1,128,4096]{2,1,0:T(8,128)(2,1)S(1)} %collective-permute-done.5), channel_id=1, source_target_pairs={{0,1},{1,0},{2,3},{3,2},{4,5},{5,4},{6,7},{7,6},{8,9},{9,8},{10,11... | collective-permute-start | bytes 3145736 | tf_op jit(solution)/shard_map/ppermute | solution.py:348
  120.1 25.8 %collective-permute-start.25 = (bf16[4,256,512]{2,1,0:T(8,128)(2,1)S(1)}, bf16[4,256,512]{2,1,0:T(8,128)(2,1)S(1)}, u32[]{:S(2)}, u32[]{:S(2)}) collective-permute-start(bf16[4,256,512]{2,1,0:T(8,128)(2,1)S(1)} %pad_maximum_fusion.1.refs_0_), channel_id=1, source_target_pairs={{0,2},{2,4},{4,6},{1,3},{3,5},{5,7},{8,10},{10,12},{12,14},{9,11},... | collective-permute-start | bytes 3145736 | tf_op jit(solution)/shard_map/ppermute | solution.py:301
  123.4 77.1 %copy-start.19 = (bf16[4,256,512]{2,1,0:T(8,128)(2,1)}, bf16[4,256,512]{2,1,0:T(8,128)(2,1)S(1)}, u32[]{:S(2)}) copy-start(bf16[4,256,512]{2,1,0:T(8,128)(2,1)S(1)} %collective-permute-done.16.refs_1_) | copy-start | bytes 3145732
  123.4 26.7 %collective-permute-start.28 = (bf16[4,256,512]{2,1,0:T(8,128)(2,1)S(1)}, bf16[4,256,512]{2,1,0:T(8,128)(2,1)S(1)}, u32[]{:S(2)}, u32[]{:S(2)}) collective-permute-start(bf16[4,256,512]{2,1,0:T(8,128)(2,1)S(1)} %pad_maximum_fusion.1.refs_0_), channel_id=1, source_target_pairs={{2,0},{4,2},{6,4},{3,1},{5,3},{7,5},{10,8},{12,10},{14,12},{11,9},... | collective-permute-start | bytes 3145736 | tf_op jit(solution)/shard_map/ppermute | solution.py:302
  125.5 26.5 %collective-permute-start.10 = (bf16[1,128,4096]{2,1,0:T(8,128)(2,1)S(1)}, bf16[1,128,4096]{2,1,0:T(8,128)(2,1)S(1)}, u32[]{:S(2)}, u32[]{:S(2)}) collective-permute-start(bf16[1,128,4096]{2,1,0:T(8,128)(2,1)S(1)} %collective-permute-done.9), channel_id=1, source_target_pairs={{0,8},{8,0},{16,24},{24,16},{1,9},{9,1},{17,25},{25,17},{2,10},{10... | collective-permute-start | bytes 3145736 | tf_op jit(solution)/shard_map/ppermute | solution.py:349
  133.0 24.3 %collective-permute-start.8 = (bf16[1,128,4096]{2,1,0:T(8,128)(2,1)S(1)}, bf16[1,128,4096]{2,1,0:T(8,128)(2,1)S(1)}, u32[]{:S(2)}, u32[]{:S(2)}) collective-permute-start(bf16[1,128,4096]{2,1,0:T(8,128)(2,1)S(1)} %collective-permute-done.7), channel_id=1, source_target_pairs={{0,8},{8,0},{16,24},{24,16},{1,9},{9,1},{17,25},{25,17},{2,10},{10... | collective-permute-start | bytes 3145736 | tf_op jit(solution)/shard_map/ppermute | solution.py:350
  136.4 64.1 %copy-start.20 = (bf16[4,256,512]{2,1,0:T(8,128)(2,1)}, bf16[4,256,512]{2,1,0:T(8,128)(2,1)S(1)}, u32[]{:S(2)}) copy-start(bf16[4,256,512]{2,1,0:T(8,128)(2,1)S(1)} %collective-permute-done.19.refs_4_) | copy-start | bytes 3145732
  136.4 25.1 %collective-permute-start.11 = (bf16[1,128,4096]{2,1,0:T(8,128)(2,1)S(1)}, bf16[1,128,4096]{2,1,0:T(8,128)(2,1)S(1)}, u32[]{:S(2)}, u32[]{:S(2)}) collective-permute-start(bf16[1,128,4096]{2,1,0:T(8,128)(2,1)S(1)} %collective-permute-done.9), channel_id=1, source_target_pairs={{0,1},{1,0},{2,3},{3,2},{4,5},{5,4},{6,7},{7,6},{8,9},{9,8},{10,11... | collective-permute-start | bytes 3145736 | tf_op jit(solution)/shard_map/ppermute | solution.py:348
  145.9 54.5 %copy-start.21 = (bf16[4,256,512]{2,1,0:T(8,128)(2,1)}, bf16[4,256,512]{2,1,0:T(8,128)(2,1)S(1)}, u32[]{:S(2)}) copy-start(bf16[4,256,512]{2,1,0:T(8,128)(2,1)S(1)} %collective-permute-done.25.refs_1_) | copy-start | bytes 3145732
  145.9 23.9 %collective-permute-start.17 = (bf16[4,256,512]{2,1,0:T(8,128)(2,1)S(1)}, bf16[4,256,512]{2,1,0:T(8,128)(2,1)}, u32[]{:S(2)}, u32[]{:S(2)}) collective-permute-start(bf16[4,256,512]{2,1,0:T(8,128)(2,1)S(1)} %collective-permute-done.16.refs_1_), channel_id=1, source_target_pairs={{2,4},{4,6},{3,5},{5,7},{10,12},{12,14},{11,13},{13,15},{18,20},{2... | collective-permute-start | bytes 3145736 | tf_op jit(solution)/shard_map/ppermute | solution.py:301
  150.1 50.3 %copy-start.22 = (bf16[4,256,512]{2,1,0:T(8,128)(2,1)}, bf16[4,256,512]{2,1,0:T(8,128)(2,1)S(1)}, u32[]{:S(2)}) copy-start(bf16[4,256,512]{2,1,0:T(8,128)(2,1)S(1)} %collective-permute-done.28.refs_4_) | copy-start | bytes 3145732
  150.1 24.7 %collective-permute-start.20 = (bf16[4,256,512]{2,1,0:T(8,128)(2,1)S(1)}, bf16[4,256,512]{2,1,0:T(8,128)(2,1)}, u32[]{:S(2)}, u32[]{:S(2)}) collective-permute-start(bf16[4,256,512]{2,1,0:T(8,128)(2,1)S(1)} %collective-permute-done.19.refs_4_), channel_id=1, source_target_pairs={{2,0},{4,2},{3,1},{5,3},{10,8},{12,10},{11,9},{13,11},{18,16},{20,... | collective-permute-start | bytes 3145736 | tf_op jit(solution)/shard_map/ppermute | solution.py:302
  152.0 40.3 %collective-permute-start.26 = (bf16[4,256,512]{2,1,0:T(8,128)(2,1)S(1)}, bf16[4,256,512]{2,1,0:T(8,128)(2,1)}, u32[]{:S(2)}, u32[]{:S(2)}) collective-permute-start(bf16[4,256,512]{2,1,0:T(8,128)(2,1)S(1)} %collective-permute-done.25.refs_1_), channel_id=1, source_target_pairs={{2,4},{4,6},{3,5},{5,7},{10,12},{12,14},{11,13},{13,15},{18,20},{2... | collective-permute-start | bytes 3145736 | tf_op jit(solution)/shard_map/ppermute | solution.py:301
  157.3 39.9 %collective-permute-start.29 = (bf16[4,256,512]{2,1,0:T(8,128)(2,1)S(1)}, bf16[4,256,512]{2,1,0:T(8,128)(2,1)}, u32[]{:S(2)}, u32[]{:S(2)}) collective-permute-start(bf16[4,256,512]{2,1,0:T(8,128)(2,1)S(1)} %collective-permute-done.28.refs_4_), channel_id=1, source_target_pairs={{2,0},{4,2},{3,1},{5,3},{10,8},{12,10},{11,9},{13,11},{18,16},{20,... | collective-permute-start | bytes 3145736 | tf_op jit(solution)/shard_map/ppermute | solution.py:302
  161.4 51.9 %collective-permute-start.12 = (bf16[1,128,4096]{2,1,0:T(8,128)(2,1)S(1)}, bf16[1,128,4096]{2,1,0:T(8,128)(2,1)}, u32[]{:S(2)}, u32[]{:S(2)}) collective-permute-start(bf16[1,128,4096]{2,1,0:T(8,128)(2,1)S(1)} %collective-permute-done.11), channel_id=1, source_target_pairs={{0,8},{8,0},{16,24},{24,16},{1,9},{9,1},{17,25},{25,17},{2,10},{10... | collective-permute-start | bytes 3145736 | tf_op jit(solution)/shard_map/ppermute | solution.py:350
  169.9 139.2 %collective-permute-start.18 = (bf16[4,256,512]{2,1,0:T(8,128)(2,1)}, bf16[4,256,512]{2,1,0:T(8,128)(2,1)}, u32[]{:S(2)}, u32[]{:S(2)}) collective-permute-start(bf16[4,256,512]{2,1,0:T(8,128)(2,1)} %collective-permute-done.17.refs_2_), channel_id=1, source_target_pairs={{4,6},{5,7},{12,14},{13,15},{20,22},{21,23},{28,30},{29,31}} | collective-permute-start | bytes 3145736 | tf_op jit(solution)/shard_map/ppermute | solution.py:301
  174.8 134.3 %collective-permute-start.21 = (bf16[4,256,512]{2,1,0:T(8,128)(2,1)}, bf16[4,256,512]{2,1,0:T(8,128)(2,1)}, u32[]{:S(2)}, u32[]{:S(2)}) collective-permute-start(bf16[4,256,512]{2,1,0:T(8,128)(2,1)} %collective-permute-done.20.refs_5_), channel_id=1, source_target_pairs={{2,0},{3,1},{10,8},{11,9},{18,16},{19,17},{26,24},{27,25}} | collective-permute-start | bytes 3145736 | tf_op jit(solution)/shard_map/ppermute | solution.py:302
  192.3 23.3 %collective-permute-start.27 = (bf16[4,256,512]{2,1,0:T(8,128)(2,1)}, bf16[4,256,512]{2,1,0:T(8,128)(2,1)}, u32[]{:S(2)}, u32[]{:S(2)}) collective-permute-start(bf16[4,256,512]{2,1,0:T(8,128)(2,1)} %collective-permute-done.26.refs_2_), channel_id=1, source_target_pairs={{4,6},{5,7},{12,14},{13,15},{20,22},{21,23},{28,30},{29,31}} | collective-permute-start | bytes 3145736 | tf_op jit(solution)/shard_map/ppermute | solution.py:301
  197.2 65.5 %collective-permute-start.30 = (bf16[4,256,512]{2,1,0:T(8,128)(2,1)}, bf16[4,256,512]{2,1,0:T(8,128)(2,1)}, u32[]{:S(2)}, u32[]{:S(2)}) collective-permute-start(bf16[4,256,512]{2,1,0:T(8,128)(2,1)} %collective-permute-done.29.refs_5_), channel_id=1, source_target_pairs={{2,0},{3,1},{10,8},{11,9},{18,16},{19,17},{26,24},{27,25}} | collective-permute-start | bytes 3145736 | tf_op jit(solution)/shard_map/ppermute | solution.py:302
  201.5 127.7 %all-to-all-start = ((bf16[16,2,128,256]{3,2,1,0:T(8,128)(2,1)}), bf16[16,2,128,256]{3,2,1,0:T(8,128)(2,1)}, u32[]{:S(2)}, u32[]{:S(2)}) async-start(bf16[16,2,128,256]{3,2,1,0:T(8,128)(2,1)} %bitcast.25), calls=%async_computation | async-start | bytes 4194304 | tf_op jit(solution)/shard_map/all_to_all | solution.py:388
  329.3 122.8 %all-to-all-start.3 = ((bf16[16,2,128,256]{3,2,1,0:T(8,128)(2,1)}), bf16[16,2,128,256]{3,2,1,0:T(8,128)(2,1)S(1)}, u32[]{:S(2)}, u32[]{:S(2)}) async-start(bf16[16,2,128,256]{3,2,1,0:T(8,128)(2,1)} %bitcast.125), calls=%async_computation.3 | async-start | bytes 4194304 | tf_op jit(solution)/shard_map/all_to_all | solution.py:402
  392.8 30.1 %collective-permute-start.31 = (bf16[512,1024]{1,0:T(8,128)(2,1)}, bf16[512,1024]{1,0:T(8,128)(2,1)}, u32[]{:S(2)}, u32[]{:S(2)}) collective-permute-start(bf16[512,1024]{1,0:T(8,128)(2,1)} %get-tuple-element.34), channel_id=1, source_target_pairs={{0,2},{1,3},{8,10},{9,11},{16,18},{17,19},{24,26},{25,27}} | collective-permute-start | bytes 3145736 | tf_op jit(solution)/shard_map/ppermute | solution.py:319
  420.0 27.6 %collective-permute-start.40 = (bf16[512,1024]{1,0:T(8,128)(2,1)}, bf16[512,1024]{1,0:T(8,128)(2,1)}, u32[]{:S(2)}, u32[]{:S(2)}) collective-permute-start(bf16[512,1024]{1,0:T(8,128)(2,1)} %get-tuple-element.30), channel_id=1, source_target_pairs={{0,2},{1,3},{8,10},{9,11},{16,18},{17,19},{24,26},{25,27}} | collective-permute-start | bytes 3145736 | tf_op jit(solution)/shard_map/ppermute | solution.py:319
  421.3 39.6 %collective-permute-start.34 = (bf16[512,1024]{1,0:T(8,128)(2,1)}, bf16[512,1024]{1,0:T(8,128)(2,1)}, u32[]{:S(2)}, u32[]{:S(2)}) collective-permute-start(bf16[512,1024]{1,0:T(8,128)(2,1)} %get-tuple-element.35), channel_id=1, source_target_pairs={{6,4},{7,5},{14,12},{15,13},{22,20},{23,21},{30,28},{31,29}} | collective-permute-start | bytes 3145736 | tf_op jit(solution)/shard_map/ppermute | solution.py:320
  425.6 44.4 %collective-permute-start.32 = (bf16[512,1024]{1,0:T(8,128)(2,1)}, bf16[512,1024]{1,0:T(8,128)(2,1)}, u32[]{:S(2)}, u32[]{:S(2)}) collective-permute-start(bf16[512,1024]{1,0:T(8,128)(2,1)} %bitcast_add_fusion.6), channel_id=1, source_target_pairs={{0,2},{2,4},{1,3},{3,5},{8,10},{10,12},{9,11},{11,13},{16,18},{18,... | collective-permute-start | bytes 3145736 | tf_op jit(solution)/shard_map/ppermute | solution.py:319
  429.0 46.0 %collective-permute-start.43 = (bf16[512,1024]{1,0:T(8,128)(2,1)S(1)}, bf16[512,1024]{1,0:T(8,128)(2,1)}, u32[]{:S(2)}, u32[]{:S(2)}) collective-permute-start(bf16[512,1024]{1,0:T(8,128)(2,1)S(1)} %get-tuple-element.31), channel_id=1, source_target_pairs={{6,4},{7,5},{14,12},{15,13},{22,20},{23,21},{30,28},{31,29}} | collective-permute-start | bytes 3145736 | tf_op jit(solution)/shard_map/ppermute | solution.py:320
  450.2 42.3 %collective-permute-start.41 = (bf16[512,1024]{1,0:T(8,128)(2,1)}, bf16[512,1024]{1,0:T(8,128)(2,1)}, u32[]{:S(2)}, u32[]{:S(2)}) collective-permute-start(bf16[512,1024]{1,0:T(8,128)(2,1)} %bitcast_add_fusion.2), channel_id=1, source_target_pairs={{0,2},{2,4},{1,3},{3,5},{8,10},{10,12},{9,11},{11,13},{16,18},{18,... | collective-permute-start | bytes 3145736 | tf_op jit(solution)/shard_map/ppermute | solution.py:319
  452.1 169.2 %all-to-all-start.1 = ((bf16[16,2,128,256]{3,2,1,0:T(8,128)(2,1)}), bf16[16,2,128,256]{3,2,1,0:T(8,128)(2,1)}, u32[]{:S(2)}, u32[]{:S(2)}) async-start(bf16[16,2,128,256]{3,2,1,0:T(8,128)(2,1)} %bitcast.124), calls=%async_computation.1 | async-start | bytes 4194304 | tf_op jit(solution)/shard_map/all_to_all | solution.py:402
  460.9 31.6 %copy-start.13 = (bf16[4,512,1024]{2,1,0:T(8,128)(2,1)S(1)}, bf16[4,512,1024]{2,1,0:T(8,128)(2,1)}, u32[]{:S(2)}) copy-start(bf16[4,512,1024]{2,1,0:T(8,128)(2,1)} %shard_map.93) | copy-start | bytes 12582916
  473.7 56.9 %collective-permute-start.35 = (bf16[512,1024]{1,0:T(8,128)(2,1)}, bf16[512,1024]{1,0:T(8,128)(2,1)}, u32[]{:S(2)}, u32[]{:S(2)}) collective-permute-start(bf16[512,1024]{1,0:T(8,128)(2,1)} %get-tuple-element.33), channel_id=1, source_target_pairs={{4,2},{6,4},{5,3},{7,5},{12,10},{14,12},{13,11},{15,13},{20,18},{2... | collective-permute-start | bytes 3145736 | tf_op jit(solution)/shard_map/ppermute | solution.py:320
  495.8 57.3 %collective-permute-start.44 = (bf16[512,1024]{1,0:T(8,128)(2,1)}, bf16[512,1024]{1,0:T(8,128)(2,1)}, u32[]{:S(2)}, u32[]{:S(2)}) collective-permute-start(bf16[512,1024]{1,0:T(8,128)(2,1)} %get-tuple-element.29), channel_id=1, source_target_pairs={{4,2},{6,4},{5,3},{7,5},{12,10},{14,12},{13,11},{15,13},{20,18},{2... | collective-permute-start | bytes 3145736 | tf_op jit(solution)/shard_map/ppermute | solution.py:320
  497.1 60.5 %collective-permute-start.33 = (bf16[512,1024]{1,0:T(8,128)(2,1)}, bf16[512,1024]{1,0:T(8,128)(2,1)S(1)}, u32[]{:S(2)}, u32[]{:S(2)}) collective-permute-start(bf16[512,1024]{1,0:T(8,128)(2,1)} %get-tuple-element.32), channel_id=1, source_target_pairs={{0,2},{2,4},{4,6},{1,3},{3,5},{5,7},{8,10},{10,12},{12,14},{9,11},... | collective-permute-start | bytes 3145736 | tf_op jit(solution)/shard_map/ppermute | solution.py:319
  533.3 42.2 %collective-permute-start.36 = (bf16[512,1024]{1,0:T(8,128)(2,1)}, bf16[512,1024]{1,0:T(8,128)(2,1)}, u32[]{:S(2)}, u32[]{:S(2)}) collective-permute-start(bf16[512,1024]{1,0:T(8,128)(2,1)} %bitcast_add_fusion.5), channel_id=1, source_target_pairs={{2,0},{4,2},{6,4},{3,1},{5,3},{7,5},{10,8},{12,10},{14,12},{11,9},... | collective-permute-start | bytes 3145736 | tf_op jit(solution)/shard_map/ppermute | solution.py:320
  535.2 45.3 %collective-permute-start.42 = (bf16[512,1024]{1,0:T(8,128)(2,1)}, bf16[512,1024]{1,0:T(8,128)(2,1)}, u32[]{:S(2)}, u32[]{:S(2)}) collective-permute-start(bf16[512,1024]{1,0:T(8,128)(2,1)} %get-tuple-element.28), channel_id=1, source_target_pairs={{0,2},{2,4},{4,6},{1,3},{3,5},{5,7},{8,10},{10,12},{12,14},{9,11},... | collective-permute-start | bytes 3145736 | tf_op jit(solution)/shard_map/ppermute | solution.py:319
  555.7 42.3 %collective-permute-start.45 = (bf16[512,1024]{1,0:T(8,128)(2,1)}, bf16[512,1024]{1,0:T(8,128)(2,1)}, u32[]{:S(2)}, u32[]{:S(2)}) collective-permute-start(bf16[512,1024]{1,0:T(8,128)(2,1)} %bitcast_add_fusion.1), channel_id=1, source_target_pairs={{2,0},{4,2},{6,4},{3,1},{5,3},{7,5},{10,8},{12,10},{14,12},{11,9},... | collective-permute-start | bytes 3145736 | tf_op jit(solution)/shard_map/ppermute | solution.py:320
  612.7 13.4 %copy-start.15 = (bf16[512,1,256]{2,1,0:T(2,128)(2,1)S(1)}, bf16[512,1,256]{2,1,0:T(2,128)(2,1)}, u32[]{:S(2)}) copy-start(bf16[512,1,256]{2,1,0:T(2,128)(2,1)} %get-tuple-element.36) | copy-start | bytes 786436
  612.7 13.5 %copy-start.14 = (bf16[512,1,256]{2,1,0:T(2,128)(2,1)S(1)}, bf16[512,1,256]{2,1,0:T(2,128)(2,1)}, u32[]{:S(2)}) copy-start(bf16[512,1,256]{2,1,0:T(2,128)(2,1)} %get-tuple-element.57) | copy-start | bytes 786436
  612.8 7.1 %collective-permute-start.46 = (bf16[512,256]{1,0:T(8,128)(2,1)S(1)}, bf16[512,256]{1,0:T(8,128)(2,1)S(1)}, u32[]{:S(2)}, u32[]{:S(2)}) collective-permute-start(bf16[512,256]{1,0:T(8,128)(2,1)S(1)} %bitcast.139), channel_id=1, source_target_pairs={{0,8},{8,0},{16,24},{24,16},{1,9},{9,1},{17,25},{25,17},{2,10},{10... | collective-permute-start | bytes 786440 | tf_op jit(solution)/shard_map/ppermute | solution.py:292
  614.5 11.8 %collective-permute-start.47 = (bf16[512,256]{1,0:T(8,128)(2,1)}, bf16[512,256]{1,0:T(8,128)(2,1)}, u32[]{:S(2)}, u32[]{:S(2)}) collective-permute-start(bf16[512,256]{1,0:T(8,128)(2,1)} %bitcast.114), channel_id=1, source_target_pairs={{0,16},{8,24},{16,0},{24,8},{1,17},{9,25},{17,1},{25,9},{2,18},{10... | collective-permute-start | bytes 786440 | tf_op jit(solution)/shard_map/ppermute | solution.py:292
  616.4 12.4 %collective-permute-start.48 = (bf16[512,256]{1,0:T(8,128)(2,1)}, bf16[512,256]{1,0:T(8,128)(2,1)}, u32[]{:S(2)}, u32[]{:S(2)}) collective-permute-start(bf16[512,256]{1,0:T(8,128)(2,1)} %bitcast.113), channel_id=1, source_target_pairs={{0,24},{8,16},{16,8},{24,0},{1,25},{9,17},{17,9},{25,1},{2,26},{10... | collective-permute-start | bytes 786440 | tf_op jit(solution)/shard_map/ppermute | solution.py:292
  616.9 13.2 %collective-permute-start.37 = (bf16[512,256]{1,0:T(8,128)(2,1)S(1)}, bf16[512,256]{1,0:T(8,128)(2,1)}, u32[]{:S(2)}, u32[]{:S(2)}) collective-permute-start(bf16[512,256]{1,0:T(8,128)(2,1)S(1)} %bitcast.138), channel_id=1, source_target_pairs={{0,8},{8,0},{16,24},{24,16},{1,9},{9,1},{17,25},{25,17},{2,10},{10... | collective-permute-start | bytes 786440 | tf_op jit(solution)/shard_map/ppermute | solution.py:292
  617.9 16.0 %collective-permute-start.38 = (bf16[512,256]{1,0:T(8,128)(2,1)}, bf16[512,256]{1,0:T(8,128)(2,1)}, u32[]{:S(2)}, u32[]{:S(2)}) collective-permute-start(bf16[512,256]{1,0:T(8,128)(2,1)} %bitcast.118), channel_id=1, source_target_pairs={{0,16},{8,24},{16,0},{24,8},{1,17},{9,25},{17,1},{25,9},{2,18},{10... | collective-permute-start | bytes 786440 | tf_op jit(solution)/shard_map/ppermute | solution.py:292
  620.6 19.1 %collective-permute-start.39 = (bf16[512,256]{1,0:T(8,128)(2,1)}, bf16[512,256]{1,0:T(8,128)(2,1)}, u32[]{:S(2)}, u32[]{:S(2)}) collective-permute-start(bf16[512,256]{1,0:T(8,128)(2,1)} %bitcast.117), channel_id=1, source_target_pairs={{0,24},{8,16},{16,8},{24,0},{1,25},{9,17},{17,9},{25,1},{2,26},{10... | collective-permute-start | bytes 786440 | tf_op jit(solution)/shard_map/ppermute | solution.py:292
  (15 other events, 52.4 us)

commit v2 on v1

v2 whole, which is shorter than its diff:
```python
import functools

import jax
import jax.numpy as jnp
from jax import lax
from jax.experimental import pallas as pl
from jax.experimental.pallas import tpu as pltpu
from jax.sharding import PartitionSpec as P

HEAD_DIM = 64
LANES = 128
CHUNKS = 2
MIB = 1024 * 1024
BF = jnp.bfloat16
F32 = jnp.float32


def dot(a, b, dims):
    return lax.dot_general(a, b, (dims, ((), ())), preferred_element_type=F32)


def params(mib):
    return pltpu.CompilerParams(vmem_limit_bytes=mib * MIB)


def pack_weights_kernel(chunks, cols, k_ref, v_ref, *outs):
    for c in range(chunks):
        outs[c][0, :, :cols] = k_ref[:, c * cols:(c + 1) * cols]
        outs[c][0, :, cols:] = v_ref[:, c * cols:(c + 1) * cols]


def pack_weights(me, w_key, w_value, n_section, chunks, cols):
    rows = w_key.shape[0]
    own = chunks * cols
    block = pl.BlockSpec((rows, own), lambda r, at: (0, at[0] ^ r))
    return pl.pallas_call(
        lambda at, *refs: pack_weights_kernel(chunks, cols, *refs),
        grid_spec=pltpu.PrefetchScalarGridSpec(
            num_scalar_prefetch=1,
            grid=(n_section,),
            in_specs=[block, block],
            out_specs=[pl.BlockSpec((1, rows, 2 * cols), lambda r, at: (r, 0, 0))] * chunks,
        ),
        out_shape=[jax.ShapeDtypeStruct((n_section, rows, 2 * cols), BF)] * chunks,
        compiler_params=params(32),
    )(me, w_key, w_value)


def pack_queries_kernel(n_section, all_filled, n_dp, at, q_ref, g_ref, *outs):
    q, g = q_ref[0], g_ref[0]
    if not all_filled:
        keep = at[n_dp + pl.program_id(0)] > 0
        q = jnp.where(keep, q, jnp.zeros_like(q))
        g = jnp.where(keep, g, jnp.zeros_like(g))
    chunks, cols = len(outs), outs[0].shape[-1]
    for s in range(n_section):
        for c in range(chunks):
            lo = (s * chunks + c) * cols
            outs[c][s, 0, 0] = q[:, lo:lo + cols]
            outs[c][s, 0, 1] = g[:, lo:lo + cols]


def pack_queries(slot, filled, query, grad, n_section, n_dp, chunks):
    dec_dev, q_rows, inner = query.shape
    cols = inner // (n_section * chunks)
    block = pl.BlockSpec((1, q_rows, inner), lambda p, at: (at[p], 0, 0))
    return pl.pallas_call(
        functools.partial(pack_queries_kernel, n_section, n_dp == dec_dev, n_dp),
        grid_spec=pltpu.PrefetchScalarGridSpec(
            num_scalar_prefetch=1,
            grid=(n_dp,),
            in_specs=[block, block],
            out_specs=[
                pl.BlockSpec((n_section, 1, 2, q_rows, cols), lambda p, at: (0, p, 0, 0, 0))
            ] * chunks,
        ),
        out_shape=[jax.ShapeDtypeStruct((n_section, n_dp, 2, q_rows, cols), BF)] * chunks,
        compiler_params=params(32),
    )(jnp.concatenate([slot, filled]).astype(jnp.int32), query, grad)


def unpack_outputs_kernel(n_section, chunks, cols, at, *refs):
    ctx_ref, gq_ref = refs[chunks * n_section:]
    me = at[0]
    for r in range(n_section):
        for c in range(chunks):
            block = refs[c * n_section + r]
            lo = pl.multiple_of(((me ^ r) * chunks + c) * cols, LANES)
            ctx_ref[0, :, pl.ds(lo, cols)] = block[0, 0]
            gq_ref[0, :, pl.ds(lo, cols)] = block[0, 1]


def unpack_outputs(me, distance, parts, dec_dev):
    chunks, n_section = len(parts), len(parts[0])
    _, _, q_rows, cols = parts[0][0].shape
    inner = n_section * chunks * cols
    block = pl.BlockSpec((1, 2, q_rows, cols), lambda j, at: (at[1 + j], 0, 0, 0))
    out = pl.BlockSpec((1, q_rows, inner), lambda j, at: (j, 0, 0))
    return pl.pallas_call(
        functools.partial(unpack_outputs_kernel, n_section, chunks, cols),
        grid_spec=pltpu.PrefetchScalarGridSpec(
            num_scalar_prefetch=1,
            grid=(dec_dev,),
            in_specs=[block] * (chunks * n_section),
            out_specs=[out, out],
        ),
        out_shape=[jax.ShapeDtypeStruct((dec_dev, q_rows, inner), BF)] * 2,
        compiler_params=params(32),
    )(jnp.concatenate([me, distance]), *[b for part in parts for b in part])


def project_kernel(n_dp, n_section, at, x_ref, all_ref, out_ref, w_ref):
    me = at[0]

    @pl.when(pl.program_id(0) == 0)
    def _():
        for d in range(n_dp):
            for r in range(n_section):
                w_ref[me ^ r, d] = all_ref[d, r]

    w = w_ref[...].reshape(x_ref.shape[1], out_ref.shape[1])
    out_ref[...] = dot(x_ref[...], w, ((1,), (0,))).astype(BF)


def project(me, flat, w_all):
    n_dp, n_section, rows, both = w_all.shape
    total, width = flat.shape
    tile = 512 if total % 512 == 0 else 256
    return pl.pallas_call(
        functools.partial(project_kernel, n_dp, n_section),
        grid_spec=pltpu.PrefetchScalarGridSpec(
            num_scalar_prefetch=1,
            grid=(total // tile,),
            in_specs=[
                pl.BlockSpec((tile, width), lambda i, at: (i, 0)),
                pl.BlockSpec(w_all.shape, lambda i, at: (0, 0, 0, 0)),
            ],
            out_specs=pl.BlockSpec((tile, both), lambda i, at: (i, 0)),
            scratch_shapes=[pltpu.VMEM((n_section, n_dp, rows, both), BF)],
        ),
        out_shape=jax.ShapeDtypeStruct((total, both), BF),
        compiler_params=params(56),
        cost_estimate=pl.CostEstimate(
            flops=2 * total * width * both,
            bytes_accessed=2 * (total * width + 2 * width * both + total * both),
            transcendentals=0,
        ),
    )(me, flat, w_all)


def weight_grad_kernel(n_section, rows, *refs):
    g_ref, out_ref = refs[n_section:]
    g = g_ref[...].reshape(out_ref.shape[0], g_ref.shape[2])
    for s in range(n_section):
        out_ref[:, s * rows:(s + 1) * rows] = dot(g, refs[s][...], ((1,), (0,))).astype(BF)


def weight_grad(flat, dkv, n_section, n_dp):
    total, width = flat.shape
    both = 2 * dkv.shape[1]
    rows = width // (n_section * n_dp)
    return pl.pallas_call(
        functools.partial(weight_grad_kernel, n_section, rows),
        grid=(n_dp,),
        in_specs=[
            pl.BlockSpec((total, rows), functools.partial(lambda s, d: (0, s * n_dp + d), s))
            for s in range(n_section)
        ] + [pl.BlockSpec((2, dkv.shape[1], total), lambda d: (0, 0, 0))],
        out_specs=pl.BlockSpec((both, n_section * rows), lambda d: (d, 0)),
        out_shape=jax.ShapeDtypeStruct((n_dp * both, n_section * rows), BF),
        compiler_params=params(56),
        cost_estimate=pl.CostEstimate(
            flops=2 * total * width * both,
            bytes_accessed=2 * (total * width + width * both + total * both),
            transcendentals=0,
        ),
    )(*([flat] * n_section), dkv)


def attend_kernel(seqs, ex_dev, seq_len, q_rows, local_ref, k_ref, v_ref, qg_ref,
                  out_ref, dkv_ref, dk_acc, dv_acc):
    section = pl.program_id(0)
    dk_acc[...] = jnp.zeros_like(dk_acc)
    dv_acc[...] = jnp.zeros_like(dv_acc)
    low = lax.broadcasted_iota(jnp.int32, (q_rows, LANES), 1) < HEAD_DIM

    def stack(rows):
        zero = jnp.zeros_like(rows)
        return jnp.concatenate([jnp.where(low, rows, zero), jnp.where(low, zero, rows)], axis=0)

    def merge(rows):
        return jnp.where(low, rows[:q_rows], rows[q_rows:])

    for i in range(seqs):
        at = local_ref[section * seqs + i]
        keys = k_ref[0, at]
        values = v_ref[0, at]
        q_two = stack(qg_ref[0, i, 0])
        g_two = stack(qg_ref[0, i, 1])
        scores = dot(q_two, keys, ((1,), (1,)))
        top = jnp.max(scores, axis=-1, keepdims=True)
        expo = jnp.exp(scores - top)
        weights = expo * (1.0 / jnp.sum(expo, axis=-1, keepdims=True))
        probs = weights.astype(BF)
        out_ref[0, i, 0] = merge(dot(probs, values, ((1,), (0,)))).astype(BF)
        dprobs = dot(g_two, values, ((1,), (1,)))
        delta = jnp.sum(weights * dprobs, axis=-1, keepdims=True)
        score_grads = (weights * (dprobs - delta)).astype(BF)
        out_ref[0, i, 1] = merge(dot(score_grads, keys, ((1,), (0,)))).astype(BF)
        dk_acc[at] += dot(q_two, score_grads, ((0,), (0,))).astype(BF).astype(F32)
        dv_acc[at] += dot(g_two, probs, ((0,), (0,))).astype(BF).astype(F32)

    for e in range(ex_dev):
        dkv_ref[0, :, e * seq_len:(e + 1) * seq_len] = dk_acc[e].astype(BF)
        dkv_ref[1, :, e * seq_len:(e + 1) * seq_len] = dv_acc[e].astype(BF)


def attend(local, kv, qg):
    n_section, ex_dev, seq_len, both = kv.shape
    seqs, q_rows, width = qg.shape[1], qg.shape[3], both // 2
    pairs = width // LANES
    rows = ex_dev * seq_len
    out_shape = qg.shape[:4] + (width,)
    qg_block = (1, seqs, 2, q_rows, LANES)
    kv_block = (1, ex_dev, seq_len, LANES)
    return pl.pallas_call(
        functools.partial(attend_kernel, seqs, ex_dev, seq_len, q_rows),
        grid_spec=pltpu.PrefetchScalarGridSpec(
            num_scalar_prefetch=1,
            grid=(n_section, pairs),
            in_specs=[
                pl.BlockSpec(kv_block, lambda s, p, _: (s, 0, 0, p)),
                pl.BlockSpec(kv_block, lambda s, p, _: (s, 0, 0, pairs + p)),
                pl.BlockSpec(qg_block, lambda s, p, _: (s, 0, 0, 0, p)),
            ],
            out_specs=[
                pl.BlockSpec(qg_block, lambda s, p, _: (s, 0, 0, 0, p)),
                pl.BlockSpec((2, LANES, rows), lambda s, p, _: (0, p, s)),
            ],
            scratch_shapes=[
                pltpu.VMEM((ex_dev, LANES, seq_len), F32),
                pltpu.VMEM((ex_dev, LANES, seq_len), F32),
            ],
        ),
        out_shape=[
            jax.ShapeDtypeStruct(out_shape, BF),
            jax.ShapeDtypeStruct((2, width, n_section * rows), BF),
        ],
        compiler_params=params(32),
        cost_estimate=pl.CostEstimate(
            flops=6 * 2 * n_section * seqs * pairs * 2 * q_rows * seq_len * LANES,
            bytes_accessed=2 * (2 * kv.size + 2 * qg.size),
            transcendentals=n_section * seqs * pairs * 2 * q_rows * seq_len,
        ),
    )(local, kv, kv, qg)


def finish_grads_kernel(n_section, chunks, cols, at, *refs):
    out_ref = refs[chunks * n_section]
    me = at[0]
    for c in range(chunks):
        for r in range(n_section):
            lo = pl.multiple_of(((me ^ r) * chunks + c) * cols, LANES)
            out_ref[0, :, pl.ds(lo, cols)] = refs[c * n_section + r][...].astype(F32).T


def finish_grads(me, parts, cols):
    chunks, n_section = len(parts), len(parts[0])
    rows = parts[0][0].shape[1]
    inner = n_section * chunks * cols
    return pl.pallas_call(
        functools.partial(finish_grads_kernel, n_section, chunks, cols),
        grid_spec=pltpu.PrefetchScalarGridSpec(
            num_scalar_prefetch=1,
            grid=(2,),
            in_specs=[pl.BlockSpec((cols, rows), lambda k, at: (k, 0))] * (chunks * n_section),
            out_specs=pl.BlockSpec((1, rows, inner), lambda k, at: (k, 0, 0)),
        ),
        out_shape=jax.ShapeDtypeStruct((2, rows, inner), F32),
        compiler_params=params(32),
    )(me, *[b for part in parts for b in part])


def section_swap(blocks):
    n_section = lax.axis_size("section")
    out = [blocks[0]]
    for r in range(1, n_section):
        out.append(lax.ppermute(blocks[r], "section", [(i, i ^ r) for i in range(n_section)]))
    return out


def to_owner_plane(out):
    n_dp = out.shape[1]
    dp_idx = lax.axis_index("dp")
    moved = []
    for k in range(n_dp):
        block = lax.dynamic_index_in_dim(out, (dp_idx + k) % n_dp, 1, keepdims=False)
        if k:
            block = lax.ppermute(block, "dp", [(i, (i + k) % n_dp) for i in range(n_dp)])
        moved.append(block)
    return moved


def to_owner_section(moved):
    me = lax.axis_index("section")
    return section_swap([
        jnp.stack([lax.dynamic_index_in_dim(b, me ^ r, 0, keepdims=False) for b in moved])
        for r in range(moved[0].shape[0])
    ])


def together(*values):
    return lax.optimization_barrier(values)


LAST_STEP = 3


def spread_examples(rows, first, last):
    ex_dev, seq_len, width = rows.shape
    n_section, n_mp = lax.axis_size("section"), lax.axis_size("mp")
    mp_idx, me = lax.axis_index("mp"), lax.axis_index("section")
    part = seq_len // n_mp
    mine = lax.dynamic_slice_in_dim(rows, mp_idx * part, part, axis=1)
    if n_mp != 2 or n_section != 4:
        every = lax.all_gather(mine, ("section", "mp"), axis=0)
        every = every.reshape(n_section, n_mp, ex_dev, part, width).swapaxes(1, 2)
        return every.reshape(n_section, ex_dev, seq_len, width), first, last
    core = [(i, i ^ 1) for i in range(4)]
    far = [(i, i ^ 2) for i in range(4)]
    swap = [(0, 1), (1, 0)]
    zero = jnp.int32(0)
    near, across = mp_idx * part, (1 - mp_idx) * part

    def put(whole, piece, r, example, row):
        return lax.dynamic_update_slice(whole, piece[None], (me ^ r, jnp.int32(example), row, zero))

    whole = put(jnp.zeros((n_section, ex_dev, seq_len, width), BF), rows, 0, 0, zero)
    from_far, from_side, other_far, other_side = [], [], [], []
    for step in range(ex_dev + 2):
        new = {}
        if step == 0:
            new["first"] = first
            new["peer"] = lax.ppermute(rows, "section", core)
        if step == LAST_STEP:
            new["last"] = last
        if step < ex_dev:
            new["far"] = lax.ppermute(mine[step:step + 1], "section", far)
        if 1 <= step <= ex_dev:
            e = step - 1
            new["side"] = lax.ppermute(from_far[e], "mp", swap)
            new["other_far"] = lax.ppermute(from_far[e], "section", core)
            whole = put(whole, from_far[e], 2, e, near)
        if step >= 2:
            e = step - 2
            new["other_side"] = lax.ppermute(from_side[e], "section", core)
            whole = put(whole, other_far[e], 3, e, near)
            whole = put(whole, from_side[e], 2, e, across)
        if step >= 3:
            whole = put(whole, other_side[step - 3], 3, step - 3, across)
        if step == ex_dev + 1:
            whole = put(whole, new["other_side"], 3, step - 2, across)
            break
        whole, mine, new = together(whole, mine, new)
        if step == 0:
            first = new["first"]
            whole = put(whole, new["peer"], 1, 0, zero)
        if step == LAST_STEP:
            last = new["last"]
        for name, into in (("far", from_far), ("side", from_side), ("other_far", other_far),
                           ("other_side", other_side)):
            if name in new:
                into.append(new[name])
    return whole, first, last


def per_device(encoder_rows, w_key, w_value, query, grad_context, source):
    ex_dev, seq_len, width = encoder_rows.shape
    dec_dev, q_rows, inner_dev = query.shape
    d_rows = w_key.shape[0]
    n_section, n_dp = lax.axis_size("section"), lax.axis_size("dp")
    section_idx, dp_idx = lax.axis_index("section"), lax.axis_index("dp")
    own = inner_dev // n_section
    chunks = min(CHUNKS, own // LANES)
    cols = own // chunks
    me = section_idx.reshape(1)

    plan = source.reshape(n_section, n_dp, dec_dev)
    holder = plan // ex_dev - jnp.arange(n_section, dtype=jnp.int32)[:, None, None] * n_dp
    reads_me = holder == dp_idx
    local = jnp.sum(jnp.where(reads_me, plan % ex_dev, 0), axis=-1).reshape(-1)
    my_holder = holder[section_idx, dp_idx]
    hit = my_holder[None, :] == jnp.arange(n_dp, dtype=jnp.int32)[:, None]
    slot = jnp.sum(jnp.where(hit, jnp.arange(dec_dev, dtype=jnp.int32)[None, :], 0), axis=1)
    filled = jnp.any(hit, axis=1)

    w_send = pack_weights(me, w_key, w_value, n_section, chunks, cols)
    qg_all = [
        lax.all_to_all(
            qg.reshape((n_section * n_dp,) + qg.shape[2:]),
            ("section", "dp"), split_axis=0, concat_axis=0, tiled=True,
        ).reshape(qg.shape)
        for qg in pack_queries(slot, filled, query, grad_context, n_section, n_dp, chunks)
    ]
    w_first = jnp.concatenate(section_swap([w_send[0][r] for r in range(n_section)]))
    plane, (w_first, qg_all[0]), qg_all[1:] = spread_examples(encoder_rows, (w_first, qg_all[0]), qg_all[1:])
    flat = plane.reshape(n_section * ex_dev * seq_len, width)

    outs, grads = [], []
    moved = None
    for c in range(chunks):
        w_own = w_first
        if c:
            w_mine = w_send[c]
            w_own = jnp.concatenate(section_swap([w_mine[r] for r in range(n_section)]))
        w_all = lax.all_gather(w_own, "dp", axis=0, tiled=True)
        w_all = w_all.reshape(n_dp, n_section, d_rows, 2 * cols)
        kv = project(me, flat, w_all)
        kv = kv.reshape(n_section, ex_dev, seq_len, 2 * cols)
        out, dkv = attend(local, kv, qg_all[c])
        if moved is not None:
            dkv, _ = together(dkv, moved)
        total = lax.psum_scatter(
            weight_grad(flat, dkv, n_section, n_dp), "dp", scatter_dimension=0, tiled=True
        )
        blocks = [
            lax.dynamic_slice_in_dim(total, (section_idx ^ r) * d_rows, d_rows, axis=1)
            for r in range(n_section)
        ]
        grads.append(section_swap(blocks))
        moved = to_owner_plane(out)
        outs.append(to_owner_section(moved))

    context, grad_query = unpack_outputs(me, (dp_idx - my_holder) % n_dp, outs, dec_dev)
    return context, grad_query, finish_grads(me, grads, cols)


def solution(mesh):
    return jax.shard_map(
        per_device,
        mesh=mesh,
        in_specs=(
            P(("section", "dp"), None, None),
            P(("section", "dp"), "mp"),
            P(("section", "dp"), "mp"),
            P(("section", "dp"), None, "mp"),
            P(("section", "dp"), None, "mp"),
            P(),
        ),
        out_specs=(
            P(("section", "dp"), None, "mp"),
            P(("section", "dp"), None, "mp"),
            P(None, ("section", "dp"), "mp"),
        ),
        check_vma=False,
    )
```

time: 646 us -> 553 us (0.86)
  starting transfers between devices: 118 us -> 44.3 us
  other arithmetic: 30.4 us -> 9.92 us
  Pallas kernels: 140 us -> 127 us
  between operations: 1.18 us -> 14.1 us
    ppermute x37 -> x19, waiting for transfers between devices: 233 us -> 107 us  [the longest x6 54.2 us: to_owner_plane(): lax.ppermute(block, 'dp', [(i, (i + k) % n_dp) for i in range(n_dp)])]
    ppermute x37 -> x19, starting transfers between devices: 72.6 us -> 19.2 us  [the longest x6 11.3 us: to_owner_plane(): lax.ppermute(block, 'dp', [(i, (i + k) % n_dp) for i in range(n_dp)])]
    reduce_scatter x0 -> x2, waiting for transfers between devices: none -> 52 us  [per_device(): lax.psum_scatter(weight_grad(flat, dkv, n_section, n_dp), 'dp', scatter_d...]
    all_gather x0 -> x2, waiting for transfers between devices: none -> 37.8 us  [per_device(): w_all = lax.all_gather(w_own, 'dp', axis=0, tiled=True)]
    all_to_all x4 -> x2, starting transfers between devices: 35.2 us -> 11.3 us  [per_device(): lax.all_to_all(qg.reshape((n_section * n_dp,) + qg.shape[2:]), ('section'...]
    ppermute x12 -> x18, waiting for transfers between devices: 43.2 us -> 61.3 us  [section_swap(): lax.ppermute(blocks[r], 'section', [(i, i ^ r) for i in range(n_section)])]
    add x6 -> x0, other arithmetic: 17.5 us -> none  [the longest x4 12.2 us: scatter_line(): send_up = own(k) if up is None else own(k) + up]
    all_to_all x4 -> x2, waiting for transfers between devices: 0.01 us -> 13.9 us  [per_device(): lax.all_to_all(qg.reshape((n_section * n_dp,) + qg.shape[2:]), ('section'...]
  transfers between devices with their start and end apart: 53 -> 43, of which waited for: 25 -> 16; matrix products, arithmetic and copies ran while one was open for 14% -> 14% of each run, Pallas kernels for 21% -> 22%
where the time goes in v2:
time: 553 us; the launch traced here: 550 us
  waiting for transfers between devices  272 us (49%)
  Pallas kernels  127 us (23%)
  local copies, waits for them, and re-layouts  83.2 us (15%)
  starting transfers between devices  44.3 us (8%)
  between operations  14.1 us (3%)
  other arithmetic  9.92 us (2%)
    ppermute x18, waiting for transfers between devices, section_swap(): lax.ppermute(blocks[r], 'section', [(i, i ^ r) for i in range(n_section)])  61.3 us
    ppermute x6, waiting for transfers between devices, to_owner_plane(): lax.ppermute(block, 'dp', [(i, (i + k) % n_dp) for i in range(n_dp)])  54.2 us
    reduce_scatter x2, waiting for transfers between devices, per_device(): lax.psum_scatter(weight_grad(flat, dkv, n_section, n_dp), 'dp', scatter_d...  52 us
    ppermute x3, waiting for transfers between devices, spread_examples(): new['far'] = lax.ppermute(mine[step:step + 1], 'section', far)  48.2 us
    pallas_call x2, Pallas kernels, attend(): pl.pallas_call(functools.partial(attend_kernel, seqs, ex_dev, seq_len, q_...  42.2 us
    pallas_call x2, Pallas kernels, weight_grad(): pl.pallas_call(functools.partial(weight_grad_kernel, n_section, rows), gr...  38.4 us
    pallas_call x2, Pallas kernels, project(): pl.pallas_call(functools.partial(project_kernel, n_dp, n_section), grid_s...  38.3 us
    all_gather x2, waiting for transfers between devices, per_device(): w_all = lax.all_gather(w_own, 'dp', axis=0, tiled=True)  37.8 us
  transfers between devices with their start and end apart: 43, of which 16 were waited for; matrix products, arithmetic and copies ran while one was open for 14% of the time, Pallas kernels for 22%

profile of v2, /device:TPU:11, one launch (start us, length us, event | category | flops | bytes accessed | tf_op | source)
XLA Modules:
  0.0 550.2 jit_solution(1649161698560739167)
XLA Ops:
  10.1 1.6 copy-done.2
  11.7 1.6 copy-done.3
  14.5 1.3 copy-done.7
  15.8 1.3 copy-done.10
  17.1 6.0 %all-to-all-start = ((bf16[16,2,128,256]{3,2,1,0:T(8,128)(2,1)}), bf16[16,2,128,256]{3,2,1,0:T(8,128)(2,1)S(1)}, u32[]{:S(2)}, u32[]{:S(2)}) async-start(bf16[16,2,128,256]{3,2,1,0:T(8,128)(2,1)} %bitcast.88), calls=%async_computation | async-start | bytes 4194304 | tf_op jit(solution)/shard_map/all_to_all | solution.py:399
  23.2 2.3 constant_dynamic-slice_fusion
  31.6 9.7 %broadcast_in_dim.62 = bf16[4,3,256,4096]{3,2,1,0:T(8,128)(2,1)} broadcast(bf16[]{:T(256)} %constant.355.clone.1), dimensions={} | broadcast | bytes 25165826 | tf_op jit(solution)/shard_map/broadcast_in_dim | solution.py:338
  41.4 3.2 bitcast_dynamic-update-slice_fusion.1
  44.5 1.9 constant_dynamic-slice_fusion.33
  46.4 30.2 %collective-permute-done.3 = bf16[256,512]{1,0:T(8,128)(2,1)S(1)} collective-permute-done((bf16[256,512]{1,0:T(8,128)(2,1)S(1)}, bf16[256,512]{1,0:T(8,128)(2,1)S(1)}, u32[]{:S(2)}, u32[]{:S(2)}) %collective-permute-start.3) | collective-permute-done | bytes 262176 | tf_op jit(solution)/shard_map/ppermute | solution.py:288
  76.6 5.0 collective-permute-done.2
  85.9 5.3 all-to-all-start.1
  91.3 1.3 collective-permute-done.24
  92.6 8.8 %collective-permute-done.23 = bf16[256,512]{1,0:T(8,128)(2,1)S(1)} collective-permute-done((bf16[256,512]{1,0:T(8,128)(2,1)}, bf16[256,512]{1,0:T(8,128)(2,1)S(1)}, u32[]{:S(2)}, u32[]{:S(2)}) %collective-permute-start.23) | collective-permute-done | bytes 262176 | tf_op jit(solution)/shard_map/ppermute | solution.py:288
  102.8 1.3 slice.38
  104.7 6.3 %bitcast_dynamic-update-slice_fusion = bf16[4,3,256,4096]{3,2,1,0:T(8,128)(2,1)} fusion(bf16[4,3,256,4096]{3,2,1,0:T(8,128)(2,1)} %bitcast_dynamic-update-slice_fusion.1, s32[]{:T(128)S(6)} %select_n.179, bf16[3,256,4096]{2,1,0:T(8,128)(2,1)} %collective-permute-done.4), kind=kLoop, calls=%fused_computation | loop fusion | bytes 12582916 | tf_op jit(solution)/shard_map/dynamic_update_slice | solution.py:336
  111.0 2.3 bitcast_dynamic-update-slice_fusion.13
  113.3 18.9 %collective-permute-done.5 = bf16[1,128,4096]{2,1,0:T(8,128)(2,1)S(1)} collective-permute-done((bf16[1,128,4096]{2,1,0:T(8,128)(2,1)S(1)}, bf16[1,128,4096]{2,1,0:T(8,128)(2,1)S(1)}, u32[]{:S(2)}, u32[]{:S(2)}) %collective-permute-start.5) | collective-permute-done | bytes 1048608 | tf_op jit(solution)/shard_map/ppermute | solution.py:348
  133.8 1.3 slice.39
  138.4 29.3 %collective-permute-done.8 = bf16[1,128,4096]{2,1,0:T(8,128)(2,1)} collective-permute-done((bf16[1,128,4096]{2,1,0:T(8,128)(2,1)S(1)}, bf16[1,128,4096]{2,1,0:T(8,128)(2,1)}, u32[]{:S(2)}, u32[]{:S(2)}) %collective-permute-start.8) | collective-permute-done | bytes 1048608 | tf_op jit(solution)/shard_map/ppermute | solution.py:348
  170.1 2.4 bitcast_dynamic-update-slice_fusion.9
  175.7 13.9 %all-to-all-done.1 = bf16[16,2,128,256]{3,2,1,0:T(8,128)(2,1)S(1)} async-done(((bf16[16,2,128,256]{3,2,1,0:T(8,128)(2,1)}), bf16[16,2,128,256]{3,2,1,0:T(8,128)(2,1)S(1)}, u32[]{:S(2)}, u32[]{:S(2)}) %all-to-all-start.1) | async-done | bytes 2097184 | tf_op jit(solution)/shard_map/all_to_all | solution.py:399
  189.6 4.3 collective-permute-done.14
  194.7 2.3 bitcast_dynamic-update-slice_fusion.5
  197.0 2.3 bitcast_dynamic-update-slice_fusion.4
  199.3 2.3 bitcast_dynamic-update-slice_fusion.3
  202.7 1.4 all-gather.3.cloned.1.call-done
  204.1 19.2 %shard_map.87 = bf16[3072,512]{1,0:T(8,128)(2,1)} custom-call(s32[1]{0:T(128)} %bitcast.at, bf16[3072,4096]{1,0:T(8,128)(2,1)} %bitcast.93, bf16[4,4,256,512]{3,2,1,0:T(8,128)(2,1)} %bitcast.106), custom_call_target="tpu_custom_call" | custom-call | flops 12884901888 | bytes 36700160 | tf_op jit(solution)/shard_map/pallas_call | solution.py:129
  223.3 1.9 copy-done.16
  225.2 21.1 %shard_map.88 = (bf16[4,4,2,128,256]{4,3,2,1,0:T(8,128)(2,1)S(1)}, bf16[2,256,3072]{2,1,0:T(8,128)(2,1)S(1)}) custom-call(s32[16]{0:T(128)S(1)} %reshape.62.local_ref, bf16[4,3,256,512]{3,2,1,0:T(8,128)(2,1)S(1)} %bitcast.91, bf16[4,3,256,512]{3,2,1,0:T(8,128)(2,1)S(1)} %bitcast.92, bf16[4,4,2,128,256]{4,3,2,1,0:T(8,128)(2,1)S(1)} %bitcast.86), custom_call_target="tpu_custom_call" | custom-call | flops 3221225472 | bytes 10485760 | tf_op jit(solution)/shard_map/pallas_call | solution.py:226
  246.3 1.6 copy-done.1
  248.0 1.3 copy-done.6
  249.3 19.1 %shard_map.92 = bf16[2048,1024]{1,0:T(8,128)(2,1)} custom-call(bf16[3072,4096]{1,0:T(8,128)(2,1)} %bitcast.94, bf16[3072,4096]{1,0:T(8,128)(2,1)} %bitcast.95, bf16[3072,4096]{1,0:T(8,128)(2,1)} %bitcast.96, bf16[3072,4096]{1,0:T(8,128)(2,1)} %bitcast.97, bf16[2,256,3072]{2,1,0:T(8,128)(2,1)} %copy-done.1), custom_call_target="tpu_custom_call" | custom-call | flops 12884901888 | bytes 32505856 | tf_op jit(solution)/shard_map/pallas_call | solution.py:162
  268.7 2.3 dynamic-slice_bitcast_fusion.5
  271.0 3.5 collective-permute-start.18
  274.5 2.2 collective-permute-start.16
  276.7 36.4 %all-gather.5.cloned.1.call-done = bf16[4096,512]{1,0:T(8,128)(2,1)} async-done(((bf16[1024,512]{1,0:T(8,128)(2,1)}), bf16[4096,512]{1,0:T(8,128)(2,1)}) %all-gather.5.cloned.1.call-update) | async-done | bytes 4194320 | tf_op jit(solution)/shard_map/all_gather | solution.py:416
  313.1 19.2 %shard_map.89 = bf16[3072,512]{1,0:T(8,128)(2,1)} custom-call(s32[1]{0:T(128)} %bitcast.at, bf16[3072,4096]{1,0:T(8,128)(2,1)} %bitcast.98, bf16[4,4,256,512]{3,2,1,0:T(8,128)(2,1)} %bitcast.105), custom_call_target="tpu_custom_call" | custom-call | flops 12884901888 | bytes 36700160 | tf_op jit(solution)/shard_map/pallas_call | solution.py:129
  332.2 1.9 copy-done.15
  334.1 21.1 %shard_map.90 = (bf16[4,4,2,128,256]{4,3,2,1,0:T(8,128)(2,1)S(1)}, bf16[2,256,3072]{2,1,0:T(8,128)(2,1)S(1)}) custom-call(s32[16]{0:T(128)S(1)} %reshape.62.local_ref, bf16[4,3,256,512]{3,2,1,0:T(8,128)(2,1)S(1)} %bitcast.89, bf16[4,3,256,512]{3,2,1,0:T(8,128)(2,1)S(1)} %bitcast.90, bf16[4,4,2,128,256]{4,3,2,1,0:T(8,128)(2,1)S(1)} %bitcast.85), custom_call_target="tpu_custom_call" | custom-call | flops 3221225472 | bytes 10485760 | tf_op jit(solution)/shard_map/pallas_call | solution.py:226
  355.3 1.6 copy-done
  356.9 1.3 copy-done.8
  358.2 19.3 %shard_map.93 = bf16[2048,1024]{1,0:T(8,128)(2,1)} custom-call(bf16[3072,4096]{1,0:T(8,128)(2,1)} %bitcast.99, bf16[3072,4096]{1,0:T(8,128)(2,1)} %bitcast.100, bf16[3072,4096]{1,0:T(8,128)(2,1)} %bitcast.101, bf16[3072,4096]{1,0:T(8,128)(2,1)} %bitcast.102, bf16[2,256,3072]{2,1,0:T(8,128)(2,1)} %copy-done), custom_call_target="tpu_custom_call" | custom-call | flops 12884901888 | bytes 32505856 | tf_op jit(solution)/shard_map/pallas_call | solution.py:162
  378.5 3.3 collective-permute-start.26
  381.8 2.4 collective-permute-start.25
  384.2 47.8 %collective-permute-done.27 = bf16[4,2,128,256]{3,2,1,0:T(8,128)(2,1)} collective-permute-done((bf16[4,2,128,256]{3,2,1,0:T(8,128)(2,1)}, bf16[4,2,128,256]{3,2,1,0:T(8,128)(2,1)}, u32[]{:S(2)}, u32[]{:S(2)}) %collective-permute-start.27) | collective-permute-done | bytes 524320 | tf_op jit(solution)/shard_map/ppermute | solution.py:299
  432.0 1.8 constant_dynamic-slice_fusion.9
  433.8 1.8 constant_dynamic-slice_fusion.10
  435.6 6.4 %collective-permute-done.25 = bf16[4,2,128,256]{3,2,1,0:T(8,128)(2,1)} collective-permute-done((bf16[4,2,128,256]{3,2,1,0:T(8,128)(2,1)S(1)}, bf16[4,2,128,256]{3,2,1,0:T(8,128)(2,1)}, u32[]{:S(2)}, u32[]{:S(2)}) %collective-permute-start.25) | collective-permute-done | bytes 524320 | tf_op jit(solution)/shard_map/ppermute | solution.py:299
  442.0 1.8 constant_dynamic-slice_fusion.11
  448.0 1.8 dynamic-slice_bitcast_fusion.10
  449.8 1.8 constant_dynamic-slice_fusion.21
  451.5 1.8 constant_dynamic-slice_fusion.22
  453.3 1.8 constant_dynamic-slice_fusion.23
  459.9 2.1 constant_dynamic-slice_fusion.5
  462.0 52.0 %reduce-scatter.5.cloned.1.call-done = bf16[512,1024]{1,0:T(8,128)(2,1)} async-done(((bf16[2048,1024]{1,0:T(8,128)(2,1)}), bf16[512,1024]{1,0:T(8,128)(2,1)}) %reduce-scatter.5.cloned.1.call-update) | async-done | bytes 1048592 | tf_op jit(solution)/shard_map/reduce_scatter | solution.py:423
  514.0 1.3 constant_dynamic-slice_fusion.1
  517.6 1.3 collective-permute-start.35
  519.8 1.4 pad_maximum_fusion.2
  521.2 3.1 shard_map.91
  524.3 6.0 %collective-permute-done.33.refs_3_ = bf16[512,256]{1,0:T(8,128)(2,1)S(1)} collective-permute-done((bf16[512,256]{1,0:T(8,128)(2,1)}, bf16[512,256]{1,0:T(8,128)(2,1)S(1)}, u32[]{:S(2)}, u32[]{:S(2)}) %collective-permute-start.33) | collective-permute-done | bytes 262176 | tf_op jit(solution)/shard_map/ppermute | solution.py:288
  530.3 3.7 collective-permute-done.35.refs_6_
  534.0 6.4 %collective-permute-done.36.refs_7_ = bf16[512,256]{1,0:T(8,128)(2,1)S(1)} collective-permute-done((bf16[512,256]{1,0:T(8,128)(2,1)S(1)}, bf16[512,256]{1,0:T(8,128)(2,1)S(1)}, u32[]{:S(2)}, u32[]{:S(2)}) %collective-permute-start.36) | collective-permute-done | bytes 262176 | tf_op jit(solution)/shard_map/ppermute | solution.py:288
  540.4 3.3 shard_map.94
  (131 shorter events, 42.8 us)
Async XLA Ops:
  7.2 75.5 %collective-permute-start.4 = (bf16[3,256,4096]{2,1,0:T(8,128)(2,1)}, bf16[3,256,4096]{2,1,0:T(8,128)(2,1)}, u32[]{:S(2)}, u32[]{:S(2)}) collective-permute-start(bf16[3,256,4096]{2,1,0:T(8,128)(2,1)} %param.6), channel_id=1, source_target_pairs={{0,8},{8,0},{16,24},{24,16},{1,9},{9,1},{17,25},{25,17},{2,10},{10... | collective-permute-start | bytes 18874376 | tf_op jit(solution)/shard_map/ppermute | solution.py:344
  10.1 1.6 copy-start.2
  11.7 1.6 copy-start.3
  13.3 13.4 %copy-start.11 = (bf16[256,2048]{1,0:T(8,128)(2,1)S(1)}, bf16[256,2048]{1,0:T(8,128)(2,1)}, u32[]{:S(2)}) copy-start(bf16[256,2048]{1,0:T(8,128)(2,1)} %refs_0_.1) | copy-start | bytes 3145732
  14.5 1.3 copy-start.7
  15.8 1.3 copy-start.10
  17.1 65.5 %all-to-all-start = ((bf16[16,2,128,256]{3,2,1,0:T(8,128)(2,1)}), bf16[16,2,128,256]{3,2,1,0:T(8,128)(2,1)S(1)}, u32[]{:S(2)}, u32[]{:S(2)}) async-start(bf16[16,2,128,256]{3,2,1,0:T(8,128)(2,1)} %bitcast.88), calls=%async_computation | async-start | bytes 4194304 | tf_op jit(solution)/shard_map/all_to_all | solution.py:399
  23.2 180.9 %all-gather.3.cloned.1.call-start = ((), (), s32[]{:S(2)}) async-start(), calls=%async_computation.4 | async-start | bytes 5242880 | tf_op jit(solution)/shard_map/all_gather | solution.py:416
  25.5 57.1 %collective-permute-start = (bf16[1,128,4096]{2,1,0:T(8,128)(2,1)}, bf16[1,128,4096]{2,1,0:T(8,128)(2,1)}, u32[]{:S(2)}, u32[]{:S(2)}) collective-permute-start(bf16[1,128,4096]{2,1,0:T(8,128)(2,1)} %constant_dynamic-slice_fusion), channel_id=1, source_target_pairs={{0,16},{8,24},{16,0},{24,8},{1,17},{9,25},{17,1},{25,9},{2,18},{10... | collective-permute-start | bytes 3145736 | tf_op jit(solution)/shard_map/ppermute | solution.py:348
  26.7 1.2 copy-start.12
  28.4 1.0 copy-start.13
  29.4 47.1 %collective-permute-start.3 = (bf16[256,512]{1,0:T(8,128)(2,1)S(1)}, bf16[256,512]{1,0:T(8,128)(2,1)S(1)}, u32[]{:S(2)}, u32[]{:S(2)}) collective-permute-start(bf16[256,512]{1,0:T(8,128)(2,1)S(1)} %get-tuple-element.98), channel_id=1, source_target_pairs={{0,24},{8,16},{16,8},{24,0},{1,25},{9,17},{17,9},{25,1},{2,26},{10... | collective-permute-start | bytes 786440 | tf_op jit(solution)/shard_map/ppermute | solution.py:288
  30.3 51.2 %collective-permute-start.2 = (bf16[256,512]{1,0:T(8,128)(2,1)S(1)}, bf16[256,512]{1,0:T(8,128)(2,1)S(1)}, u32[]{:S(2)}, u32[]{:S(2)}) collective-permute-start(bf16[256,512]{1,0:T(8,128)(2,1)S(1)} %get-tuple-element.99), channel_id=1, source_target_pairs={{0,16},{8,24},{16,0},{24,8},{1,17},{9,25},{17,1},{25,9},{2,18},{10... | collective-permute-start | bytes 786440 | tf_op jit(solution)/shard_map/ppermute | solution.py:288
  31.5 9.9 %slice-start = ((s8[6291456]{0:T(1024)(128)(4,1)}), s8[4194304]{0:T(1024)(128)(4,1)S(1)}, s32[]{:S(2)}) async-start(s8[6291456]{0:T(1024)(128)(4,1)} %bitcast.103), calls=%async_computation.8 | async-start | bytes 8388608
  31.5 9.9 %slice-start.1 = ((s8[6291456]{0:T(1024)(128)(4,1)}), s8[2097152]{0:T(1024)(128)(4,1)S(1)}, s32[]{:S(2)}) async-start(s8[6291456]{0:T(1024)(128)(4,1)} %bitcast.103), calls=%async_computation.9 | async-start | bytes 4194304
  31.5 50.0 %collective-permute-start.1 = (bf16[256,512]{1,0:T(8,128)(2,1)S(1)}, bf16[256,512]{1,0:T(8,128)(2,1)S(1)}, u32[]{:S(2)}, u32[]{:S(2)}) collective-permute-start(bf16[256,512]{1,0:T(8,128)(2,1)S(1)} %get-tuple-element.100), channel_id=1, source_target_pairs={{0,8},{8,0},{16,24},{24,16},{1,9},{9,1},{17,25},{25,17},{2,10},{10... | collective-permute-start | bytes 786440 | tf_op jit(solution)/shard_map/ppermute | solution.py:288
  44.5 38.1 %copy-start.14 = (bf16[4,256,512]{2,1,0:T(8,128)(2,1)S(1)}, bf16[4,256,512]{2,1,0:T(8,128)(2,1)}, u32[]{:S(2)}) copy-start(bf16[4,256,512]{2,1,0:T(8,128)(2,1)} %copy-done.13) | copy-start | bytes 3145732
  82.6 3.2 copy-start.4
  83.6 8.9 %collective-permute-start.24 = (bf16[256,512]{1,0:T(8,128)(2,1)}, bf16[256,512]{1,0:T(8,128)(2,1)S(1)}, u32[]{:S(2)}, u32[]{:S(2)}) collective-permute-start(bf16[256,512]{1,0:T(8,128)(2,1)} %get-tuple-element.94), channel_id=1, source_target_pairs={{0,24},{8,16},{16,8},{24,0},{1,25},{9,17},{17,9},{25,1},{2,26},{10... | collective-permute-start | bytes 786440 | tf_op jit(solution)/shard_map/ppermute | solution.py:288
  84.7 16.7 %collective-permute-start.23 = (bf16[256,512]{1,0:T(8,128)(2,1)}, bf16[256,512]{1,0:T(8,128)(2,1)S(1)}, u32[]{:S(2)}, u32[]{:S(2)}) collective-permute-start(bf16[256,512]{1,0:T(8,128)(2,1)} %get-tuple-element.95), channel_id=1, source_target_pairs={{0,16},{8,24},{16,0},{24,8},{1,17},{9,25},{17,1},{25,9},{2,18},{10... | collective-permute-start | bytes 786440 | tf_op jit(solution)/shard_map/ppermute | solution.py:288
  85.9 15.5 %collective-permute-start.22 = (bf16[256,512]{1,0:T(8,128)(2,1)}, bf16[256,512]{1,0:T(8,128)(2,1)S(1)}, u32[]{:S(2)}, u32[]{:S(2)}) collective-permute-start(bf16[256,512]{1,0:T(8,128)(2,1)} %get-tuple-element.96), channel_id=1, source_target_pairs={{0,8},{8,0},{16,24},{24,16},{1,9},{9,1},{17,25},{25,17},{2,10},{10... | collective-permute-start | bytes 786440 | tf_op jit(solution)/shard_map/ppermute | solution.py:288
  85.9 103.7 %all-to-all-start.1 = ((bf16[16,2,128,256]{3,2,1,0:T(8,128)(2,1)}), bf16[16,2,128,256]{3,2,1,0:T(8,128)(2,1)S(1)}, u32[]{:S(2)}, u32[]{:S(2)}) async-start(bf16[16,2,128,256]{3,2,1,0:T(8,128)(2,1)} %bitcast.87), calls=%async_computation.1 | async-start | bytes 4194304 | tf_op jit(solution)/shard_map/all_to_all | solution.py:399
  91.1 221.9 %all-gather.5.cloned.1.call-start = ((), (), s32[]{:S(2)}) async-start(), calls=%async_computation.5 | async-start | bytes 5242880 | tf_op jit(solution)/shard_map/all_gather | solution.py:416
  102.4 357.5 %reduce-scatter.3.cloned.1.call-start = ((), (), s32[]{:S(2)}) async-start(), calls=%async_computation.6 | async-start | bytes 5242880 | tf_op jit(solution)/shard_map/reduce_scatter | solution.py:423
  102.5 29.7 %collective-permute-start.6 = (bf16[1,128,4096]{2,1,0:T(8,128)(2,1)}, bf16[1,128,4096]{2,1,0:T(8,128)(2,1)S(1)}, u32[]{:S(2)}, u32[]{:S(2)}) collective-permute-start(bf16[1,128,4096]{2,1,0:T(8,128)(2,1)} %collective-permute-done), channel_id=1, source_target_pairs={{0,8},{8,0},{16,24},{24,16},{1,9},{9,1},{17,25},{25,17},{2,10},{10... | collective-permute-start | bytes 3145736 | tf_op jit(solution)/shard_map/ppermute | solution.py:352
  102.5 29.7 %collective-permute-start.7 = (bf16[1,128,4096]{2,1,0:T(8,128)(2,1)}, bf16[1,128,4096]{2,1,0:T(8,128)(2,1)S(1)}, u32[]{:S(2)}, u32[]{:S(2)}) collective-permute-start(bf16[1,128,4096]{2,1,0:T(8,128)(2,1)} %collective-permute-done), channel_id=1, source_target_pairs={{0,1},{1,0},{2,3},{3,2},{4,5},{5,4},{6,7},{7,6},{8,9},{9,8},{10,11... | collective-permute-start | bytes 3145736 | tf_op jit(solution)/shard_map/ppermute | solution.py:351
  104.1 28.0 %collective-permute-start.5 = (bf16[1,128,4096]{2,1,0:T(8,128)(2,1)S(1)}, bf16[1,128,4096]{2,1,0:T(8,128)(2,1)S(1)}, u32[]{:S(2)}, u32[]{:S(2)}) collective-permute-start(bf16[1,128,4096]{2,1,0:T(8,128)(2,1)S(1)} %slice.38), channel_id=1, source_target_pairs={{0,16},{8,24},{16,0},{24,8},{1,17},{9,25},{17,1},{25,9},{2,18},{10... | collective-permute-start | bytes 3145736 | tf_op jit(solution)/shard_map/ppermute | solution.py:348
  132.2 35.5 %collective-permute-start.9 = (bf16[1,128,4096]{2,1,0:T(8,128)(2,1)S(1)}, bf16[1,128,4096]{2,1,0:T(8,128)(2,1)S(1)}, u32[]{:S(2)}, u32[]{:S(2)}) collective-permute-start(bf16[1,128,4096]{2,1,0:T(8,128)(2,1)S(1)} %collective-permute-done.5), channel_id=1, source_target_pairs={{0,8},{8,0},{16,24},{24,16},{1,9},{9,1},{17,25},{25,17},{2,10},{10... | collective-permute-start | bytes 3145736 | tf_op jit(solution)/shard_map/ppermute | solution.py:352
  132.4 35.2 %collective-permute-start.11 = (bf16[1,128,4096]{2,1,0:T(8,128)(2,1)S(1)}, bf16[1,128,4096]{2,1,0:T(8,128)(2,1)S(1)}, u32[]{:S(2)}, u32[]{:S(2)}) collective-permute-start(bf16[1,128,4096]{2,1,0:T(8,128)(2,1)S(1)} %collective-permute-done.5), channel_id=1, source_target_pairs={{0,1},{1,0},{2,3},{3,2},{4,5},{5,4},{6,7},{7,6},{8,9},{9,8},{10,11... | collective-permute-start | bytes 3145736 | tf_op jit(solution)/shard_map/ppermute | solution.py:351
  135.1 32.6 %collective-permute-start.8 = (bf16[1,128,4096]{2,1,0:T(8,128)(2,1)S(1)}, bf16[1,128,4096]{2,1,0:T(8,128)(2,1)}, u32[]{:S(2)}, u32[]{:S(2)}) collective-permute-start(bf16[1,128,4096]{2,1,0:T(8,128)(2,1)S(1)} %slice.39), channel_id=1, source_target_pairs={{0,16},{8,24},{16,0},{24,8},{1,17},{9,25},{17,1},{25,9},{2,18},{10... | collective-permute-start | bytes 3145736 | tf_op jit(solution)/shard_map/ppermute | solution.py:348
  135.6 32.0 %collective-permute-start.10 = (bf16[1,128,4096]{2,1,0:T(8,128)(2,1)S(1)}, bf16[1,128,4096]{2,1,0:T(8,128)(2,1)S(1)}, u32[]{:S(2)}, u32[]{:S(2)}) collective-permute-start(bf16[1,128,4096]{2,1,0:T(8,128)(2,1)S(1)} %collective-permute-done.7), channel_id=1, source_target_pairs={{0,8},{8,0},{16,24},{24,16},{1,9},{9,1},{17,25},{25,17},{2,10},{10... | collective-permute-start | bytes 3145736 | tf_op jit(solution)/shard_map/ppermute | solution.py:356
  167.7 21.9 %collective-permute-start.12 = (bf16[1,128,4096]{2,1,0:T(8,128)(2,1)}, bf16[1,128,4096]{2,1,0:T(8,128)(2,1)}, u32[]{:S(2)}, u32[]{:S(2)}) collective-permute-start(bf16[1,128,4096]{2,1,0:T(8,128)(2,1)} %collective-permute-done.8), channel_id=1, source_target_pairs={{0,8},{8,0},{16,24},{24,16},{1,9},{9,1},{17,25},{25,17},{2,10},{10... | collective-permute-start | bytes 3145736 | tf_op jit(solution)/shard_map/ppermute | solution.py:352
  168.8 25.1 %collective-permute-start.14 = (bf16[1,128,4096]{2,1,0:T(8,128)(2,1)}, bf16[1,128,4096]{2,1,0:T(8,128)(2,1)}, u32[]{:S(2)}, u32[]{:S(2)}) collective-permute-start(bf16[1,128,4096]{2,1,0:T(8,128)(2,1)} %collective-permute-done.8), channel_id=1, source_target_pairs={{0,1},{1,0},{2,3},{3,2},{4,5},{5,4},{6,7},{7,6},{8,9},{9,8},{10,11... | collective-permute-start | bytes 3145736 | tf_op jit(solution)/shard_map/ppermute | solution.py:351
  169.8 19.8 %collective-permute-start.13 = (bf16[1,128,4096]{2,1,0:T(8,128)(2,1)S(1)}, bf16[1,128,4096]{2,1,0:T(8,128)(2,1)}, u32[]{:S(2)}, u32[]{:S(2)}) collective-permute-start(bf16[1,128,4096]{2,1,0:T(8,128)(2,1)S(1)} %collective-permute-done.11), channel_id=1, source_target_pairs={{0,8},{8,0},{16,24},{24,16},{1,9},{9,1},{17,25},{25,17},{2,10},{10... | collective-permute-start | bytes 3145736 | tf_op jit(solution)/shard_map/ppermute | solution.py:356
  193.8 7.8 %collective-permute-start.15 = (bf16[1,128,4096]{2,1,0:T(8,128)(2,1)}, bf16[1,128,4096]{2,1,0:T(8,128)(2,1)S(1)}, u32[]{:S(2)}, u32[]{:S(2)}) collective-permute-start(bf16[1,128,4096]{2,1,0:T(8,128)(2,1)} %collective-permute-done.14), channel_id=1, source_target_pairs={{0,8},{8,0},{16,24},{24,16},{1,9},{9,1},{17,25},{25,17},{2,10},{10... | collective-permute-start | bytes 3145736 | tf_op jit(solution)/shard_map/ppermute | solution.py:356
  204.1 19.2 %copy-start.5 = (bf16[16,2,128,256]{3,2,1,0:T(8,128)(2,1)S(1)}, bf16[16,2,128,256]{3,2,1,0:T(8,128)(2,1)}, u32[]{:S(2)}) copy-start(bf16[16,2,128,256]{3,2,1,0:T(8,128)(2,1)} %copy-done.4) | copy-start | bytes 6291460
  223.3 1.9 copy-start.16
  246.3 1.7 copy-start.1
  248.0 1.3 copy-start.6
  268.4 245.6 %reduce-scatter.5.cloned.1.call-start = ((), (), s32[]{:S(2)}) async-start(), calls=%async_computation.7 | async-start | bytes 5242880 | tf_op jit(solution)/shard_map/reduce_scatter | solution.py:423
  271.0 87.2 %collective-permute-start.18 = (bf16[4,2,128,256]{3,2,1,0:T(8,128)(2,1)}, bf16[4,2,128,256]{3,2,1,0:T(8,128)(2,1)}, u32[]{:S(2)}, u32[]{:S(2)}) collective-permute-start(bf16[4,2,128,256]{3,2,1,0:T(8,128)(2,1)} %get-tuple-element.83), channel_id=1, source_target_pairs={{0,6},{2,0},{4,2},{6,4},{1,7},{3,1},{5,3},{7,5},{8,14},{10,8},{12,... | collective-permute-start | bytes 1572872 | tf_op jit(solution)/shard_map/ppermute | solution.py:299
  274.5 83.7 %collective-permute-start.17 = (bf16[4,2,128,256]{3,2,1,0:T(8,128)(2,1)S(1)}, bf16[4,2,128,256]{3,2,1,0:T(8,128)(2,1)}, u32[]{:S(2)}, u32[]{:S(2)}) collective-permute-start(bf16[4,2,128,256]{3,2,1,0:T(8,128)(2,1)S(1)} %get-tuple-element.84), channel_id=1, source_target_pairs={{0,4},{2,6},{4,0},{6,2},{1,5},{3,7},{5,1},{7,3},{8,12},{10,14},{12... | collective-permute-start | bytes 1572872 | tf_op jit(solution)/shard_map/ppermute | solution.py:299
  274.5 83.7 %collective-permute-start.16 = (bf16[4,2,128,256]{3,2,1,0:T(8,128)(2,1)S(1)}, bf16[4,2,128,256]{3,2,1,0:T(8,128)(2,1)}, u32[]{:S(2)}, u32[]{:S(2)}) collective-permute-start(bf16[4,2,128,256]{3,2,1,0:T(8,128)(2,1)S(1)} %get-tuple-element.82), channel_id=1, source_target_pairs={{0,2},{2,4},{4,6},{6,0},{1,3},{3,5},{5,7},{7,1},{8,10},{10,12},{12... | collective-permute-start | bytes 1572872 | tf_op jit(solution)/shard_map/ppermute | solution.py:299
  332.2 1.9 copy-start.15
  355.3 1.6 copy-start
  356.9 1.3 copy-start.8
  358.2 19.3 %copy-start.9 = (bf16[4,4,2,128,256]{4,3,2,1,0:T(8,128)(2,1)S(1)}, bf16[4,4,2,128,256]{4,3,2,1,0:T(8,128)(2,1)}, u32[]{:S(2)}) copy-start(bf16[4,4,2,128,256]{4,3,2,1,0:T(8,128)(2,1)} %copy-done.8) | copy-start | bytes 6291460
  378.5 53.5 %collective-permute-start.27 = (bf16[4,2,128,256]{3,2,1,0:T(8,128)(2,1)}, bf16[4,2,128,256]{3,2,1,0:T(8,128)(2,1)}, u32[]{:S(2)}, u32[]{:S(2)}) collective-permute-start(bf16[4,2,128,256]{3,2,1,0:T(8,128)(2,1)} %get-tuple-element.76), channel_id=1, source_target_pairs={{0,6},{2,0},{4,2},{6,4},{1,7},{3,1},{5,3},{7,5},{8,14},{10,8},{12,... | collective-permute-start | bytes 1572872 | tf_op jit(solution)/shard_map/ppermute | solution.py:299
  378.5 55.3 %collective-permute-start.26 = (bf16[4,2,128,256]{3,2,1,0:T(8,128)(2,1)S(1)}, bf16[4,2,128,256]{3,2,1,0:T(8,128)(2,1)}, u32[]{:S(2)}, u32[]{:S(2)}) collective-permute-start(bf16[4,2,128,256]{3,2,1,0:T(8,128)(2,1)S(1)} %get-tuple-element.77), channel_id=1, source_target_pairs={{0,4},{2,6},{4,0},{6,2},{1,5},{3,7},{5,1},{7,3},{8,12},{10,14},{12... | collective-permute-start | bytes 1572872 | tf_op jit(solution)/shard_map/ppermute | solution.py:299
  381.8 60.2 %collective-permute-start.25 = (bf16[4,2,128,256]{3,2,1,0:T(8,128)(2,1)S(1)}, bf16[4,2,128,256]{3,2,1,0:T(8,128)(2,1)}, u32[]{:S(2)}, u32[]{:S(2)}) collective-permute-start(bf16[4,2,128,256]{3,2,1,0:T(8,128)(2,1)S(1)} %get-tuple-element.75), channel_id=1, source_target_pairs={{0,2},{2,4},{4,6},{6,0},{1,3},{3,5},{5,7},{7,1},{8,10},{10,12},{12... | collective-permute-start | bytes 1572872 | tf_op jit(solution)/shard_map/ppermute | solution.py:299
  443.8 15.3 %collective-permute-start.28 = (bf16[4,2,128,256]{3,2,1,0:T(8,128)(2,1)S(1)}, bf16[4,2,128,256]{3,2,1,0:T(8,128)(2,1)S(1)}, u32[]{:S(2)}, u32[]{:S(2)}) collective-permute-start(bf16[4,2,128,256]{3,2,1,0:T(8,128)(2,1)S(1)} %pad_maximum_fusion.7), channel_id=1, source_target_pairs={{0,8},{8,0},{16,24},{24,16},{1,9},{9,1},{17,25},{25,17},{2,10},{10... | collective-permute-start | bytes 1572872 | tf_op jit(solution)/shard_map/ppermute | solution.py:288
  445.5 16.5 %collective-permute-start.29 = (bf16[4,2,128,256]{3,2,1,0:T(8,128)(2,1)}, bf16[4,2,128,256]{3,2,1,0:T(8,128)(2,1)S(1)}, u32[]{:S(2)}, u32[]{:S(2)}) collective-permute-start(bf16[4,2,128,256]{3,2,1,0:T(8,128)(2,1)} %pad_maximum_fusion.8), channel_id=1, source_target_pairs={{0,16},{8,24},{16,0},{24,8},{1,17},{9,25},{17,1},{25,9},{2,18},{10... | collective-permute-start | bytes 1572872 | tf_op jit(solution)/shard_map/ppermute | solution.py:288
  447.5 67.7 %collective-permute-start.30 = (bf16[4,2,128,256]{3,2,1,0:T(8,128)(2,1)}, bf16[4,2,128,256]{3,2,1,0:T(8,128)(2,1)S(1)}, u32[]{:S(2)}, u32[]{:S(2)}) collective-permute-start(bf16[4,2,128,256]{3,2,1,0:T(8,128)(2,1)} %pad_maximum_fusion.9), channel_id=1, source_target_pairs={{0,24},{8,16},{16,8},{24,0},{1,25},{9,17},{17,9},{25,1},{2,26},{10... | collective-permute-start | bytes 1572872 | tf_op jit(solution)/shard_map/ppermute | solution.py:288
  456.0 60.6 %collective-permute-start.19 = (bf16[4,2,128,256]{3,2,1,0:T(8,128)(2,1)}, bf16[4,2,128,256]{3,2,1,0:T(8,128)(2,1)S(1)}, u32[]{:S(2)}, u32[]{:S(2)}) collective-permute-start(bf16[4,2,128,256]{3,2,1,0:T(8,128)(2,1)} %pad_maximum_fusion.3), channel_id=1, source_target_pairs={{0,8},{8,0},{16,24},{24,16},{1,9},{9,1},{17,25},{25,17},{2,10},{10... | collective-permute-start | bytes 1572872 | tf_op jit(solution)/shard_map/ppermute | solution.py:288
  457.0 60.6 %collective-permute-start.20 = (bf16[4,2,128,256]{3,2,1,0:T(8,128)(2,1)}, bf16[4,2,128,256]{3,2,1,0:T(8,128)(2,1)S(1)}, u32[]{:S(2)}, u32[]{:S(2)}) collective-permute-start(bf16[4,2,128,256]{3,2,1,0:T(8,128)(2,1)} %pad_maximum_fusion.4), channel_id=1, source_target_pairs={{0,16},{8,24},{16,0},{24,8},{1,17},{9,25},{17,1},{25,9},{2,18},{10... | collective-permute-start | bytes 1572872 | tf_op jit(solution)/shard_map/ppermute | solution.py:288
  459.1 58.5 %collective-permute-start.21 = (bf16[4,2,128,256]{3,2,1,0:T(8,128)(2,1)}, bf16[4,2,128,256]{3,2,1,0:T(8,128)(2,1)S(1)}, u32[]{:S(2)}, u32[]{:S(2)}) collective-permute-start(bf16[4,2,128,256]{3,2,1,0:T(8,128)(2,1)} %pad_maximum_fusion.5), channel_id=1, source_target_pairs={{0,24},{8,16},{16,8},{24,0},{1,25},{9,17},{17,9},{25,1},{2,26},{10... | collective-permute-start | bytes 1572872 | tf_op jit(solution)/shard_map/ppermute | solution.py:288
  462.0 56.9 %collective-permute-start.31 = (bf16[512,256]{1,0:T(8,128)(2,1)}, bf16[512,256]{1,0:T(8,128)(2,1)}, u32[]{:S(2)}, u32[]{:S(2)}) collective-permute-start(bf16[512,256]{1,0:T(8,128)(2,1)} %get-tuple-element.91), channel_id=1, source_target_pairs={{0,8},{8,0},{16,24},{24,16},{1,9},{9,1},{17,25},{25,17},{2,10},{10... | collective-permute-start | bytes 786440 | tf_op jit(solution)/shard_map/ppermute | solution.py:288
  515.3 9.0 %collective-permute-start.32 = (bf16[512,256]{1,0:T(8,128)(2,1)}, bf16[512,256]{1,0:T(8,128)(2,1)S(1)}, u32[]{:S(2)}, u32[]{:S(2)}) collective-permute-start(bf16[512,256]{1,0:T(8,128)(2,1)} %get-tuple-element.90), channel_id=1, source_target_pairs={{0,16},{8,24},{16,0},{24,8},{1,17},{9,25},{17,1},{25,9},{2,18},{10... | collective-permute-start | bytes 786440 | tf_op jit(solution)/shard_map/ppermute | solution.py:288
  516.5 13.8 %collective-permute-start.33 = (bf16[512,256]{1,0:T(8,128)(2,1)}, bf16[512,256]{1,0:T(8,128)(2,1)S(1)}, u32[]{:S(2)}, u32[]{:S(2)}) collective-permute-start(bf16[512,256]{1,0:T(8,128)(2,1)} %get-tuple-element.89), channel_id=1, source_target_pairs={{0,24},{8,16},{16,8},{24,0},{1,25},{9,17},{17,9},{25,1},{2,26},{10... | collective-permute-start | bytes 786440 | tf_op jit(solution)/shard_map/ppermute | solution.py:288
  517.6 12.7 %collective-permute-start.34 = (bf16[512,256]{1,0:T(8,128)(2,1)S(1)}, bf16[512,256]{1,0:T(8,128)(2,1)S(1)}, u32[]{:S(2)}, u32[]{:S(2)}) collective-permute-start(bf16[512,256]{1,0:T(8,128)(2,1)S(1)} %get-tuple-element.87), channel_id=1, source_target_pairs={{0,8},{8,0},{16,24},{24,16},{1,9},{9,1},{17,25},{25,17},{2,10},{10... | collective-permute-start | bytes 786440 | tf_op jit(solution)/shard_map/ppermute | solution.py:288
  517.6 16.4 %collective-permute-start.35 = (bf16[512,256]{1,0:T(8,128)(2,1)S(1)}, bf16[512,256]{1,0:T(8,128)(2,1)S(1)}, u32[]{:S(2)}, u32[]{:S(2)}) collective-permute-start(bf16[512,256]{1,0:T(8,128)(2,1)S(1)} %get-tuple-element.86), channel_id=1, source_target_pairs={{0,16},{8,24},{16,0},{24,8},{1,17},{9,25},{17,1},{25,9},{2,18},{10... | collective-permute-start | bytes 786440 | tf_op jit(solution)/shard_map/ppermute | solution.py:288
  518.9 21.5 %collective-permute-start.36 = (bf16[512,256]{1,0:T(8,128)(2,1)S(1)}, bf16[512,256]{1,0:T(8,128)(2,1)S(1)}, u32[]{:S(2)}, u32[]{:S(2)}) collective-permute-start(bf16[512,256]{1,0:T(8,128)(2,1)S(1)} %get-tuple-element.85), channel_id=1, source_target_pairs={{0,24},{8,16},{16,8},{24,0},{1,25},{9,17},{17,9},{25,1},{2,26},{10... | collective-permute-start | bytes 786440 | tf_op jit(solution)/shard_map/ppermute | solution.py:288
Sparse Core Ops, SparseCore 0:
  82.8 121.2 all-gather.2
  205.6 107.3 all-gather.4
  315.9 120.1 reduce-scatter.2
  438.4 75.5 reduce-scatter.4

commit v3 on v2

--- a/solution.py
+++ b/solution.py
@@ -148,33 +148,36 @@
     )(me, flat, w_all)
 
 
-def weight_grad_kernel(n_section, rows, *refs):
+def weight_grad_kernel(n_section, at, *refs):
     g_ref, out_ref = refs[n_section:]
-    g = g_ref[...].reshape(out_ref.shape[0], g_ref.shape[2])
-    for s in range(n_section):
-        out_ref[:, s * rows:(s + 1) * rows] = dot(g, refs[s][...], ((1,), (0,))).astype(BF)
-
-
-def weight_grad(flat, dkv, n_section, n_dp):
+    g = g_ref[...].reshape(out_ref.shape[1], g_ref.shape[2])
+    for r in range(n_section):
+        out_ref[r] = dot(g, refs[r][...], ((1,), (0,))).astype(BF)
+
+
+def weight_grad(me, flat, dkv, n_section, n_dp):
     total, width = flat.shape
     both = 2 * dkv.shape[1]
     rows = width // (n_section * n_dp)
     return pl.pallas_call(
-        functools.partial(weight_grad_kernel, n_section, rows),
-        grid=(n_dp,),
-        in_specs=[
-            pl.BlockSpec((total, rows), functools.partial(lambda s, d: (0, s * n_dp + d), s))
-            for s in range(n_section)
-        ] + [pl.BlockSpec((2, dkv.shape[1], total), lambda d: (0, 0, 0))],
-        out_specs=pl.BlockSpec((both, n_section * rows), lambda d: (d, 0)),
-        out_shape=jax.ShapeDtypeStruct((n_dp * both, n_section * rows), BF),
+        functools.partial(weight_grad_kernel, n_section),
+        grid_spec=pltpu.PrefetchScalarGridSpec(
+            num_scalar_prefetch=1,
+            grid=(n_dp,),
+            in_specs=[
+                pl.BlockSpec((total, rows), functools.partial(lambda r, d, at: (0, (at[0] ^ r) * n_dp + d), r))
+                for r in range(n_section)
+            ] + [pl.BlockSpec((2, dkv.shape[1], total), lambda d, at: (0, 0, 0))],
+            out_specs=pl.BlockSpec((n_section, both, rows), lambda d, at: (d, 0, 0)),
+        ),
+        out_shape=jax.ShapeDtypeStruct((n_dp * n_section, both, rows), BF),
         compiler_params=params(56),
         cost_estimate=pl.CostEstimate(
             flops=2 * total * width * both,
             bytes_accessed=2 * (total * width + width * both + total * both),
             transcendentals=0,
         ),
-    )(*([flat] * n_section), dkv)
+    )(me, *([flat] * n_section), dkv)
 
 
 def attend_kernel(seqs, ex_dev, seq_len, q_rows, local_ref, k_ref, v_ref, qg_ref,
@@ -264,9 +267,8 @@
             out_ref[0, :, pl.ds(lo, cols)] = refs[c * n_section + r][...].astype(F32).T
 
 
-def finish_grads(me, parts, cols):
+def finish_grads(me, parts, cols, rows):
     chunks, n_section = len(parts), len(parts[0])
-    rows = parts[0][0].shape[1]
     inner = n_section * chunks * cols
     return pl.pallas_call(
         functools.partial(finish_grads_kernel, n_section, chunks, cols),
@@ -313,19 +315,20 @@
     return lax.optimization_barrier(values)
 
 
-LAST_STEP = 3
-
-
-def spread_examples(rows, first, last):
+def my_share(rows):
+    part = rows.shape[1] // lax.axis_size("mp")
+    return lax.dynamic_slice_in_dim(rows, lax.axis_index("mp") * part, part, axis=1)
+
+
+def spread_examples(rows, mine, due):
     ex_dev, seq_len, width = rows.shape
     n_section, n_mp = lax.axis_size("section"), lax.axis_size("mp")
     mp_idx, me = lax.axis_index("mp"), lax.axis_index("section")
     part = seq_len // n_mp
-    mine = lax.dynamic_slice_in_dim(rows, mp_idx * part, part, axis=1)
     if n_mp != 2 or n_section != 4:
         every = lax.all_gather(mine, ("section", "mp"), axis=0)
         every = every.reshape(n_section, n_mp, ex_dev, part, width).swapaxes(1, 2)
-        return every.reshape(n_section, ex_dev, seq_len, width), first, last
+        return every.reshape(n_section, ex_dev, seq_len, width), due
     core = [(i, i ^ 1) for i in range(4)]
     far = [(i, i ^ 2) for i in range(4)]
     swap = [(0, 1), (1, 0)]
@@ -340,10 +343,9 @@
     for step in range(ex_dev + 2):
         new = {}
         if step == 0:
-            new["first"] = first
             new["peer"] = lax.ppermute(rows, "section", core)
-        if step == LAST_STEP:
-            new["last"] = last
+        if step in due:
+            new["due"] = due[step]
         if step < ex_dev:
             new["far"] = lax.ppermute(mine[step:step + 1], "section", far)
         if 1 <= step <= ex_dev:
@@ -363,15 +365,14 @@
             break
         whole, mine, new = together(whole, mine, new)
         if step == 0:
-            first = new["first"]
             whole = put(whole, new["peer"], 1, 0, zero)
-        if step == LAST_STEP:
-            last = new["last"]
+        if step in due:
+            due[step] = new["due"]
         for name, into in (("far", from_far), ("side", from_side), ("other_far", other_far),
                            ("other_side", other_side)):
             if name in new:
                 into.append(new[name])
-    return whole, first, last
+    return whole, due
 
 
 def per_device(encoder_rows, w_key, w_value, query, grad_context, source):
@@ -395,18 +396,22 @@
     filled = jnp.any(hit, axis=1)
 
     w_send = pack_weights(me, w_key, w_value, n_section, chunks, cols)
+    w_first = jnp.concatenate(section_swap([w_send[0][r] for r in range(n_section)]))
+    qg_send = pack_queries(slot, filled, query, grad_context, n_section, n_dp, chunks)
+    mine = my_share(encoder_rows)
+    w_first, mine, qg_send = together(w_first, mine, qg_send)
     qg_all = [
         lax.all_to_all(
             qg.reshape((n_section * n_dp,) + qg.shape[2:]),
             ("section", "dp"), split_axis=0, concat_axis=0, tiled=True,
         ).reshape(qg.shape)
-        for qg in pack_queries(slot, filled, query, grad_context, n_section, n_dp, chunks)
+        for qg in qg_send
     ]
-    w_first = jnp.concatenate(section_swap([w_send[0][r] for r in range(n_section)]))
-    plane, (w_first, qg_all[0]), qg_all[1:] = spread_examples(encoder_rows, (w_first, qg_all[0]), qg_all[1:])
+    plane, due = spread_examples(encoder_rows, mine, {3: qg_all[0]})
+    qg_all[0] = due[3]
     flat = plane.reshape(n_section * ex_dev * seq_len, width)
 
-    outs, grads = [], []
+    outs, totals = [], []
     moved = None
     for c in range(chunks):
         w_own = w_first
@@ -418,21 +423,25 @@
         kv = project(me, flat, w_all)
         kv = kv.reshape(n_section, ex_dev, seq_len, 2 * cols)
         out, dkv = attend(local, kv, qg_all[c])
+        if c == 0:
+            dkv, qg_all = together(dkv, qg_all)
         if moved is not None:
             dkv, _ = together(dkv, moved)
-        total = lax.psum_scatter(
-            weight_grad(flat, dkv, n_section, n_dp), "dp", scatter_dimension=0, tiled=True
-        )
-        blocks = [
-            lax.dynamic_slice_in_dim(total, (section_idx ^ r) * d_rows, d_rows, axis=1)
-            for r in range(n_section)
-        ]
-        grads.append(section_swap(blocks))
+        part = weight_grad(me, flat, dkv, n_section, n_dp)
+        totals.append(lax.psum_scatter(
+            part.reshape(n_dp * n_section * 2 * cols, d_rows), "dp", scatter_dimension=0, tiled=True
+        ))
         moved = to_owner_plane(out)
         outs.append(to_owner_section(moved))
 
     context, grad_query = unpack_outputs(me, (dp_idx - my_holder) % n_dp, outs, dec_dev)
-    return context, grad_query, finish_grads(me, grads, cols)
+    grads = []
+    for total in totals:
+        if grads:
+            total, grads[-1] = together(total, grads[-1])
+        blocks = [total] + [total[r * 2 * cols:(r + 1) * 2 * cols] for r in range(1, n_section)]
+        grads.append(section_swap(blocks))
+    return context, grad_query, finish_grads(me, grads, cols, d_rows)
 
 
 def solution(mesh):

time: 553 us -> 554 us (level)
  the two profiles are of different devices: /device:TPU:11 before, /device:TPU:0 now
where the time goes in v3:
time: 554 us; the launch traced here: 553 us
  waiting for transfers between devices  250 us (45%)
  Pallas kernels  130 us (23%)
  local copies, waits for them, and re-layouts  76.8 us (14%)
  starting transfers between devices  65.7 us (12%)
  other arithmetic  15.8 us (3%)
  between operations  14.2 us (3%)
    ppermute x6, waiting for transfers between devices, to_owner_plane(): lax.ppermute(block, 'dp', [(i, (i + k) % n_dp) for i in range(n_dp)])  104 us
    ppermute x3, waiting for transfers between devices, spread_examples(): new['far'] = lax.ppermute(mine[step:step + 1], 'section', far)  62.9 us
    all_to_all x2, waiting for transfers between devices, per_device(): lax.all_to_all(qg.reshape((n_section * n_dp,) + qg.shape[2:]), ('section'...  44.5 us
    pallas_call x2, Pallas kernels, attend(): pl.pallas_call(functools.partial(attend_kernel, seqs, ex_dev, seq_len, q_...  42.9 us
    pallas_call x2, Pallas kernels, weight_grad(): pl.pallas_call(functools.partial(weight_grad_kernel, n_section), grid_spe...  38.4 us
    pallas_call x2, Pallas kernels, project(): pl.pallas_call(functools.partial(project_kernel, n_dp, n_section), grid_s...  38.3 us
    ppermute x6, starting transfers between devices, to_owner_plane(): lax.ppermute(block, 'dp', [(i, (i + k) % n_dp) for i in range(n_dp)])  30.6 us
    ppermute x18, waiting for transfers between devices, section_swap(): lax.ppermute(blocks[r], 'section', [(i, i ^ r) for i in range(n_section)])  28.6 us
  transfers between devices with their start and end apart: 43, of which 16 were waited for; matrix products, arithmetic and copies ran while one was open for 14% of the time, Pallas kernels for 23%

profile of v3, /device:TPU:0, one launch (start us, length us, event | category | flops | bytes accessed | tf_op | source)
XLA Modules:
  0.0 553.0 jit_solution(11992963488565218852)
XLA Ops:
  11.1 2.4 collective-permute-start.2
  15.9 4.1 constant_dynamic-slice_fusion.24
  20.5 3.0 shard_map.86
  23.5 2.8 collective-permute-done.1
  26.4 2.2 pad_maximum_fusion
  29.6 2.4 collective-permute-start.24
  33.6 2.0 collective-permute-start.3
  35.6 9.0 %broadcast_in_dim.62 = bf16[4,3,256,4096]{3,2,1,0:T(8,128)(2,1)} broadcast(bf16[]{:T(256)} %constant.354.clone.1), dimensions={} | broadcast | bytes 25165826 | tf_op jit(solution)/shard_map/broadcast_in_dim | solution.py:341
  44.6 3.1 bitcast_dynamic-update-slice_fusion.1
  47.7 5.0 all-to-all-start
  52.8 2.1 pad_maximum_fusion.1
  55.0 19.5 %collective-permute-done.3 = bf16[1,128,4096]{2,1,0:T(8,128)(2,1)} collective-permute-done((bf16[1,128,4096]{2,1,0:T(8,128)(2,1)S(1)}, bf16[1,128,4096]{2,1,0:T(8,128)(2,1)}, u32[]{:S(2)}, u32[]{:S(2)}) %collective-permute-start.3) | collective-permute-done | bytes 1048608 | tf_op jit(solution)/shard_map/ppermute | solution.py:350
  74.5 2.2 collective-permute-start.7
  78.0 2.3 collective-permute-start.5
  80.3 6.3 %bitcast_dynamic-update-slice_fusion = bf16[4,3,256,4096]{3,2,1,0:T(8,128)(2,1)} fusion(bf16[4,3,256,4096]{3,2,1,0:T(8,128)(2,1)} %bitcast_dynamic-update-slice_fusion.1, s32[]{:T(128)S(6)} %select_n.163, bf16[3,256,4096]{2,1,0:T(8,128)(2,1)} %collective-permute-done.4), kind=kLoop, calls=%fused_computation | loop fusion | bytes 12582916 | tf_op jit(solution)/shard_map/dynamic_update_slice | solution.py:339
  86.6 2.3 bitcast_dynamic-update-slice_fusion.13
  88.9 21.8 %collective-permute-done.5 = bf16[1,128,4096]{2,1,0:T(8,128)(2,1)S(1)} collective-permute-done((bf16[1,128,4096]{2,1,0:T(8,128)(2,1)S(1)}, bf16[1,128,4096]{2,1,0:T(8,128)(2,1)S(1)}, u32[]{:S(2)}, u32[]{:S(2)}) %collective-permute-start.5) | collective-permute-done | bytes 1048608 | tf_op jit(solution)/shard_map/ppermute | solution.py:350
  110.7 1.7 collective-permute-start.11
  114.7 1.7 collective-permute-start.8
  118.5 21.6 %collective-permute-done.8 = bf16[1,128,4096]{2,1,0:T(8,128)(2,1)} collective-permute-done((bf16[1,128,4096]{2,1,0:T(8,128)(2,1)S(1)}, bf16[1,128,4096]{2,1,0:T(8,128)(2,1)}, u32[]{:S(2)}, u32[]{:S(2)}) %collective-permute-start.8) | collective-permute-done | bytes 1048608 | tf_op jit(solution)/shard_map/ppermute | solution.py:350
  140.8 2.3 bitcast_dynamic-update-slice_fusion.9
  146.3 5.1 all-to-all-done
  151.4 4.4 all-to-all-start.1
  155.9 10.2 %collective-permute-done.14 = bf16[1,128,4096]{2,1,0:T(8,128)(2,1)} collective-permute-done((bf16[1,128,4096]{2,1,0:T(8,128)(2,1)}, bf16[1,128,4096]{2,1,0:T(8,128)(2,1)}, u32[]{:S(2)}, u32[]{:S(2)}) %collective-permute-start.14) | collective-permute-done | bytes 1048608 | tf_op jit(solution)/shard_map/ppermute | solution.py:353
  166.2 2.4 bitcast_dynamic-update-slice_fusion.5
  168.5 2.3 bitcast_dynamic-update-slice_fusion.4
  170.8 2.3 bitcast_dynamic-update-slice_fusion.3
  174.2 18.8 %shard_map.87 = bf16[3072,512]{1,0:T(8,128)(2,1)} custom-call(s32[1]{0:T(128)} %bitcast.at, bf16[3072,4096]{1,0:T(8,128)(2,1)} %bitcast.92, bf16[4,4,256,512]{3,2,1,0:T(8,128)(2,1)} %bitcast.107), custom_call_target="tpu_custom_call" | custom-call | flops 12884901888 | bytes 36700160 | tf_op jit(solution)/shard_map/pallas_call | solution.py:129
  193.1 1.9 copy-done.16
  195.0 21.1 %shard_map.88 = (bf16[4,4,2,128,256]{4,3,2,1,0:T(8,128)(2,1)S(1)}, bf16[2,256,3072]{2,1,0:T(8,128)(2,1)S(1)}) custom-call(s32[16]{0:T(128)S(1)} %reshape.68.local_ref, bf16[4,3,256,512]{3,2,1,0:T(8,128)(2,1)S(1)} %bitcast.90, bf16[4,3,256,512]{3,2,1,0:T(8,128)(2,1)S(1)} %bitcast.91, bf16[4,4,2,128,256]{4,3,2,1,0:T(8,128)(2,1)S(1)} %bitcast.87), custom_call_target="tpu_custom_call" | custom-call | flops 3221225472 | bytes 10485760 | tf_op jit(solution)/shard_map/pallas_call | solution.py:229
  216.1 1.6 copy-done.3
  217.7 39.4 %all-to-all-done.1 = bf16[16,2,128,256]{3,2,1,0:T(8,128)(2,1)} async-done(((bf16[16,2,128,256]{3,2,1,0:T(8,128)(2,1)}), bf16[16,2,128,256]{3,2,1,0:T(8,128)(2,1)}, u32[]{:S(2)}, u32[]{:S(2)}) %all-to-all-start.1) | async-done | bytes 2097184 | tf_op jit(solution)/shard_map/all_to_all | solution.py:404
  257.1 19.1 %shard_map.93 = bf16[16,512,256]{2,1,0:T(8,128)(2,1)} custom-call(s32[1]{0:T(128)} %bitcast.at, bf16[3072,4096]{1,0:T(8,128)(2,1)} %bitcast.93, bf16[3072,4096]{1,0:T(8,128)(2,1)} %bitcast.94, bf16[3072,4096]{1,0:T(8,128)(2,1)} %bitcast.95, bf16[3072,4096]{1,0:T(8,128)(2,1)} %bitcast.96, bf16[2,256,3072]{2,1,0:T(8,128)(2,1)} %copy-done.3), custom_call_target="tpu_custom_call" | custom-call | flops 12884901888 | bytes 32505856 | tf_op jit(solution)/shard_map/pallas_call | solution.py:162
  277.5 4.9 collective-permute-start.18
  282.9 19.5 %shard_map.89 = bf16[3072,512]{1,0:T(8,128)(2,1)} custom-call(s32[1]{0:T(128)} %bitcast.at, bf16[3072,4096]{1,0:T(8,128)(2,1)} %bitcast.97, bf16[4,4,256,512]{3,2,1,0:T(8,128)(2,1)} %bitcast.106), custom_call_target="tpu_custom_call" | custom-call | flops 12884901888 | bytes 36700160 | tf_op jit(solution)/shard_map/pallas_call | solution.py:129
  302.4 1.9 copy-done.15
  304.3 21.8 %shard_map.90 = (bf16[4,4,2,128,256]{4,3,2,1,0:T(8,128)(2,1)S(1)}, bf16[2,256,3072]{2,1,0:T(8,128)(2,1)S(1)}) custom-call(s32[16]{0:T(128)S(1)} %reshape.68.local_ref, bf16[4,3,256,512]{3,2,1,0:T(8,128)(2,1)S(1)} %bitcast.88, bf16[4,3,256,512]{3,2,1,0:T(8,128)(2,1)S(1)} %bitcast.89, bf16[4,4,2,128,256]{4,3,2,1,0:T(8,128)(2,1)} %bitcast.39.qg_ref), custom_call_target="tpu_custom_call" | custom-call | flops 3221225472 | bytes 10485760 | tf_op jit(solution)/shard_map/pallas_call | solution.py:229
  326.1 1.6 copy-done.2
  329.0 36.6 %collective-permute-done.17 = bf16[4,2,128,256]{3,2,1,0:T(8,128)(2,1)} collective-permute-done((bf16[4,2,128,256]{3,2,1,0:T(8,128)(2,1)S(1)}, bf16[4,2,128,256]{3,2,1,0:T(8,128)(2,1)}, u32[]{:S(2)}, u32[]{:S(2)}) %collective-permute-start.17) | collective-permute-done | bytes 524320 | tf_op jit(solution)/shard_map/ppermute | solution.py:301
  365.6 19.3 %shard_map.92 = bf16[16,512,256]{2,1,0:T(8,128)(2,1)} custom-call(s32[1]{0:T(128)} %bitcast.at, bf16[3072,4096]{1,0:T(8,128)(2,1)} %bitcast.98, bf16[3072,4096]{1,0:T(8,128)(2,1)} %bitcast.99, bf16[3072,4096]{1,0:T(8,128)(2,1)} %bitcast.100, bf16[3072,4096]{1,0:T(8,128)(2,1)} %bitcast.101, bf16[2,256,3072]{2,1,0:T(8,128)(2,1)} %copy-done.2), custom_call_target="tpu_custom_call" | custom-call | flops 12884901888 | bytes 32505856 | tf_op jit(solution)/shard_map/pallas_call | solution.py:162
  385.0 1.5 dynamic-slice_bitcast_fusion.2
  386.5 23.2 %collective-permute-start.26 = (bf16[4,2,128,256]{3,2,1,0:T(8,128)(2,1)S(1)}, bf16[4,2,128,256]{3,2,1,0:T(8,128)(2,1)}, u32[]{:S(2)}, u32[]{:S(2)}) collective-permute-start(bf16[4,2,128,256]{3,2,1,0:T(8,128)(2,1)S(1)} %get-tuple-element.95), channel_id=1, source_target_pairs={{0,4},{2,6},{4,0},{6,2},{1,5},{3,7},{5,1},{7,3},{8,12},{10,14},{12... | collective-permute-start | bytes 1572872 | tf_op jit(solution)/shard_map/ppermute | solution.py:301
  409.7 1.9 collective-permute-start.25
  411.7 1.9 dynamic-slice_bitcast_fusion.6
  413.6 1.8 constant_dynamic-slice_fusion.12
  415.4 1.8 constant_dynamic-slice_fusion.13
  417.2 1.8 constant_dynamic-slice_fusion.14
  420.7 1.6 collective-permute-start.20
  425.4 67.4 %collective-permute-done.26 = bf16[4,2,128,256]{3,2,1,0:T(8,128)(2,1)} collective-permute-done((bf16[4,2,128,256]{3,2,1,0:T(8,128)(2,1)S(1)}, bf16[4,2,128,256]{3,2,1,0:T(8,128)(2,1)}, u32[]{:S(2)}, u32[]{:S(2)}) %collective-permute-start.26) | collective-permute-done | bytes 524320 | tf_op jit(solution)/shard_map/ppermute | solution.py:301
  492.8 1.8 constant_dynamic-slice_fusion.1
  494.6 1.9 constant_dynamic-slice_fusion.2
  498.3 1.8 pad_maximum_fusion.7
  500.4 1.8 pad_maximum_fusion.8
  502.3 1.9 pad_maximum_fusion.9
  504.1 1.4 collective-permute-done.32.refs_2_
  507.5 2.8 collective-permute-done.33.refs_3_
  511.1 1.9 collective-permute-start.30
  514.6 1.5 collective-permute-start.35
  517.9 4.6 collective-permute-done.29.refs_6_
  522.5 10.4 %collective-permute-done.30.refs_7_ = bf16[4,2,128,256]{3,2,1,0:T(8,128)(2,1)} collective-permute-done((bf16[4,2,128,256]{3,2,1,0:T(8,128)(2,1)}, bf16[4,2,128,256]{3,2,1,0:T(8,128)(2,1)}, u32[]{:S(2)}, u32[]{:S(2)}) %collective-permute-start.30) | collective-permute-done | bytes 524320 | tf_op jit(solution)/shard_map/ppermute | solution.py:290
  532.9 4.7 shard_map.91
  537.6 1.7 collective-permute-done.35.refs_6_
  539.3 4.8 collective-permute-done.36.refs_7_
  544.1 2.4 shard_map.94
  (131 shorter events, 36.5 us)
Async XLA Ops:
  7.2 13.3 %copy-start.4 = (bf16[4,128,2048]{2,1,0:T(8,128)(2,1)S(1)}, bf16[4,128,2048]{2,1,0:T(8,128)(2,1)}, u32[]{:S(2)}) copy-start(bf16[4,128,2048]{2,1,0:T(8,128)(2,1)} %q_ref.1) | copy-start | bytes 6291460
  7.2 167.1 %all-gather.3.cloned.1.call-start = ((), (), s32[]{:S(2)}) async-start(), calls=%async_computation.4 | async-start | bytes 5242880 | tf_op jit(solution)/shard_map/all_gather | solution.py:421
  7.2 1.4 copy-start.9
  8.6 1.2 copy-start.10
  11.1 12.4 %collective-permute-start.2 = (bf16[256,512]{1,0:T(8,128)(2,1)}, bf16[256,512]{1,0:T(8,128)(2,1)}, u32[]{:S(2)}, u32[]{:S(2)}) collective-permute-start(bf16[256,512]{1,0:T(8,128)(2,1)} %get-tuple-element.114), channel_id=1, source_target_pairs={{0,24},{8,16},{16,8},{24,0},{1,25},{9,17},{17,9},{25,1},{2,26},{10... | collective-permute-start | bytes 786440 | tf_op jit(solution)/shard_map/ppermute | solution.py:290
  13.6 12.8 %collective-permute-start.1 = (bf16[256,512]{1,0:T(8,128)(2,1)}, bf16[256,512]{1,0:T(8,128)(2,1)}, u32[]{:S(2)}, u32[]{:S(2)}) collective-permute-start(bf16[256,512]{1,0:T(8,128)(2,1)} %get-tuple-element.115), channel_id=1, source_target_pairs={{0,16},{8,24},{16,0},{24,8},{1,17},{9,25},{17,1},{25,9},{2,18},{10... | collective-permute-start | bytes 786440 | tf_op jit(solution)/shard_map/ppermute | solution.py:290
  14.2 12.2 %collective-permute-start = (bf16[256,512]{1,0:T(8,128)(2,1)}, bf16[256,512]{1,0:T(8,128)(2,1)}, u32[]{:S(2)}, u32[]{:S(2)}) collective-permute-start(bf16[256,512]{1,0:T(8,128)(2,1)} %get-tuple-element.116), channel_id=1, source_target_pairs={{0,8},{8,0},{16,24},{24,16},{1,9},{9,1},{17,25},{25,17},{2,10},{10... | collective-permute-start | bytes 786440 | tf_op jit(solution)/shard_map/ppermute | solution.py:290
  15.9 4.6 copy-start.5
  28.6 45.9 %collective-permute-start.4 = (bf16[3,256,4096]{2,1,0:T(8,128)(2,1)}, bf16[3,256,4096]{2,1,0:T(8,128)(2,1)}, u32[]{:S(2)}, u32[]{:S(2)}) collective-permute-start(bf16[3,256,4096]{2,1,0:T(8,128)(2,1)} %param.6), channel_id=1, source_target_pairs={{0,8},{8,0},{16,24},{24,16},{1,9},{9,1},{17,25},{25,17},{2,10},{10... | collective-permute-start | bytes 18874376 | tf_op jit(solution)/shard_map/ppermute | solution.py:346
  29.6 23.2 %collective-permute-start.24 = (bf16[256,512]{1,0:T(8,128)(2,1)}, bf16[256,512]{1,0:T(8,128)(2,1)}, u32[]{:S(2)}, u32[]{:S(2)}) collective-permute-start(bf16[256,512]{1,0:T(8,128)(2,1)} %get-tuple-element.110), channel_id=1, source_target_pairs={{0,24},{8,16},{16,8},{24,0},{1,25},{9,17},{17,9},{25,1},{2,26},{10... | collective-permute-start | bytes 786440 | tf_op jit(solution)/shard_map/ppermute | solution.py:290
  32.0 20.8 %collective-permute-start.23 = (bf16[256,512]{1,0:T(8,128)(2,1)}, bf16[256,512]{1,0:T(8,128)(2,1)}, u32[]{:S(2)}, u32[]{:S(2)}) collective-permute-start(bf16[256,512]{1,0:T(8,128)(2,1)} %get-tuple-element.111), channel_id=1, source_target_pairs={{0,16},{8,24},{16,0},{24,8},{1,17},{9,25},{17,1},{25,9},{2,18},{10... | collective-permute-start | bytes 786440 | tf_op jit(solution)/shard_map/ppermute | solution.py:290
  32.0 20.8 %collective-permute-start.22 = (bf16[256,512]{1,0:T(8,128)(2,1)}, bf16[256,512]{1,0:T(8,128)(2,1)}, u32[]{:S(2)}, u32[]{:S(2)}) collective-permute-start(bf16[256,512]{1,0:T(8,128)(2,1)} %get-tuple-element.112), channel_id=1, source_target_pairs={{0,8},{8,0},{16,24},{24,16},{1,9},{9,1},{17,25},{25,17},{2,10},{10... | collective-permute-start | bytes 786440 | tf_op jit(solution)/shard_map/ppermute | solution.py:290
  32.1 12.4 %slice-start = ((s8[6291456]{0:T(1024)(128)(4,1)}), s8[4194304]{0:T(1024)(128)(4,1)S(1)}, s32[]{:S(2)}) async-start(s8[6291456]{0:T(1024)(128)(4,1)} %bitcast.104), calls=%async_computation.8 | async-start | bytes 8388608
  33.6 11.0 %slice-start.1 = ((s8[6291456]{0:T(1024)(128)(4,1)}), s8[2097152]{0:T(1024)(128)(4,1)S(1)}, s32[]{:S(2)}) async-start(s8[6291456]{0:T(1024)(128)(4,1)} %bitcast.104), calls=%async_computation.9 | async-start | bytes 4194304
  33.6 40.9 %collective-permute-start.3 = (bf16[1,128,4096]{2,1,0:T(8,128)(2,1)S(1)}, bf16[1,128,4096]{2,1,0:T(8,128)(2,1)}, u32[]{:S(2)}, u32[]{:S(2)}) collective-permute-start(bf16[1,128,4096]{2,1,0:T(8,128)(2,1)S(1)} %slice.55), channel_id=1, source_target_pairs={{0,16},{8,24},{16,0},{24,8},{1,17},{9,25},{17,1},{25,9},{2,18},{10... | collective-permute-start | bytes 3145736 | tf_op jit(solution)/shard_map/ppermute | solution.py:350
  47.7 103.7 %all-to-all-start = ((bf16[16,2,128,256]{3,2,1,0:T(8,128)(2,1)}), bf16[16,2,128,256]{3,2,1,0:T(8,128)(2,1)S(1)}, u32[]{:S(2)}, u32[]{:S(2)}) async-start(bf16[16,2,128,256]{3,2,1,0:T(8,128)(2,1)} %bitcast.16), calls=%async_computation | async-start | bytes 4194304 | tf_op jit(solution)/shard_map/all_to_all | solution.py:404
  52.8 230.2 %all-gather.5.cloned.1.call-start = ((), (), s32[]{:S(2)}) async-start(), calls=%async_computation.5 | async-start | bytes 5242880 | tf_op jit(solution)/shard_map/all_gather | solution.py:421
  74.5 36.1 %collective-permute-start.6 = (bf16[1,128,4096]{2,1,0:T(8,128)(2,1)}, bf16[1,128,4096]{2,1,0:T(8,128)(2,1)S(1)}, u32[]{:S(2)}, u32[]{:S(2)}) collective-permute-start(bf16[1,128,4096]{2,1,0:T(8,128)(2,1)} %collective-permute-done.3), channel_id=1, source_target_pairs={{0,8},{8,0},{16,24},{24,16},{1,9},{9,1},{17,25},{25,17},{2,10},{10... | collective-permute-start | bytes 3145736 | tf_op jit(solution)/shard_map/ppermute | solution.py:354
  74.5 36.1 %collective-permute-start.7 = (bf16[1,128,4096]{2,1,0:T(8,128)(2,1)}, bf16[1,128,4096]{2,1,0:T(8,128)(2,1)S(1)}, u32[]{:S(2)}, u32[]{:S(2)}) collective-permute-start(bf16[1,128,4096]{2,1,0:T(8,128)(2,1)} %collective-permute-done.3), channel_id=1, source_target_pairs={{0,1},{1,0},{2,3},{3,2},{4,5},{5,4},{6,7},{7,6},{8,9},{9,8},{10,11... | collective-permute-start | bytes 3145736 | tf_op jit(solution)/shard_map/ppermute | solution.py:353
  78.0 32.7 %collective-permute-start.5 = (bf16[1,128,4096]{2,1,0:T(8,128)(2,1)S(1)}, bf16[1,128,4096]{2,1,0:T(8,128)(2,1)S(1)}, u32[]{:S(2)}, u32[]{:S(2)}) collective-permute-start(bf16[1,128,4096]{2,1,0:T(8,128)(2,1)S(1)} %slice.56), channel_id=1, source_target_pairs={{0,16},{8,24},{16,0},{24,8},{1,17},{9,25},{17,1},{25,9},{2,18},{10... | collective-permute-start | bytes 3145736 | tf_op jit(solution)/shard_map/ppermute | solution.py:350
  110.7 29.5 %collective-permute-start.9 = (bf16[1,128,4096]{2,1,0:T(8,128)(2,1)S(1)}, bf16[1,128,4096]{2,1,0:T(8,128)(2,1)S(1)}, u32[]{:S(2)}, u32[]{:S(2)}) collective-permute-start(bf16[1,128,4096]{2,1,0:T(8,128)(2,1)S(1)} %collective-permute-done.5), channel_id=1, source_target_pairs={{0,8},{8,0},{16,24},{24,16},{1,9},{9,1},{17,25},{25,17},{2,10},{10... | collective-permute-start | bytes 3145736 | tf_op jit(solution)/shard_map/ppermute | solution.py:354
  110.7 29.5 %collective-permute-start.11 = (bf16[1,128,4096]{2,1,0:T(8,128)(2,1)S(1)}, bf16[1,128,4096]{2,1,0:T(8,128)(2,1)S(1)}, u32[]{:S(2)}, u32[]{:S(2)}) collective-permute-start(bf16[1,128,4096]{2,1,0:T(8,128)(2,1)S(1)} %collective-permute-done.5), channel_id=1, source_target_pairs={{0,1},{1,0},{2,3},{3,2},{4,5},{5,4},{6,7},{7,6},{8,9},{9,8},{10,11... | collective-permute-start | bytes 3145736 | tf_op jit(solution)/shard_map/ppermute | solution.py:353
  114.7 25.4 %collective-permute-start.8 = (bf16[1,128,4096]{2,1,0:T(8,128)(2,1)S(1)}, bf16[1,128,4096]{2,1,0:T(8,128)(2,1)}, u32[]{:S(2)}, u32[]{:S(2)}) collective-permute-start(bf16[1,128,4096]{2,1,0:T(8,128)(2,1)S(1)} %slice.57), channel_id=1, source_target_pairs={{0,16},{8,24},{16,0},{24,8},{1,17},{9,25},{17,1},{25,9},{2,18},{10... | collective-permute-start | bytes 3145736 | tf_op jit(solution)/shard_map/ppermute | solution.py:350
  116.4 23.8 %collective-permute-start.10 = (bf16[1,128,4096]{2,1,0:T(8,128)(2,1)S(1)}, bf16[1,128,4096]{2,1,0:T(8,128)(2,1)S(1)}, u32[]{:S(2)}, u32[]{:S(2)}) collective-permute-start(bf16[1,128,4096]{2,1,0:T(8,128)(2,1)S(1)} %collective-permute-done.7), channel_id=1, source_target_pairs={{0,8},{8,0},{16,24},{24,16},{1,9},{9,1},{17,25},{25,17},{2,10},{10... | collective-permute-start | bytes 3145736 | tf_op jit(solution)/shard_map/ppermute | solution.py:358
  140.2 15.7 %collective-permute-start.12 = (bf16[1,128,4096]{2,1,0:T(8,128)(2,1)}, bf16[1,128,4096]{2,1,0:T(8,128)(2,1)}, u32[]{:S(2)}, u32[]{:S(2)}) collective-permute-start(bf16[1,128,4096]{2,1,0:T(8,128)(2,1)} %collective-permute-done.8), channel_id=1, source_target_pairs={{0,8},{8,0},{16,24},{24,16},{1,9},{9,1},{17,25},{25,17},{2,10},{10... | collective-permute-start | bytes 3145736 | tf_op jit(solution)/shard_map/ppermute | solution.py:354
  140.3 25.9 %collective-permute-start.14 = (bf16[1,128,4096]{2,1,0:T(8,128)(2,1)}, bf16[1,128,4096]{2,1,0:T(8,128)(2,1)}, u32[]{:S(2)}, u32[]{:S(2)}) collective-permute-start(bf16[1,128,4096]{2,1,0:T(8,128)(2,1)} %collective-permute-done.8), channel_id=1, source_target_pairs={{0,1},{1,0},{2,3},{3,2},{4,5},{5,4},{6,7},{7,6},{8,9},{9,8},{10,11... | collective-permute-start | bytes 3145736 | tf_op jit(solution)/shard_map/ppermute | solution.py:353
  140.7 15.2 %collective-permute-start.13 = (bf16[1,128,4096]{2,1,0:T(8,128)(2,1)S(1)}, bf16[1,128,4096]{2,1,0:T(8,128)(2,1)}, u32[]{:S(2)}, u32[]{:S(2)}) collective-permute-start(bf16[1,128,4096]{2,1,0:T(8,128)(2,1)S(1)} %collective-permute-done.11), channel_id=1, source_target_pairs={{0,8},{8,0},{16,24},{24,16},{1,9},{9,1},{17,25},{25,17},{2,10},{10... | collective-permute-start | bytes 3145736 | tf_op jit(solution)/shard_map/ppermute | solution.py:358
  151.4 22.8 %copy-start.6 = (bf16[16,2,128,256]{3,2,1,0:T(8,128)(2,1)}, bf16[16,2,128,256]{3,2,1,0:T(8,128)(2,1)S(1)}, u32[]{:S(2)}) copy-start(bf16[16,2,128,256]{3,2,1,0:T(8,128)(2,1)S(1)} %all-to-all-done) | copy-start | bytes 6291460
  151.4 105.7 %all-to-all-start.1 = ((bf16[16,2,128,256]{3,2,1,0:T(8,128)(2,1)}), bf16[16,2,128,256]{3,2,1,0:T(8,128)(2,1)}, u32[]{:S(2)}, u32[]{:S(2)}) async-start(bf16[16,2,128,256]{3,2,1,0:T(8,128)(2,1)} %bitcast.38), calls=%async_computation.1 | async-start | bytes 4194304 | tf_op jit(solution)/shard_map/all_to_all | solution.py:404
  155.9 268.4 %reduce-scatter.5.cloned.1.call-start = ((), (), s32[]{:S(2)}) async-start(), calls=%async_computation.7 | async-start | bytes 5242880 | tf_op jit(solution)/shard_map/reduce_scatter | solution.py:431
  166.1 7.0 %collective-permute-start.15 = (bf16[1,128,4096]{2,1,0:T(8,128)(2,1)}, bf16[1,128,4096]{2,1,0:T(8,128)(2,1)S(1)}, u32[]{:S(2)}, u32[]{:S(2)}) collective-permute-start(bf16[1,128,4096]{2,1,0:T(8,128)(2,1)} %collective-permute-done.14), channel_id=1, source_target_pairs={{0,8},{8,0},{16,24},{24,16},{1,9},{9,1},{17,25},{25,17},{2,10},{10... | collective-permute-start | bytes 3145736 | tf_op jit(solution)/shard_map/ppermute | solution.py:358
  174.2 18.8 %copy-start.7 = (bf16[16,2,128,256]{3,2,1,0:T(8,128)(2,1)S(1)}, bf16[16,2,128,256]{3,2,1,0:T(8,128)(2,1)}, u32[]{:S(2)}) copy-start(bf16[16,2,128,256]{3,2,1,0:T(8,128)(2,1)} %copy-done.6) | copy-start | bytes 6291460
  193.1 1.9 copy-start.16
  216.1 1.7 copy-start.3
  276.3 236.9 %reduce-scatter.3.cloned.1.call-start = ((), (), s32[]{:S(2)}) async-start(), calls=%async_computation.6 | async-start | bytes 5242880 | tf_op jit(solution)/shard_map/reduce_scatter | solution.py:431
  277.5 51.5 %collective-permute-start.18 = (bf16[4,2,128,256]{3,2,1,0:T(8,128)(2,1)}, bf16[4,2,128,256]{3,2,1,0:T(8,128)(2,1)}, u32[]{:S(2)}, u32[]{:S(2)}) collective-permute-start(bf16[4,2,128,256]{3,2,1,0:T(8,128)(2,1)} %get-tuple-element.101), channel_id=1, source_target_pairs={{0,6},{2,0},{4,2},{6,4},{1,7},{3,1},{5,3},{7,5},{8,14},{10,8},{12,... | collective-permute-start | bytes 1572872 | tf_op jit(solution)/shard_map/ppermute | solution.py:301
  282.4 83.2 %collective-permute-start.17 = (bf16[4,2,128,256]{3,2,1,0:T(8,128)(2,1)S(1)}, bf16[4,2,128,256]{3,2,1,0:T(8,128)(2,1)}, u32[]{:S(2)}, u32[]{:S(2)}) collective-permute-start(bf16[4,2,128,256]{3,2,1,0:T(8,128)(2,1)S(1)} %get-tuple-element.102), channel_id=1, source_target_pairs={{0,4},{2,6},{4,0},{6,2},{1,5},{3,7},{5,1},{7,3},{8,12},{10,14},{12... | collective-permute-start | bytes 1572872 | tf_op jit(solution)/shard_map/ppermute | solution.py:301
  282.4 83.2 %collective-permute-start.16 = (bf16[4,2,128,256]{3,2,1,0:T(8,128)(2,1)S(1)}, bf16[4,2,128,256]{3,2,1,0:T(8,128)(2,1)}, u32[]{:S(2)}, u32[]{:S(2)}) collective-permute-start(bf16[4,2,128,256]{3,2,1,0:T(8,128)(2,1)S(1)} %get-tuple-element.100), channel_id=1, source_target_pairs={{0,2},{2,4},{4,6},{6,0},{1,3},{3,5},{5,7},{7,1},{8,10},{10,12},{12... | collective-permute-start | bytes 1572872 | tf_op jit(solution)/shard_map/ppermute | solution.py:301
  302.4 1.9 copy-start.15
  326.1 1.6 copy-start.2
  327.7 1.3 copy-start.8
  386.5 36.7 %collective-permute-start.27 = (bf16[4,2,128,256]{3,2,1,0:T(8,128)(2,1)S(1)}, bf16[4,2,128,256]{3,2,1,0:T(8,128)(2,1)S(1)}, u32[]{:S(2)}, u32[]{:S(2)}) collective-permute-start(bf16[4,2,128,256]{3,2,1,0:T(8,128)(2,1)S(1)} %get-tuple-element.94), channel_id=1, source_target_pairs={{0,6},{2,0},{4,2},{6,4},{1,7},{3,1},{5,3},{7,5},{8,14},{10,8},{12,... | collective-permute-start | bytes 1572872 | tf_op jit(solution)/shard_map/ppermute | solution.py:301
  386.5 106.3 %collective-permute-start.26 = (bf16[4,2,128,256]{3,2,1,0:T(8,128)(2,1)S(1)}, bf16[4,2,128,256]{3,2,1,0:T(8,128)(2,1)}, u32[]{:S(2)}, u32[]{:S(2)}) collective-permute-start(bf16[4,2,128,256]{3,2,1,0:T(8,128)(2,1)S(1)} %get-tuple-element.95), channel_id=1, source_target_pairs={{0,4},{2,6},{4,0},{6,2},{1,5},{3,7},{5,1},{7,3},{8,12},{10,14},{12... | collective-permute-start | bytes 1572872 | tf_op jit(solution)/shard_map/ppermute | solution.py:301
  409.7 84.9 %collective-permute-start.25 = (bf16[4,2,128,256]{3,2,1,0:T(8,128)(2,1)S(1)}, bf16[4,2,128,256]{3,2,1,0:T(8,128)(2,1)}, u32[]{:S(2)}, u32[]{:S(2)}) collective-permute-start(bf16[4,2,128,256]{3,2,1,0:T(8,128)(2,1)S(1)} %get-tuple-element.93), channel_id=1, source_target_pairs={{0,2},{2,4},{4,6},{6,0},{1,3},{3,5},{5,7},{7,1},{8,10},{10,12},{12... | collective-permute-start | bytes 1572872 | tf_op jit(solution)/shard_map/ppermute | solution.py:301
  419.8 77.9 %collective-permute-start.19 = (bf16[4,2,128,256]{3,2,1,0:T(8,128)(2,1)}, bf16[4,2,128,256]{3,2,1,0:T(8,128)(2,1)S(1)}, u32[]{:S(2)}, u32[]{:S(2)}) collective-permute-start(bf16[4,2,128,256]{3,2,1,0:T(8,128)(2,1)} %pad_maximum_fusion.3), channel_id=1, source_target_pairs={{0,8},{8,0},{16,24},{24,16},{1,9},{9,1},{17,25},{25,17},{2,10},{10... | collective-permute-start | bytes 1572872 | tf_op jit(solution)/shard_map/ppermute | solution.py:290
  420.7 93.8 %collective-permute-start.20 = (bf16[4,2,128,256]{3,2,1,0:T(8,128)(2,1)}, bf16[4,2,128,256]{3,2,1,0:T(8,128)(2,1)S(1)}, u32[]{:S(2)}, u32[]{:S(2)}) collective-permute-start(bf16[4,2,128,256]{3,2,1,0:T(8,128)(2,1)} %pad_maximum_fusion.4), channel_id=1, source_target_pairs={{0,16},{8,24},{16,0},{24,8},{1,17},{9,25},{17,1},{25,9},{2,18},{10... | collective-permute-start | bytes 1572872 | tf_op jit(solution)/shard_map/ppermute | solution.py:290
  423.2 91.4 %collective-permute-start.21 = (bf16[4,2,128,256]{3,2,1,0:T(8,128)(2,1)}, bf16[4,2,128,256]{3,2,1,0:T(8,128)(2,1)S(1)}, u32[]{:S(2)}, u32[]{:S(2)}) collective-permute-start(bf16[4,2,128,256]{3,2,1,0:T(8,128)(2,1)} %pad_maximum_fusion.5), channel_id=1, source_target_pairs={{0,24},{8,16},{16,8},{24,0},{1,25},{9,17},{17,9},{25,1},{2,26},{10... | collective-permute-start | bytes 1572872 | tf_op jit(solution)/shard_map/ppermute | solution.py:290
  492.8 7.3 %collective-permute-start.31 = (bf16[512,256]{1,0:T(8,128)(2,1)S(1)}, bf16[512,256]{1,0:T(8,128)(2,1)S(1)}, u32[]{:S(2)}, u32[]{:S(2)}) collective-permute-start(bf16[512,256]{1,0:T(8,128)(2,1)S(1)} %get-tuple-element.108), channel_id=1, source_target_pairs={{0,8},{8,0},{16,24},{24,16},{1,9},{9,1},{17,25},{25,17},{2,10},{10... | collective-permute-start | bytes 786440 | tf_op jit(solution)/shard_map/ppermute | solution.py:290
  494.6 49.5 %copy-start = (bf16[2048,256]{1,0:T(8,128)(2,1)S(1)}, bf16[2048,256]{1,0:T(8,128)(2,1)}, u32[]{:S(2)}) copy-start(bf16[2048,256]{1,0:T(8,128)(2,1)} %reduce-scatter.5.cloned.1.call-done.refs_0_) | copy-start | bytes 3145732
  496.5 9.1 %collective-permute-start.32 = (bf16[512,256]{1,0:T(8,128)(2,1)S(1)}, bf16[512,256]{1,0:T(8,128)(2,1)S(1)}, u32[]{:S(2)}, u32[]{:S(2)}) collective-permute-start(bf16[512,256]{1,0:T(8,128)(2,1)S(1)} %get-tuple-element.107), channel_id=1, source_target_pairs={{0,16},{8,24},{16,0},{24,8},{1,17},{9,25},{17,1},{25,9},{2,18},{10... | collective-permute-start | bytes 786440 | tf_op jit(solution)/shard_map/ppermute | solution.py:290
  497.7 12.6 %collective-permute-start.33 = (bf16[512,256]{1,0:T(8,128)(2,1)S(1)}, bf16[512,256]{1,0:T(8,128)(2,1)S(1)}, u32[]{:S(2)}, u32[]{:S(2)}) collective-permute-start(bf16[512,256]{1,0:T(8,128)(2,1)S(1)} %get-tuple-element.106), channel_id=1, source_target_pairs={{0,24},{8,16},{16,8},{24,0},{1,25},{9,17},{17,9},{25,1},{2,26},{10... | collective-permute-start | bytes 786440 | tf_op jit(solution)/shard_map/ppermute | solution.py:290
  500.1 16.0 %collective-permute-start.28 = (bf16[4,2,128,256]{3,2,1,0:T(8,128)(2,1)}, bf16[4,2,128,256]{3,2,1,0:T(8,128)(2,1)S(1)}, u32[]{:S(2)}, u32[]{:S(2)}) collective-permute-start(bf16[4,2,128,256]{3,2,1,0:T(8,128)(2,1)} %pad_maximum_fusion.7), channel_id=1, source_target_pairs={{0,8},{8,0},{16,24},{24,16},{1,9},{9,1},{17,25},{25,17},{2,10},{10... | collective-permute-start | bytes 1572872 | tf_op jit(solution)/shard_map/ppermute | solution.py:290
  505.6 0.7 copy-start.11
  506.3 16.2 %collective-permute-start.29 = (bf16[4,2,128,256]{3,2,1,0:T(8,128)(2,1)}, bf16[4,2,128,256]{3,2,1,0:T(8,128)(2,1)}, u32[]{:S(2)}, u32[]{:S(2)}) collective-permute-start(bf16[4,2,128,256]{3,2,1,0:T(8,128)(2,1)} %pad_maximum_fusion.8), channel_id=1, source_target_pairs={{0,16},{8,24},{16,0},{24,8},{1,17},{9,25},{17,1},{25,9},{2,18},{10... | collective-permute-start | bytes 1572872 | tf_op jit(solution)/shard_map/ppermute | solution.py:290
  510.4 0.7 copy-start.13
  511.1 21.9 %collective-permute-start.30 = (bf16[4,2,128,256]{3,2,1,0:T(8,128)(2,1)}, bf16[4,2,128,256]{3,2,1,0:T(8,128)(2,1)}, u32[]{:S(2)}, u32[]{:S(2)}) collective-permute-start(bf16[4,2,128,256]{3,2,1,0:T(8,128)(2,1)} %pad_maximum_fusion.9), channel_id=1, source_target_pairs={{0,24},{8,16},{16,8},{24,0},{1,25},{9,17},{17,9},{25,1},{2,26},{10... | collective-permute-start | bytes 1572872 | tf_op jit(solution)/shard_map/ppermute | solution.py:290
  513.2 30.8 %copy-start.1 = (bf16[2048,256]{1,0:T(8,128)(2,1)S(1)}, bf16[2048,256]{1,0:T(8,128)(2,1)}, u32[]{:S(2)}) copy-start(bf16[2048,256]{1,0:T(8,128)(2,1)} %reduce-scatter.3.cloned.1.call-done.refs_4_) | copy-start | bytes 3145732
  513.2 30.8 %copy-start.12 = (bf16[512,256]{1,0:T(8,128)(2,1)S(1)}, bf16[512,256]{1,0:T(8,128)(2,1)}, u32[]{:S(2)}) copy-start(bf16[512,256]{1,0:T(8,128)(2,1)} %copy-done.11) | copy-start | bytes 786436
  513.2 30.9 %copy-start.14 = (bf16[512,256]{1,0:T(8,128)(2,1)S(1)}, bf16[512,256]{1,0:T(8,128)(2,1)}, u32[]{:S(2)}) copy-start(bf16[512,256]{1,0:T(8,128)(2,1)} %copy-done.13) | copy-start | bytes 786436
  514.5 23.1 %collective-permute-start.34 = (bf16[512,256]{1,0:T(8,128)(2,1)S(1)}, bf16[512,256]{1,0:T(8,128)(2,1)S(1)}, u32[]{:S(2)}, u32[]{:S(2)}) collective-permute-start(bf16[512,256]{1,0:T(8,128)(2,1)S(1)} %get-tuple-element.105), channel_id=1, source_target_pairs={{0,8},{8,0},{16,24},{24,16},{1,9},{9,1},{17,25},{25,17},{2,10},{10... | collective-permute-start | bytes 786440 | tf_op jit(solution)/shard_map/ppermute | solution.py:290
  514.6 24.7 %collective-permute-start.35 = (bf16[512,256]{1,0:T(8,128)(2,1)S(1)}, bf16[512,256]{1,0:T(8,128)(2,1)S(1)}, u32[]{:S(2)}, u32[]{:S(2)}) collective-permute-start(bf16[512,256]{1,0:T(8,128)(2,1)S(1)} %get-tuple-element.104), channel_id=1, source_target_pairs={{0,16},{8,24},{16,0},{24,8},{1,17},{9,25},{17,1},{25,9},{2,18},{10... | collective-permute-start | bytes 786440 | tf_op jit(solution)/shard_map/ppermute | solution.py:290
  516.1 27.9 %collective-permute-start.36 = (bf16[512,256]{1,0:T(8,128)(2,1)S(1)}, bf16[512,256]{1,0:T(8,128)(2,1)S(1)}, u32[]{:S(2)}, u32[]{:S(2)}) collective-permute-start(bf16[512,256]{1,0:T(8,128)(2,1)S(1)} %get-tuple-element.103), channel_id=1, source_target_pairs={{0,24},{8,16},{16,8},{24,0},{1,25},{9,17},{17,9},{25,1},{2,26},{10... | collective-permute-start | bytes 786440 | tf_op jit(solution)/shard_map/ppermute | solution.py:290
Sparse Core Ops, SparseCore 0:
  28.7 127.3 all-gather.2
  157.7 114.7 all-gather.4
  276.4 116.2 reduce-scatter.4
  395.0 118.2 reduce-scatter.2

commit v4 on v3

--- a/solution.py
+++ b/solution.py
@@ -291,16 +291,12 @@
     return out
 
 
-def to_owner_plane(out):
+def to_owner(out, k):
     n_dp = out.shape[1]
-    dp_idx = lax.axis_index("dp")
-    moved = []
-    for k in range(n_dp):
-        block = lax.dynamic_index_in_dim(out, (dp_idx + k) % n_dp, 1, keepdims=False)
-        if k:
-            block = lax.ppermute(block, "dp", [(i, (i + k) % n_dp) for i in range(n_dp)])
-        moved.append(block)
-    return moved
+    block = lax.dynamic_index_in_dim(out, (lax.axis_index("dp") + k) % n_dp, 1, keepdims=False)
+    if k == 0:
+        return block
+    return lax.ppermute(block, "dp", [(i, (i + k) % n_dp) for i in range(n_dp)])
 
 
 def to_owner_section(moved):
@@ -411,7 +407,7 @@
     qg_all[0] = due[3]
     flat = plane.reshape(n_section * ex_dev * seq_len, width)
 
-    outs, totals = [], []
+    outs, grads = [], []
     moved = None
     for c in range(chunks):
         w_own = w_first
@@ -425,22 +421,22 @@
         out, dkv = attend(local, kv, qg_all[c])
         if c == 0:
             dkv, qg_all = together(dkv, qg_all)
+        moving = [to_owner(out, k) for k in range(n_dp)]
+        part = weight_grad(me, flat, dkv, n_section, n_dp)
         if moved is not None:
-            dkv, _ = together(dkv, moved)
-        part = weight_grad(me, flat, dkv, n_section, n_dp)
-        totals.append(lax.psum_scatter(
+            part, moved, moving[1] = together(part, moved, moving[1])
+        moved = moving
+        total = lax.psum_scatter(
             part.reshape(n_dp * n_section * 2 * cols, d_rows), "dp", scatter_dimension=0, tiled=True
-        ))
-        moved = to_owner_plane(out)
-        outs.append(to_owner_section(moved))
-
-    context, grad_query = unpack_outputs(me, (dp_idx - my_holder) % n_dp, outs, dec_dev)
-    grads = []
-    for total in totals:
+        )
         if grads:
-            total, grads[-1] = together(total, grads[-1])
+            moving, grads[-1] = together(moving, grads[-1])
+        outs.append(to_owner_section(moving))
+        total, outs[-1] = together(total, outs[-1])
         blocks = [total] + [total[r * 2 * cols:(r + 1) * 2 * cols] for r in range(1, n_section)]
         grads.append(section_swap(blocks))
+
+    context, grad_query = unpack_outputs(me, (dp_idx - my_holder) % n_dp, outs, dec_dev)
     return context, grad_query, finish_grads(me, grads, cols, d_rows)
 
 

time: 554 us -> 563 us (1.016)
  the two profiles are of different devices: /device:TPU:0 before, /device:TPU:11 now
where the time goes in v4:
time: 563 us; the launch traced here: 561 us
  waiting for transfers between devices  276 us (49%)
  Pallas kernels  130 us (23%)
  local copies, waits for them, and re-layouts  75.9 us (13%)
  starting transfers between devices  56.1 us (10%)
  between operations  14.2 us (3%)
  other arithmetic  9.23 us (2%)
    ppermute x6, waiting for transfers between devices, to_owner(): return lax.ppermute(block, 'dp', [(i, (i + k) % n_dp) for i in range(n_dp)])  120 us
    ppermute x3, waiting for transfers between devices, spread_examples(): new['far'] = lax.ppermute(mine[step:step + 1], 'section', far)  61.6 us
    ppermute x18, waiting for transfers between devices, section_swap(): lax.ppermute(blocks[r], 'section', [(i, i ^ r) for i in range(n_section)])  43.8 us
    pallas_call x2, Pallas kernels, attend(): pl.pallas_call(functools.partial(attend_kernel, seqs, ex_dev, seq_len, q_...  42.9 us
    pallas_call x2, Pallas kernels, weight_grad(): pl.pallas_call(functools.partial(weight_grad_kernel, n_section), grid_spe...  38.4 us
    pallas_call x2, Pallas kernels, project(): pl.pallas_call(functools.partial(project_kernel, n_dp, n_section), grid_s...  38.2 us
    all_to_all x2, waiting for transfers between devices, per_device(): lax.all_to_all(qg.reshape((n_section * n_dp,) + qg.shape[2:]), ('section'...  35.3 us
    dynamic_update_slice x14, local copies, waits for them, and re-layouts, put(): lax.dynamic_update_slice(whole, piece[None], (me ^ r, jnp.int32(example),...  28.5 us
  transfers between devices with their start and end apart: 43, of which 18 were waited for; matrix products, arithmetic and copies ran while one was open for 11% of the time, Pallas kernels for 23%

profile of v4, /device:TPU:11, one launch (start us, length us, event | category | flops | bytes accessed | tf_op | source)
XLA Modules:
  0.0 561.1 jit_solution(9818796948942254937)
XLA Ops:
  11.0 1.8 collective-permute-start.2
  14.9 3.9 constant_dynamic-slice_fusion.28
  19.3 1.6 copy-done.4
  20.9 1.6 copy-done.5
  22.5 3.0 shard_map.86
  25.8 2.2 pad_maximum_fusion
  29.4 1.2 collective-permute-start.24
  31.6 1.3 slice.55
  32.9 1.3 collective-permute-start.3
  34.2 9.0 %broadcast_in_dim.62 = bf16[4,3,256,4096]{3,2,1,0:T(8,128)(2,1)} broadcast(bf16[]{:T(256)} %constant.258.clone.1), dimensions={} | broadcast | bytes 25165826 | tf_op jit(solution)/shard_map/broadcast_in_dim | solution.py:337
  43.2 3.2 bitcast_dynamic-update-slice_fusion.1
  46.5 5.7 %all-to-all-start = ((bf16[16,2,128,256]{3,2,1,0:T(8,128)(2,1)}), bf16[16,2,128,256]{3,2,1,0:T(8,128)(2,1)S(1)}, u32[]{:S(2)}, u32[]{:S(2)}) async-start(bf16[16,2,128,256]{3,2,1,0:T(8,128)(2,1)} %bitcast.16), calls=%async_computation | async-start | bytes 4194304 | tf_op jit(solution)/shard_map/all_to_all | solution.py:400
  52.2 2.2 pad_maximum_fusion.1
  54.4 15.3 %collective-permute-done.3 = bf16[1,128,4096]{2,1,0:T(8,128)(2,1)} collective-permute-done((bf16[1,128,4096]{2,1,0:T(8,128)(2,1)S(1)}, bf16[1,128,4096]{2,1,0:T(8,128)(2,1)}, u32[]{:S(2)}, u32[]{:S(2)}) %collective-permute-start.3) | collective-permute-done | bytes 1048608 | tf_op jit(solution)/shard_map/ppermute | solution.py:346
  69.7 1.6 collective-permute-start.6
  71.5 1.3 slice.56
  72.8 1.3 collective-permute-start.5
  74.2 6.2 %bitcast_dynamic-update-slice_fusion = bf16[4,3,256,4096]{3,2,1,0:T(8,128)(2,1)} fusion(bf16[4,3,256,4096]{3,2,1,0:T(8,128)(2,1)} %bitcast_dynamic-update-slice_fusion.1, s32[]{:T(128)S(6)} %select_n.161, bf16[3,256,4096]{2,1,0:T(8,128)(2,1)} %collective-permute-done.4), kind=kLoop, calls=%fused_computation | loop fusion | bytes 12582916 | tf_op jit(solution)/shard_map/dynamic_update_slice | solution.py:335
  80.4 2.3 bitcast_dynamic-update-slice_fusion.13
  82.7 19.6 %collective-permute-done.5 = bf16[1,128,4096]{2,1,0:T(8,128)(2,1)S(1)} collective-permute-done((bf16[1,128,4096]{2,1,0:T(8,128)(2,1)S(1)}, bf16[1,128,4096]{2,1,0:T(8,128)(2,1)S(1)}, u32[]{:S(2)}, u32[]{:S(2)}) %collective-permute-start.5) | collective-permute-done | bytes 1048608 | tf_op jit(solution)/shard_map/ppermute | solution.py:346
  103.3 1.3 collective-permute-start.11
  105.6 1.3 slice.57
  106.9 1.6 collective-permute-start.8
  111.3 26.6 %collective-permute-done.8 = bf16[1,128,4096]{2,1,0:T(8,128)(2,1)} collective-permute-done((bf16[1,128,4096]{2,1,0:T(8,128)(2,1)S(1)}, bf16[1,128,4096]{2,1,0:T(8,128)(2,1)}, u32[]{:S(2)}, u32[]{:S(2)}) %collective-permute-start.8) | collective-permute-done | bytes 1048608 | tf_op jit(solution)/shard_map/ppermute | solution.py:346
  139.5 2.4 bitcast_dynamic-update-slice_fusion.9
  145.4 9.3 %all-to-all-start.1 = ((bf16[16,2,128,256]{3,2,1,0:T(8,128)(2,1)}), bf16[16,2,128,256]{3,2,1,0:T(8,128)(2,1)}, u32[]{:S(2)}, u32[]{:S(2)}) async-start(bf16[16,2,128,256]{3,2,1,0:T(8,128)(2,1)} %bitcast.25), calls=%async_computation.1 | async-start | bytes 4194304 | tf_op jit(solution)/shard_map/all_to_all | solution.py:400
  154.8 9.2 %collective-permute-done.14 = bf16[1,128,4096]{2,1,0:T(8,128)(2,1)} collective-permute-done((bf16[1,128,4096]{2,1,0:T(8,128)(2,1)}, bf16[1,128,4096]{2,1,0:T(8,128)(2,1)}, u32[]{:S(2)}, u32[]{:S(2)}) %collective-permute-start.14) | collective-permute-done | bytes 1048608 | tf_op jit(solution)/shard_map/ppermute | solution.py:349
  164.8 2.4 bitcast_dynamic-update-slice_fusion.5
  167.2 2.3 bitcast_dynamic-update-slice_fusion.4
  169.5 2.3 bitcast_dynamic-update-slice_fusion.3
  172.9 18.7 %shard_map.87 = bf16[3072,512]{1,0:T(8,128)(2,1)} custom-call(s32[1]{0:T(128)} %bitcast.at, bf16[3072,4096]{1,0:T(8,128)(2,1)} %bitcast.86, bf16[4,4,256,512]{3,2,1,0:T(8,128)(2,1)} %bitcast.101), custom_call_target="tpu_custom_call" | custom-call | flops 12884901888 | bytes 36700160 | tf_op jit(solution)/shard_map/pallas_call | solution.py:129
  191.6 1.6 copy-done.7
  193.2 1.9 copy-done.15
  195.1 21.1 %shard_map.88 = (bf16[4,4,2,128,256]{4,3,2,1,0:T(8,128)(2,1)S(1)}, bf16[2,256,3072]{2,1,0:T(8,128)(2,1)S(1)}) custom-call(s32[16]{0:T(128)S(1)} %reshape.67.local_ref, bf16[4,3,256,512]{3,2,1,0:T(8,128)(2,1)S(1)} %bitcast.84, bf16[4,3,256,512]{3,2,1,0:T(8,128)(2,1)S(1)} %bitcast.85, bf16[4,4,2,128,256]{4,3,2,1,0:T(8,128)(2,1)S(1)} %bitcast.81), custom_call_target="tpu_custom_call" | custom-call | flops 3221225472 | bytes 10485760 | tf_op jit(solution)/shard_map/pallas_call | solution.py:229
  216.2 1.6 copy-done.3
  217.8 34.9 %all-to-all-done.1 = bf16[16,2,128,256]{3,2,1,0:T(8,128)(2,1)} async-done(((bf16[16,2,128,256]{3,2,1,0:T(8,128)(2,1)}), bf16[16,2,128,256]{3,2,1,0:T(8,128)(2,1)}, u32[]{:S(2)}, u32[]{:S(2)}) %all-to-all-start.1) | async-done | bytes 2097184 | tf_op jit(solution)/shard_map/all_to_all | solution.py:400
  252.7 19.1 %shard_map.89 = bf16[16,512,256]{2,1,0:T(8,128)(2,1)} custom-call(s32[1]{0:T(128)} %bitcast.at, bf16[3072,4096]{1,0:T(8,128)(2,1)} %bitcast.87, bf16[3072,4096]{1,0:T(8,128)(2,1)} %bitcast.88, bf16[3072,4096]{1,0:T(8,128)(2,1)} %bitcast.89, bf16[3072,4096]{1,0:T(8,128)(2,1)} %bitcast.90, bf16[2,256,3072]{2,1,0:T(8,128)(2,1)} %copy-done.3), custom_call_target="tpu_custom_call" | custom-call | flops 12884901888 | bytes 32505856 | tf_op jit(solution)/shard_map/pallas_call | solution.py:162
  273.3 3.7 collective-permute-start.18
  277.1 2.7 collective-permute-start.17
  279.7 2.4 collective-permute-start.16
  282.1 19.5 %shard_map.90 = bf16[3072,512]{1,0:T(8,128)(2,1)} custom-call(s32[1]{0:T(128)} %bitcast.at, bf16[3072,4096]{1,0:T(8,128)(2,1)} %bitcast.91, bf16[4,4,256,512]{3,2,1,0:T(8,128)(2,1)} %bitcast.100), custom_call_target="tpu_custom_call" | custom-call | flops 12884901888 | bytes 36700160 | tf_op jit(solution)/shard_map/pallas_call | solution.py:129
  301.6 1.9 copy-done.14
  303.4 21.8 %shard_map.91 = (bf16[4,4,2,128,256]{4,3,2,1,0:T(8,128)(2,1)S(1)}, bf16[2,256,3072]{2,1,0:T(8,128)(2,1)S(1)}) custom-call(s32[16]{0:T(128)S(1)} %reshape.67.local_ref, bf16[4,3,256,512]{3,2,1,0:T(8,128)(2,1)S(1)} %bitcast.82, bf16[4,3,256,512]{3,2,1,0:T(8,128)(2,1)S(1)} %bitcast.83, bf16[4,4,2,128,256]{4,3,2,1,0:T(8,128)(2,1)} %bitcast.26.qg_ref), custom_call_target="tpu_custom_call" | custom-call | flops 3221225472 | bytes 10485760 | tf_op jit(solution)/shard_map/pallas_call | solution.py:229
  325.2 1.6 copy-done.2
  328.0 19.3 %shard_map.92 = bf16[16,512,256]{2,1,0:T(8,128)(2,1)} custom-call(s32[1]{0:T(128)} %bitcast.at, bf16[3072,4096]{1,0:T(8,128)(2,1)} %bitcast.92, bf16[3072,4096]{1,0:T(8,128)(2,1)} %bitcast.93, bf16[3072,4096]{1,0:T(8,128)(2,1)} %bitcast.94, bf16[3072,4096]{1,0:T(8,128)(2,1)} %bitcast.95, bf16[2,256,3072]{2,1,0:T(8,128)(2,1)} %copy-done.2), custom_call_target="tpu_custom_call" | custom-call | flops 12884901888 | bytes 32505856 | tf_op jit(solution)/shard_map/pallas_call | solution.py:162
  347.3 17.3 %collective-permute-done.16 = bf16[4,2,128,256]{3,2,1,0:T(8,128)(2,1)} collective-permute-done((bf16[4,2,128,256]{3,2,1,0:T(8,128)(2,1)}, bf16[4,2,128,256]{3,2,1,0:T(8,128)(2,1)}, u32[]{:S(2)}, u32[]{:S(2)}) %collective-permute-start.16) | collective-permute-done | bytes 524320 | tf_op jit(solution)/shard_map/ppermute | solution.py:299
  364.7 36.4 %collective-permute-done.25 = bf16[4,2,128,256]{3,2,1,0:T(8,128)(2,1)S(1)} collective-permute-done((bf16[4,2,128,256]{3,2,1,0:T(8,128)(2,1)S(1)}, bf16[4,2,128,256]{3,2,1,0:T(8,128)(2,1)S(1)}, u32[]{:S(2)}, u32[]{:S(2)}) %collective-permute-start.25) | collective-permute-done | bytes 524320 | tf_op jit(solution)/shard_map/ppermute | solution.py:299
  404.7 3.4 collective-permute-start.19
  408.2 1.5 collective-permute-start.20
  410.1 3.4 collective-permute-start.27
  413.5 8.4 %collective-permute-done.20.refs_2_ = bf16[4,2,128,256]{3,2,1,0:T(8,128)(2,1)S(1)} collective-permute-done((bf16[4,2,128,256]{3,2,1,0:T(8,128)(2,1)S(1)}, bf16[4,2,128,256]{3,2,1,0:T(8,128)(2,1)S(1)}, u32[]{:S(2)}, u32[]{:S(2)}) %collective-permute-start.20) | collective-permute-done | bytes 524320 | tf_op jit(solution)/shard_map/ppermute | solution.py:290
  421.9 11.6 %collective-permute-done.21.refs_3_ = bf16[4,2,128,256]{3,2,1,0:T(8,128)(2,1)S(1)} collective-permute-done((bf16[4,2,128,256]{3,2,1,0:T(8,128)(2,1)S(1)}, bf16[4,2,128,256]{3,2,1,0:T(8,128)(2,1)S(1)}, u32[]{:S(2)}, u32[]{:S(2)}) %collective-permute-start.21) | collective-permute-done | bytes 524320 | tf_op jit(solution)/shard_map/ppermute | solution.py:290
  434.8 1.5 collective-permute-start.29
  436.9 29.0 %collective-permute-done.26 = bf16[4,2,128,256]{3,2,1,0:T(8,128)(2,1)} collective-permute-done((bf16[4,2,128,256]{3,2,1,0:T(8,128)(2,1)}, bf16[4,2,128,256]{3,2,1,0:T(8,128)(2,1)}, u32[]{:S(2)}, u32[]{:S(2)}) %collective-permute-start.26) | collective-permute-done | bytes 524320 | tf_op jit(solution)/shard_map/ppermute | solution.py:299
  465.9 37.0 %collective-permute-done.27 = bf16[4,2,128,256]{3,2,1,0:T(8,128)(2,1)} collective-permute-done((bf16[4,2,128,256]{3,2,1,0:T(8,128)(2,1)}, bf16[4,2,128,256]{3,2,1,0:T(8,128)(2,1)}, u32[]{:S(2)}, u32[]{:S(2)}) %collective-permute-start.27) | collective-permute-done | bytes 524320 | tf_op jit(solution)/shard_map/ppermute | solution.py:299
  502.9 1.5 constant_dynamic-slice_fusion
  507.5 1.5 collective-permute-start.32
  510.1 6.2 %reduce-scatter.5.cloned.1.call-done.refs_4_ = bf16[2048,256]{1,0:T(8,128)(2,1)} async-done(((bf16[8192,256]{1,0:T(8,128)(2,1)}), bf16[2048,256]{1,0:T(8,128)(2,1)}) %reduce-scatter.5.cloned.1.call-update) | async-done | bytes 1048592 | tf_op jit(solution)/shard_map/reduce_scatter | solution.py:429
  516.2 5.1 collective-permute-done.32.refs_6_
  521.4 11.3 %collective-permute-done.33.refs_7_ = bf16[4,2,128,256]{3,2,1,0:T(8,128)(2,1)} collective-permute-done((bf16[4,2,128,256]{3,2,1,0:T(8,128)(2,1)}, bf16[4,2,128,256]{3,2,1,0:T(8,128)(2,1)}, u32[]{:S(2)}, u32[]{:S(2)}) %collective-permute-start.33) | collective-permute-done | bytes 524320 | tf_op jit(solution)/shard_map/ppermute | solution.py:290
  534.2 1.5 collective-permute-start.35
  536.1 4.7 shard_map.93
  541.9 5.9 %collective-permute-done.36.refs_7_ = bf16[512,256]{1,0:T(8,128)(2,1)S(1)} collective-permute-done((bf16[512,256]{1,0:T(8,128)(2,1)S(1)}, bf16[512,256]{1,0:T(8,128)(2,1)S(1)}, u32[]{:S(2)}, u32[]{:S(2)}) %collective-permute-start.36) | collective-permute-done | bytes 262176 | tf_op jit(solution)/shard_map/ppermute | solution.py:290
  552.2 2.3 shard_map.94
  (128 shorter events, 41.3 us)
Async XLA Ops:
  7.2 165.7 %all-gather.3.cloned.1.call-start = ((), (), s32[]{:S(2)}) async-start(), calls=%async_computation.4 | async-start | bytes 5242880 | tf_op jit(solution)/shard_map/all_gather | solution.py:417
  7.2 1.2 copy-start.8
  8.4 1.2 copy-start.9
  9.7 33.6 %slice-start = ((s8[6291456]{0:T(1024)(128)(4,1)}), s8[2097152]{0:T(1024)(128)(4,1)S(1)}, s32[]{:S(2)}) async-start(s8[6291456]{0:T(1024)(128)(4,1)} %bitcast.98), calls=%async_computation.8 | async-start | bytes 4194304
  11.0 14.5 %collective-permute-start.2 = (bf16[256,512]{1,0:T(8,128)(2,1)}, bf16[256,512]{1,0:T(8,128)(2,1)}, u32[]{:S(2)}, u32[]{:S(2)}) collective-permute-start(bf16[256,512]{1,0:T(8,128)(2,1)} %get-tuple-element.139), channel_id=1, source_target_pairs={{0,24},{8,16},{16,8},{24,0},{1,25},{9,17},{17,9},{25,1},{2,26},{10... | collective-permute-start | bytes 786440 | tf_op jit(solution)/shard_map/ppermute | solution.py:290
  12.8 12.9 %collective-permute-start.1 = (bf16[256,512]{1,0:T(8,128)(2,1)}, bf16[256,512]{1,0:T(8,128)(2,1)}, u32[]{:S(2)}, u32[]{:S(2)}) collective-permute-start(bf16[256,512]{1,0:T(8,128)(2,1)} %get-tuple-element.140), channel_id=1, source_target_pairs={{0,16},{8,24},{16,0},{24,8},{1,17},{9,25},{17,1},{25,9},{2,18},{10... | collective-permute-start | bytes 786440 | tf_op jit(solution)/shard_map/ppermute | solution.py:290
  13.0 12.7 %collective-permute-start = (bf16[256,512]{1,0:T(8,128)(2,1)}, bf16[256,512]{1,0:T(8,128)(2,1)}, u32[]{:S(2)}, u32[]{:S(2)}) collective-permute-start(bf16[256,512]{1,0:T(8,128)(2,1)} %get-tuple-element.141), channel_id=1, source_target_pairs={{0,8},{8,0},{16,24},{24,16},{1,9},{9,1},{17,25},{25,17},{2,10},{10... | collective-permute-start | bytes 786440 | tf_op jit(solution)/shard_map/ppermute | solution.py:290
  19.3 1.6 copy-start.4
  20.9 1.6 copy-start.5
  28.0 41.7 %collective-permute-start.4 = (bf16[3,256,4096]{2,1,0:T(8,128)(2,1)}, bf16[3,256,4096]{2,1,0:T(8,128)(2,1)}, u32[]{:S(2)}, u32[]{:S(2)}) collective-permute-start(bf16[3,256,4096]{2,1,0:T(8,128)(2,1)} %param.6), channel_id=1, source_target_pairs={{0,8},{8,0},{16,24},{24,16},{1,9},{9,1},{17,25},{25,17},{2,10},{10... | collective-permute-start | bytes 18874376 | tf_op jit(solution)/shard_map/ppermute | solution.py:342
  29.4 22.8 %collective-permute-start.24 = (bf16[256,512]{1,0:T(8,128)(2,1)}, bf16[256,512]{1,0:T(8,128)(2,1)}, u32[]{:S(2)}, u32[]{:S(2)}) collective-permute-start(bf16[256,512]{1,0:T(8,128)(2,1)} %get-tuple-element.135), channel_id=1, source_target_pairs={{0,24},{8,16},{16,8},{24,0},{1,25},{9,17},{17,9},{25,1},{2,26},{10... | collective-permute-start | bytes 786440 | tf_op jit(solution)/shard_map/ppermute | solution.py:290
  30.7 21.5 %collective-permute-start.23 = (bf16[256,512]{1,0:T(8,128)(2,1)}, bf16[256,512]{1,0:T(8,128)(2,1)}, u32[]{:S(2)}, u32[]{:S(2)}) collective-permute-start(bf16[256,512]{1,0:T(8,128)(2,1)} %get-tuple-element.136), channel_id=1, source_target_pairs={{0,16},{8,24},{16,0},{24,8},{1,17},{9,25},{17,1},{25,9},{2,18},{10... | collective-permute-start | bytes 786440 | tf_op jit(solution)/shard_map/ppermute | solution.py:290
  30.8 21.4 %collective-permute-start.22 = (bf16[256,512]{1,0:T(8,128)(2,1)}, bf16[256,512]{1,0:T(8,128)(2,1)}, u32[]{:S(2)}, u32[]{:S(2)}) collective-permute-start(bf16[256,512]{1,0:T(8,128)(2,1)} %get-tuple-element.137), channel_id=1, source_target_pairs={{0,8},{8,0},{16,24},{24,16},{1,9},{9,1},{17,25},{25,17},{2,10},{10... | collective-permute-start | bytes 786440 | tf_op jit(solution)/shard_map/ppermute | solution.py:290
  32.9 10.4 %slice-start.1 = ((s8[6291456]{0:T(1024)(128)(4,1)}), s8[4194304]{0:T(1024)(128)(4,1)S(1)}, s32[]{:S(2)}) async-start(s8[6291456]{0:T(1024)(128)(4,1)} %bitcast.98), calls=%async_computation.9 | async-start | bytes 8388608
  32.9 36.8 %collective-permute-start.3 = (bf16[1,128,4096]{2,1,0:T(8,128)(2,1)S(1)}, bf16[1,128,4096]{2,1,0:T(8,128)(2,1)}, u32[]{:S(2)}, u32[]{:S(2)}) collective-permute-start(bf16[1,128,4096]{2,1,0:T(8,128)(2,1)S(1)} %slice.55), channel_id=1, source_target_pairs={{0,16},{8,24},{16,0},{24,8},{1,17},{9,25},{17,1},{25,9},{2,18},{10... | collective-permute-start | bytes 3145736 | tf_op jit(solution)/shard_map/ppermute | solution.py:346
  46.5 99.0 %all-to-all-start = ((bf16[16,2,128,256]{3,2,1,0:T(8,128)(2,1)}), bf16[16,2,128,256]{3,2,1,0:T(8,128)(2,1)S(1)}, u32[]{:S(2)}, u32[]{:S(2)}) async-start(bf16[16,2,128,256]{3,2,1,0:T(8,128)(2,1)} %bitcast.16), calls=%async_computation | async-start | bytes 4194304 | tf_op jit(solution)/shard_map/all_to_all | solution.py:400
  52.1 229.9 %all-gather.5.cloned.1.call-start = ((), (), s32[]{:S(2)}) async-start(), calls=%async_computation.6 | async-start | bytes 5242880 | tf_op jit(solution)/shard_map/all_gather | solution.py:417
  69.7 32.6 %collective-permute-start.6 = (bf16[1,128,4096]{2,1,0:T(8,128)(2,1)}, bf16[1,128,4096]{2,1,0:T(8,128)(2,1)S(1)}, u32[]{:S(2)}, u32[]{:S(2)}) collective-permute-start(bf16[1,128,4096]{2,1,0:T(8,128)(2,1)} %collective-permute-done.3), channel_id=1, source_target_pairs={{0,8},{8,0},{16,24},{24,16},{1,9},{9,1},{17,25},{25,17},{2,10},{10... | collective-permute-start | bytes 3145736 | tf_op jit(solution)/shard_map/ppermute | solution.py:350
  71.3 31.0 %collective-permute-start.7 = (bf16[1,128,4096]{2,1,0:T(8,128)(2,1)}, bf16[1,128,4096]{2,1,0:T(8,128)(2,1)S(1)}, u32[]{:S(2)}, u32[]{:S(2)}) collective-permute-start(bf16[1,128,4096]{2,1,0:T(8,128)(2,1)} %collective-permute-done.3), channel_id=1, source_target_pairs={{0,1},{1,0},{2,3},{3,2},{4,5},{5,4},{6,7},{7,6},{8,9},{9,8},{10,11... | collective-permute-start | bytes 3145736 | tf_op jit(solution)/shard_map/ppermute | solution.py:349
  72.8 29.5 %collective-permute-start.5 = (bf16[1,128,4096]{2,1,0:T(8,128)(2,1)S(1)}, bf16[1,128,4096]{2,1,0:T(8,128)(2,1)S(1)}, u32[]{:S(2)}, u32[]{:S(2)}) collective-permute-start(bf16[1,128,4096]{2,1,0:T(8,128)(2,1)S(1)} %slice.56), channel_id=1, source_target_pairs={{0,16},{8,24},{16,0},{24,8},{1,17},{9,25},{17,1},{25,9},{2,18},{10... | collective-permute-start | bytes 3145736 | tf_op jit(solution)/shard_map/ppermute | solution.py:346
  102.3 35.6 %collective-permute-start.9 = (bf16[1,128,4096]{2,1,0:T(8,128)(2,1)S(1)}, bf16[1,128,4096]{2,1,0:T(8,128)(2,1)S(1)}, u32[]{:S(2)}, u32[]{:S(2)}) collective-permute-start(bf16[1,128,4096]{2,1,0:T(8,128)(2,1)S(1)} %collective-permute-done.5), channel_id=1, source_target_pairs={{0,8},{8,0},{16,24},{24,16},{1,9},{9,1},{17,25},{25,17},{2,10},{10... | collective-permute-start | bytes 3145736 | tf_op jit(solution)/shard_map/ppermute | solution.py:350
  103.3 34.6 %collective-permute-start.11 = (bf16[1,128,4096]{2,1,0:T(8,128)(2,1)S(1)}, bf16[1,128,4096]{2,1,0:T(8,128)(2,1)S(1)}, u32[]{:S(2)}, u32[]{:S(2)}) collective-permute-start(bf16[1,128,4096]{2,1,0:T(8,128)(2,1)S(1)} %collective-permute-done.5), channel_id=1, source_target_pairs={{0,1},{1,0},{2,3},{3,2},{4,5},{5,4},{6,7},{7,6},{8,9},{9,8},{10,11... | collective-permute-start | bytes 3145736 | tf_op jit(solution)/shard_map/ppermute | solution.py:349
  106.9 31.0 %collective-permute-start.8 = (bf16[1,128,4096]{2,1,0:T(8,128)(2,1)S(1)}, bf16[1,128,4096]{2,1,0:T(8,128)(2,1)}, u32[]{:S(2)}, u32[]{:S(2)}) collective-permute-start(bf16[1,128,4096]{2,1,0:T(8,128)(2,1)S(1)} %slice.57), channel_id=1, source_target_pairs={{0,16},{8,24},{16,0},{24,8},{1,17},{9,25},{17,1},{25,9},{2,18},{10... | collective-permute-start | bytes 3145736 | tf_op jit(solution)/shard_map/ppermute | solution.py:346
  108.6 29.4 %collective-permute-start.10 = (bf16[1,128,4096]{2,1,0:T(8,128)(2,1)S(1)}, bf16[1,128,4096]{2,1,0:T(8,128)(2,1)S(1)}, u32[]{:S(2)}, u32[]{:S(2)}) collective-permute-start(bf16[1,128,4096]{2,1,0:T(8,128)(2,1)S(1)} %collective-permute-done.7), channel_id=1, source_target_pairs={{0,8},{8,0},{16,24},{24,16},{1,9},{9,1},{17,25},{25,17},{2,10},{10... | collective-permute-start | bytes 3145736 | tf_op jit(solution)/shard_map/ppermute | solution.py:354
  137.9 16.8 %collective-permute-start.12 = (bf16[1,128,4096]{2,1,0:T(8,128)(2,1)}, bf16[1,128,4096]{2,1,0:T(8,128)(2,1)}, u32[]{:S(2)}, u32[]{:S(2)}) collective-permute-start(bf16[1,128,4096]{2,1,0:T(8,128)(2,1)} %collective-permute-done.8), channel_id=1, source_target_pairs={{0,8},{8,0},{16,24},{24,16},{1,9},{9,1},{17,25},{25,17},{2,10},{10... | collective-permute-start | bytes 3145736 | tf_op jit(solution)/shard_map/ppermute | solution.py:350
  138.9 25.1 %collective-permute-start.14 = (bf16[1,128,4096]{2,1,0:T(8,128)(2,1)}, bf16[1,128,4096]{2,1,0:T(8,128)(2,1)}, u32[]{:S(2)}, u32[]{:S(2)}) collective-permute-start(bf16[1,128,4096]{2,1,0:T(8,128)(2,1)} %collective-permute-done.8), channel_id=1, source_target_pairs={{0,1},{1,0},{2,3},{3,2},{4,5},{5,4},{6,7},{7,6},{8,9},{9,8},{10,11... | collective-permute-start | bytes 3145736 | tf_op jit(solution)/shard_map/ppermute | solution.py:349
  139.1 15.6 %collective-permute-start.13 = (bf16[1,128,4096]{2,1,0:T(8,128)(2,1)S(1)}, bf16[1,128,4096]{2,1,0:T(8,128)(2,1)}, u32[]{:S(2)}, u32[]{:S(2)}) collective-permute-start(bf16[1,128,4096]{2,1,0:T(8,128)(2,1)S(1)} %collective-permute-done.11), channel_id=1, source_target_pairs={{0,8},{8,0},{16,24},{24,16},{1,9},{9,1},{17,25},{25,17},{2,10},{10... | collective-permute-start | bytes 3145736 | tf_op jit(solution)/shard_map/ppermute | solution.py:354
  145.4 46.1 %copy-start.6 = (bf16[16,2,128,256]{3,2,1,0:T(8,128)(2,1)}, bf16[16,2,128,256]{3,2,1,0:T(8,128)(2,1)S(1)}, u32[]{:S(2)}) copy-start(bf16[16,2,128,256]{3,2,1,0:T(8,128)(2,1)S(1)} %all-to-all-done) | copy-start | bytes 6291460
  145.4 107.3 %all-to-all-start.1 = ((bf16[16,2,128,256]{3,2,1,0:T(8,128)(2,1)}), bf16[16,2,128,256]{3,2,1,0:T(8,128)(2,1)}, u32[]{:S(2)}, u32[]{:S(2)}) async-start(bf16[16,2,128,256]{3,2,1,0:T(8,128)(2,1)} %bitcast.25), calls=%async_computation.1 | async-start | bytes 4194304 | tf_op jit(solution)/shard_map/all_to_all | solution.py:400
  154.7 278.8 %reduce-scatter.3.cloned.1.call-start = ((), (), s32[]{:S(2)}) async-start(), calls=%async_computation.5 | async-start | bytes 5242880 | tf_op jit(solution)/shard_map/reduce_scatter | solution.py:429
  163.9 7.9 %collective-permute-start.15 = (bf16[1,128,4096]{2,1,0:T(8,128)(2,1)}, bf16[1,128,4096]{2,1,0:T(8,128)(2,1)S(1)}, u32[]{:S(2)}, u32[]{:S(2)}) collective-permute-start(bf16[1,128,4096]{2,1,0:T(8,128)(2,1)} %collective-permute-done.14), channel_id=1, source_target_pairs={{0,8},{8,0},{16,24},{24,16},{1,9},{9,1},{17,25},{25,17},{2,10},{10... | collective-permute-start | bytes 3145736 | tf_op jit(solution)/shard_map/ppermute | solution.py:354
  191.6 1.6 copy-start.7
  193.2 1.9 copy-start.15
  216.2 1.7 copy-start.3
  271.9 244.3 %reduce-scatter.5.cloned.1.call-start = ((), (), s32[]{:S(2)}) async-start(), calls=%async_computation.7 | async-start | bytes 5242880 | tf_op jit(solution)/shard_map/reduce_scatter | solution.py:429
  273.3 74.0 %collective-permute-start.18 = (bf16[4,2,128,256]{3,2,1,0:T(8,128)(2,1)}, bf16[4,2,128,256]{3,2,1,0:T(8,128)(2,1)}, u32[]{:S(2)}, u32[]{:S(2)}) collective-permute-start(bf16[4,2,128,256]{3,2,1,0:T(8,128)(2,1)} %get-tuple-element.126), channel_id=1, source_target_pairs={{0,6},{2,0},{4,2},{6,4},{1,7},{3,1},{5,3},{7,5},{8,14},{10,8},{12,... | collective-permute-start | bytes 1572872 | tf_op jit(solution)/shard_map/ppermute | solution.py:299
  277.1 70.3 %collective-permute-start.17 = (bf16[4,2,128,256]{3,2,1,0:T(8,128)(2,1)}, bf16[4,2,128,256]{3,2,1,0:T(8,128)(2,1)}, u32[]{:S(2)}, u32[]{:S(2)}) collective-permute-start(bf16[4,2,128,256]{3,2,1,0:T(8,128)(2,1)} %get-tuple-element.127), channel_id=1, source_target_pairs={{0,4},{2,6},{4,0},{6,2},{1,5},{3,7},{5,1},{7,3},{8,12},{10,14},{12... | collective-permute-start | bytes 1572872 | tf_op jit(solution)/shard_map/ppermute | solution.py:299
  279.7 85.0 %collective-permute-start.16 = (bf16[4,2,128,256]{3,2,1,0:T(8,128)(2,1)}, bf16[4,2,128,256]{3,2,1,0:T(8,128)(2,1)}, u32[]{:S(2)}, u32[]{:S(2)}) collective-permute-start(bf16[4,2,128,256]{3,2,1,0:T(8,128)(2,1)} %get-tuple-element.125), channel_id=1, source_target_pairs={{0,2},{2,4},{4,6},{6,0},{1,3},{3,5},{5,7},{7,1},{8,10},{10,12},{12... | collective-permute-start | bytes 1572872 | tf_op jit(solution)/shard_map/ppermute | solution.py:299
  301.6 1.9 copy-start.14
  325.2 1.6 copy-start.2
  328.0 73.1 %collective-permute-start.25 = (bf16[4,2,128,256]{3,2,1,0:T(8,128)(2,1)S(1)}, bf16[4,2,128,256]{3,2,1,0:T(8,128)(2,1)S(1)}, u32[]{:S(2)}, u32[]{:S(2)}) collective-permute-start(bf16[4,2,128,256]{3,2,1,0:T(8,128)(2,1)S(1)} %get-tuple-element.120), channel_id=1, source_target_pairs={{0,2},{2,4},{4,6},{6,0},{1,3},{3,5},{5,7},{7,1},{8,10},{10,12},{12... | collective-permute-start | bytes 1572872 | tf_op jit(solution)/shard_map/ppermute | solution.py:299
  404.7 8.8 %collective-permute-start.19 = (bf16[4,2,128,256]{3,2,1,0:T(8,128)(2,1)S(1)}, bf16[4,2,128,256]{3,2,1,0:T(8,128)(2,1)S(1)}, u32[]{:S(2)}, u32[]{:S(2)}) collective-permute-start(bf16[4,2,128,256]{3,2,1,0:T(8,128)(2,1)S(1)} %pad_maximum_fusion.3), channel_id=1, source_target_pairs={{0,8},{8,0},{16,24},{24,16},{1,9},{9,1},{17,25},{25,17},{2,10},{10... | collective-permute-start | bytes 1572872 | tf_op jit(solution)/shard_map/ppermute | solution.py:290
  408.2 13.7 %collective-permute-start.20 = (bf16[4,2,128,256]{3,2,1,0:T(8,128)(2,1)S(1)}, bf16[4,2,128,256]{3,2,1,0:T(8,128)(2,1)S(1)}, u32[]{:S(2)}, u32[]{:S(2)}) collective-permute-start(bf16[4,2,128,256]{3,2,1,0:T(8,128)(2,1)S(1)} %pad_maximum_fusion.4), channel_id=1, source_target_pairs={{0,16},{8,24},{16,0},{24,8},{1,17},{9,25},{17,1},{25,9},{2,18},{10... | collective-permute-start | bytes 1572872 | tf_op jit(solution)/shard_map/ppermute | solution.py:290
  409.8 23.8 %collective-permute-start.21 = (bf16[4,2,128,256]{3,2,1,0:T(8,128)(2,1)S(1)}, bf16[4,2,128,256]{3,2,1,0:T(8,128)(2,1)S(1)}, u32[]{:S(2)}, u32[]{:S(2)}) collective-permute-start(bf16[4,2,128,256]{3,2,1,0:T(8,128)(2,1)S(1)} %pad_maximum_fusion.5), channel_id=1, source_target_pairs={{0,24},{8,16},{16,8},{24,0},{1,25},{9,17},{17,9},{25,1},{2,26},{10... | collective-permute-start | bytes 1572872 | tf_op jit(solution)/shard_map/ppermute | solution.py:290
  410.1 55.9 %collective-permute-start.26 = (bf16[4,2,128,256]{3,2,1,0:T(8,128)(2,1)}, bf16[4,2,128,256]{3,2,1,0:T(8,128)(2,1)}, u32[]{:S(2)}, u32[]{:S(2)}) collective-permute-start(bf16[4,2,128,256]{3,2,1,0:T(8,128)(2,1)} %get-tuple-element.118), channel_id=1, source_target_pairs={{0,4},{2,6},{4,0},{6,2},{1,5},{3,7},{5,1},{7,3},{8,12},{10,14},{12... | collective-permute-start | bytes 1572872 | tf_op jit(solution)/shard_map/ppermute | solution.py:299
  410.1 92.8 %collective-permute-start.27 = (bf16[4,2,128,256]{3,2,1,0:T(8,128)(2,1)}, bf16[4,2,128,256]{3,2,1,0:T(8,128)(2,1)}, u32[]{:S(2)}, u32[]{:S(2)}) collective-permute-start(bf16[4,2,128,256]{3,2,1,0:T(8,128)(2,1)} %get-tuple-element.117), channel_id=1, source_target_pairs={{0,6},{2,0},{4,2},{6,4},{1,7},{3,1},{5,3},{7,5},{8,14},{10,8},{12,... | collective-permute-start | bytes 1572872 | tf_op jit(solution)/shard_map/ppermute | solution.py:299
  434.7 68.2 %collective-permute-start.28 = (bf16[512,256]{1,0:T(8,128)(2,1)S(1)}, bf16[512,256]{1,0:T(8,128)(2,1)S(1)}, u32[]{:S(2)}, u32[]{:S(2)}) collective-permute-start(bf16[512,256]{1,0:T(8,128)(2,1)S(1)} %get-tuple-element.133), channel_id=1, source_target_pairs={{0,8},{8,0},{16,24},{24,16},{1,9},{9,1},{17,25},{25,17},{2,10},{10... | collective-permute-start | bytes 786440 | tf_op jit(solution)/shard_map/ppermute | solution.py:290
  434.8 68.1 %collective-permute-start.29 = (bf16[512,256]{1,0:T(8,128)(2,1)S(1)}, bf16[512,256]{1,0:T(8,128)(2,1)S(1)}, u32[]{:S(2)}, u32[]{:S(2)}) collective-permute-start(bf16[512,256]{1,0:T(8,128)(2,1)S(1)} %get-tuple-element.132), channel_id=1, source_target_pairs={{0,16},{8,24},{16,0},{24,8},{1,17},{9,25},{17,1},{25,9},{2,18},{10... | collective-permute-start | bytes 786440 | tf_op jit(solution)/shard_map/ppermute | solution.py:290
  436.3 66.6 %collective-permute-start.30 = (bf16[512,256]{1,0:T(8,128)(2,1)S(1)}, bf16[512,256]{1,0:T(8,128)(2,1)S(1)}, u32[]{:S(2)}, u32[]{:S(2)}) collective-permute-start(bf16[512,256]{1,0:T(8,128)(2,1)S(1)} %get-tuple-element.131), channel_id=1, source_target_pairs={{0,24},{8,16},{16,8},{24,0},{1,25},{9,17},{17,9},{25,1},{2,26},{10... | collective-permute-start | bytes 786440 | tf_op jit(solution)/shard_map/ppermute | solution.py:290
  502.9 7.1 %copy-start.10 = (bf16[512,256]{1,0:T(8,128)(2,1)}, bf16[512,256]{1,0:T(8,128)(2,1)S(1)}, u32[]{:S(2)}) copy-start(bf16[512,256]{1,0:T(8,128)(2,1)S(1)} %collective-permute-done.29.refs_2_) | copy-start | bytes 786436
  502.9 7.0 %copy-start.12 = (bf16[512,256]{1,0:T(8,128)(2,1)}, bf16[512,256]{1,0:T(8,128)(2,1)S(1)}, u32[]{:S(2)}) copy-start(bf16[512,256]{1,0:T(8,128)(2,1)S(1)} %collective-permute-done.30.refs_3_) | copy-start | bytes 786436
  505.4 10.8 %collective-permute-start.31 = (bf16[4,2,128,256]{3,2,1,0:T(8,128)(2,1)}, bf16[4,2,128,256]{3,2,1,0:T(8,128)(2,1)S(1)}, u32[]{:S(2)}, u32[]{:S(2)}) collective-permute-start(bf16[4,2,128,256]{3,2,1,0:T(8,128)(2,1)} %pad_maximum_fusion.7), channel_id=1, source_target_pairs={{0,8},{8,0},{16,24},{24,16},{1,9},{9,1},{17,25},{25,17},{2,10},{10... | collective-permute-start | bytes 1572872 | tf_op jit(solution)/shard_map/ppermute | solution.py:290
  507.5 13.9 %collective-permute-start.32 = (bf16[4,2,128,256]{3,2,1,0:T(8,128)(2,1)}, bf16[4,2,128,256]{3,2,1,0:T(8,128)(2,1)}, u32[]{:S(2)}, u32[]{:S(2)}) collective-permute-start(bf16[4,2,128,256]{3,2,1,0:T(8,128)(2,1)} %pad_maximum_fusion.8), channel_id=1, source_target_pairs={{0,16},{8,24},{16,0},{24,8},{1,17},{9,25},{17,1},{25,9},{2,18},{10... | collective-permute-start | bytes 1572872 | tf_op jit(solution)/shard_map/ppermute | solution.py:290
  509.8 22.9 %collective-permute-start.33 = (bf16[4,2,128,256]{3,2,1,0:T(8,128)(2,1)}, bf16[4,2,128,256]{3,2,1,0:T(8,128)(2,1)}, u32[]{:S(2)}, u32[]{:S(2)}) collective-permute-start(bf16[4,2,128,256]{3,2,1,0:T(8,128)(2,1)} %pad_maximum_fusion.9), channel_id=1, source_target_pairs={{0,24},{8,16},{16,8},{24,0},{1,25},{9,17},{17,9},{25,1},{2,26},{10... | collective-permute-start | bytes 1572872 | tf_op jit(solution)/shard_map/ppermute | solution.py:290
  533.8 7.0 %collective-permute-start.34 = (bf16[512,256]{1,0:T(8,128)(2,1)S(1)}, bf16[512,256]{1,0:T(8,128)(2,1)S(1)}, u32[]{:S(2)}, u32[]{:S(2)}) collective-permute-start(bf16[512,256]{1,0:T(8,128)(2,1)S(1)} %get-tuple-element.130), channel_id=1, source_target_pairs={{0,8},{8,0},{16,24},{24,16},{1,9},{9,1},{17,25},{25,17},{2,10},{10... | collective-permute-start | bytes 786440 | tf_op jit(solution)/shard_map/ppermute | solution.py:290
  534.2 7.7 %collective-permute-start.35 = (bf16[512,256]{1,0:T(8,128)(2,1)S(1)}, bf16[512,256]{1,0:T(8,128)(2,1)S(1)}, u32[]{:S(2)}, u32[]{:S(2)}) collective-permute-start(bf16[512,256]{1,0:T(8,128)(2,1)S(1)} %get-tuple-element.129), channel_id=1, source_target_pairs={{0,16},{8,24},{16,0},{24,8},{1,17},{9,25},{17,1},{25,9},{2,18},{10... | collective-permute-start | bytes 786440 | tf_op jit(solution)/shard_map/ppermute | solution.py:290
  535.7 12.2 %collective-permute-start.36 = (bf16[512,256]{1,0:T(8,128)(2,1)S(1)}, bf16[512,256]{1,0:T(8,128)(2,1)S(1)}, u32[]{:S(2)}, u32[]{:S(2)}) collective-permute-start(bf16[512,256]{1,0:T(8,128)(2,1)S(1)} %get-tuple-element.128), channel_id=1, source_target_pairs={{0,24},{8,16},{16,8},{24,0},{1,25},{9,17},{17,9},{25,1},{2,26},{10... | collective-permute-start | bytes 786440 | tf_op jit(solution)/shard_map/ppermute | solution.py:290
  547.9 1.2 copy-start
  549.1 1.2 copy-start.1
  550.3 0.9 copy-start.11
  551.3 0.9 copy-start.13
Sparse Core Ops, SparseCore 0:
  28.1 122.7 all-gather.2
  152.4 115.1 all-gather.4
  272.0 133.5 reduce-scatter.2
  407.8 108.3 reduce-scatter.4
